TPU v7x, 32 devices: a whole 2x2x4 slice. The times are simulated.
32 devices in a mesh: seq: 8 (over z, y), head: 4 (over x, core).
Axes of the slice: x: 2, y: 2, z: 4, core: 2. Of those that a mesh axis runs over, the one named last changes fastest.
Arguments:
- queries: bfloat16 [4096, 2048], P('seq', 'head'), may hold values from -6 to 6
- keys: bfloat16 [4096, 2048], P('seq', 'head'), may hold values from -6 to 6
- values: bfloat16 [4096, 2048], P('seq', 'head'), may hold values from -6 to 6
- out_grad: bfloat16 [4096, 4096], P('seq', 'head'), may hold values from -6 to 6
- out_weight: bfloat16 [4096, 2048], P(None, 'head'), may hold values from -0.125 to 0.125
Outputs:
- query_grad: bfloat16 [4096, 2048], P('seq', 'head')
- key_grad: bfloat16 [4096, 2048], P('seq', 'head')
- value_grad: bfloat16 [4096, 2048], P('seq', 'head')
- weight_grad: float32 [4096, 2048], P('seq', 'head')
All inputs are finite; a program needn't handle non-finite values.
Results may differ from a plain program's by a relative error of at most 0.0058.
Values may be sent and summed in bfloat16 or wider, within the bound.
No kernel may reach another device: no remote copies, remote signals or barrier semaphores. Data moves between devices by JAX's collectives and lax.ppermute only.
A program may use at most 128 MiB of HBM per device.

v0:
```python
import math

import jax
import jax.numpy as jnp
from jax import lax
from jax.sharding import PartitionSpec as P

HD = 128


def prefix(shard, axis, combine, identity):
    length, mine = (lax.axis_size(axis), lax.axis_index(axis))
    everything = lax.all_gather(shard, axis)
    start = jnp.broadcast_to(jnp.asarray(identity, shard.dtype), shard.shape)

    def turn(k, before):
        at = length - 1 - k
        reached = at > mine
        new = combine(before, everything[at])
        return jnp.where(reached, new, before)

    return lax.fori_loop(0, length, turn, start)


def add_states(earlier, later_part):
    return earlier + later_part


def per_device(queries, keys, values, out_grad, out_weight):
    rows = queries.shape[0]
    local_heads = queries.shape[1] // HD
    total = lax.axis_size("seq") * rows
    scale = 1.0 / math.sqrt(HD * total)
    full_grad = lax.all_gather(out_grad, "head", axis=1, tiled=True)
    attn_grad = jnp.dot(full_grad, out_weight, preferred_element_type=jnp.float32).astype(
        jnp.bfloat16
    )
    shape = (rows, local_heads, HD)
    query = queries.reshape(shape)
    key = keys.reshape(shape)
    value = values.reshape(shape)
    dout = attn_grad.reshape(shape)
    kv_term = scale * jnp.einsum("tha,thb->hab", key, value, preferred_element_type=jnp.float32)
    back_term = scale * jnp.einsum("tha,thb->hab", query, dout, preferred_element_type=jnp.float32)
    zeros = jnp.zeros_like(kv_term)
    position = lax.axis_index("seq")
    piece = lax.all_gather(kv_term[None], "seq", axis=0, tiled=True)
    index = jnp.arange(piece.shape[0], dtype=jnp.int32)
    keep = (index < position).astype(jnp.float32)
    prior_sum = jnp.sum(piece * keep[:, None, None, None], axis=0)
    later_sum = prefix(back_term, "seq", add_states, zeros)
    prior = prior_sum.astype(jnp.bfloat16)
    later = later_sum.astype(jnp.bfloat16)
    mask = jnp.tril(jnp.ones((rows, rows), jnp.float32))
    probs = (
        scale * jnp.einsum("tha,sha->hts", query, key, preferred_element_type=jnp.float32) * mask
    ).astype(jnp.bfloat16)
    grads = (
        scale * jnp.einsum("thb,shb->hts", dout, value, preferred_element_type=jnp.float32) * mask
    ).astype(jnp.bfloat16)
    outputs = (
        jnp.einsum("hts,shb->thb", probs, value, preferred_element_type=jnp.float32)
        + jnp.einsum("tha,hab->thb", query, prior, preferred_element_type=jnp.float32)
    ).astype(jnp.bfloat16)
    query_grad = (
        jnp.einsum("hts,sha->tha", grads, key, preferred_element_type=jnp.float32)
        + jnp.einsum("thb,hab->tha", dout, prior, preferred_element_type=jnp.float32)
    ).astype(jnp.bfloat16)
    key_grad = (
        jnp.einsum("hts,tha->sha", grads, query, preferred_element_type=jnp.float32)
        + jnp.einsum("shb,hab->sha", value, later, preferred_element_type=jnp.float32)
    ).astype(jnp.bfloat16)
    value_grad = (
        jnp.einsum("hts,thb->shb", probs, dout, preferred_element_type=jnp.float32)
        + jnp.einsum("sha,hab->shb", key, later, preferred_element_type=jnp.float32)
    ).astype(jnp.bfloat16)
    flat_out = outputs.reshape(rows, local_heads * HD)
    factor = 1.0 / math.sqrt(total)
    product = lax.dot_general(
        full_grad, flat_out, (((0,), (0,)), ((), ())), preferred_element_type=jnp.float32
    )
    weight_grad = lax.psum_scatter(product * factor, "seq", scatter_dimension=0, tiled=True)
    flat = (rows, local_heads * HD)
    return (query_grad.reshape(flat), key_grad.reshape(flat), value_grad.reshape(flat), weight_grad)


def solution(mesh):
    return jax.shard_map(
        per_device,
        mesh=mesh,
        in_specs=(
            P("seq", "head"),
            P("seq", "head"),
            P("seq", "head"),
            P("seq", "head"),
            P(None, "head"),
        ),
        out_specs=(P("seq", "head"), P("seq", "head"), P("seq", "head"), P("seq", "head")),
        check_vma=False,
    )
```

profile of v0, /device:TPU:0, one launch (start us, length us, event | category | flops | bytes accessed | tf_op | source)
XLA Modules:
  0.0 309.4 jit_solution(8979682335063335261)
XLA Ops:
  7.2 0.0 copy-start
  7.2 0.0 copy-start.6
  7.2 0.0 all-gather.6.cloned.1.call-start
  7.2 0.7 all-gather.6.cloned.1.call-update
  7.9 0.0 all-gather.8.cloned.1.call-start
  8.0 1.3 copy.55
  9.2 1.1 convolution_multiply_fusion.1
  10.3 0.0 all-gather.8.cloned.1.call-update
  10.3 0.0 all-gather.10.cloned.1.call-start
  10.4 36.4 %all-gather.6.cloned.1.call-done = bf16[512,4096]{1,0:T(8,128)(2,1)} async-done(((bf16[512,1024]{1,0:T(8,128)(2,1)}), bf16[512,4096]{1,0:T(8,128)(2,1)}) %all-gather.6.cloned.1.call-update) | async-done | bytes 4194320 | tf_op jit(solution)/shard_map/all_gather | solution.py:34
  46.8 5.8 %convolution_convert_fusion = bf16[512,512]{0,1:T(8,128)(2,1)S(1)} fusion(bf16[512,4096]{1,0:T(8,128)(2,1)} %all-gather.6.cloned.1.call-done, bf16[4096,512]{1,0:T(8,128)(2,1)} %param.11), kind=kOutput, calls=%fused_computation.15 | convolution fusion | flops 2147745792 | bytes 8912896 | tf_op jit(solution)/shard_map/dot_general | solution.py:35
  52.7 0.8 copy-done.3
  53.4 0.3 fusion.7
  53.7 0.8 copy.38
  54.6 0.0 all-gather.10.cloned.1.call-update
  54.6 0.0 reduce-scatter.2.cloned.1.call-start
  54.7 0.1 select_multiply_fusion
  54.8 1.0 copy-done.2
  55.8 1.8 multiply_convert_fusion
  57.5 1.8 convolution_bitcast_fusion.1
  59.3 39.5 %all-gather.8.cloned.1.call-done = f32[32,128,128]{2,1,0:T(8,128)} async-done(((f32[4,128,128]{2,1,0:T(8,128)}), f32[32,128,128]{2,1,0:T(8,128)}) %all-gather.8.cloned.1.call-update) | async-done | bytes 2097168 | tf_op jit(solution)/shard_map/all_gather | solution.py:47
  98.8 2.0 multiply_reduce_fusion
  100.8 1.6 fusion.6
  102.4 5.6 %multiply_bitcast_fusion = f32[4096,512]{0,1:T(8,128)} fusion(bf16[512,512]{0,1:T(8,128)(2,1)S(1)} %bitcast.112, bf16[512,4096]{1,0:T(8,128)(2,1)S(1)} %copy-done.9), kind=kOutput, calls=%fused_computation.1 | convolution fusion | flops 2149580800 | bytes 13107200 | tf_op jit(solution)/shard_map/dot_general | solution.py:79
  108.0 0.0 reduce-scatter.2.cloned.1.call-update
  108.0 2.2 multiply_convert_fusion.1
  110.3 0.8 convolution_bitcast_fusion.2
  111.1 0.6 copy-done.4
  111.7 1.1 fusion.3
  112.8 2.1 copy.47
  114.8 3.1 %convolution_bitcast_fusion = f32[512,4,128]{0,2,1:T(8,128)} fusion(bf16[4,512,512]{2,1,0:T(8,128)(2,1)} %copy-done.1, bf16[512,512]{1,0:T(8,128)(2,1)S(1)} %copy-done), kind=kOutput, calls=%fused_computation.5 | convolution fusion | flops 268435456 | bytes 3670016 | tf_op jit(solution)/shard_map/hts,tha->sha/dot_general | solution.py:70
  117.9 1.4 fusion.28
  119.3 29.6 %all-gather.10.cloned.1.call-done = f32[32,128,128]{2,1,0:T(8,128)} async-done(((f32[4,128,128]{2,1,0:T(8,128)}), f32[32,128,128]{2,1,0:T(8,128)}) %all-gather.10.cloned.1.call-update) | async-done | bytes 2097168 | tf_op jit(solution)/shard_map/all_gather | solution.py:13
  148.9 8.5 %while.16 = (s32[]{:T(128)}, f32[4,128,128]{2,1,0:T(8,128)S(1)}, s32[]{:T(128)}, f32[8,4,128,128]{3,2,1,0:T(8,128)}, s32[]{:T(128)}, /*index=5*/s32[]{:T(128)}, s32[]{:T(128)}, s32[]{:T(128)}) while((s32[]{:T(128)}, f32[4,128,128]{2,1,0:T(8,128)S(1)}, s32[]{:T(128)}, f32[8,4,128,128]{3,2,1,0:T(8,128)}, s32[]{:T(128)}, ...), condition=%wide.region_2.3_spmd.clone, body=%wide.region_1.2_spmd.clone.sunk | while | flops 196616 | bytes 786595 | solution.py:22
  148.9 1.0 add_select_fusion.2
  150.0 1.0 add_select_fusion.2
  151.1 1.0 add_select_fusion.2
  152.1 1.0 add_select_fusion.2
  153.2 1.0 add_select_fusion.2
  154.3 1.0 add_select_fusion.2
  155.3 1.0 add_select_fusion.2
  156.4 1.0 add_select_fusion.2
  157.5 1.9 fusion.4
  159.4 1.0 copy.48
  160.4 0.3 fusion.5
  160.8 1.0 copy.49
  161.8 138.5 %reduce-scatter.2.cloned.1.call-done = f32[512,512]{0,1:T(8,128)} async-done(((f32[4096,512]{0,1:T(8,128)}), f32[512,512]{0,1:T(8,128)}) %reduce-scatter.2.cloned.1.call-update) | async-done | bytes 1048592 | tf_op jit(solution)/shard_map/reduce_scatter | solution.py:82
  300.3 2.5 copy.50
  (19 shorter events, 0.1 us)
Async XLA Ops:
  7.2 46.3 %copy-start = (bf16[512,512]{1,0:T(8,128)(2,1)S(1)}, bf16[512,512]{1,0:T(8,128)(2,1)}, u32[]{:S(2)}) copy-start(bf16[512,512]{1,0:T(8,128)(2,1)} %param.7) | copy-start | bytes 1572868
  7.2 2.1 copy-start.6
  7.2 39.6 %all-gather.6.cloned.1.call-start = ((), (), s32[]{:S(2)}) async-start(), calls=%async_computation.1 | async-start | bytes 5242880 | tf_op jit(solution)/shard_map/all_gather | solution.py:34
  7.9 90.9 %all-gather.8.cloned.1.call-start = ((), (), s32[]{:S(2)}) async-start(), calls=%async_computation.3 | async-start | bytes 2359296 | tf_op jit(solution)/shard_map/all_gather | solution.py:47
  10.3 138.6 %all-gather.10.cloned.1.call-start = ((), (), s32[]{:S(2)}) async-start(), calls=%async_computation.4 | async-start | bytes 2359296 | tf_op jit(solution)/shard_map/all_gather | solution.py:13
  52.6 0.8 copy-start.3
  54.6 245.7 %reduce-scatter.2.cloned.1.call-start = ((), (), s32[]{:S(2)}) async-start(), calls=%async_computation.2 | async-start | bytes 9437184 | tf_op jit(solution)/shard_map/reduce_scatter | solution.py:82
  54.8 1.0 copy-start.2
  98.8 3.6 %copy-start.9 = (bf16[512,4096]{1,0:T(8,128)(2,1)S(1)}, bf16[512,4096]{1,0:T(8,128)(2,1)}, u32[]{:S(2)}) copy-start(bf16[512,4096]{1,0:T(8,128)(2,1)} %all-gather.6.cloned.1.call-done) | copy-start | bytes 12582916
  108.0 2.2 copy-start.7
  110.2 2.5 copy-start.1
  110.2 1.4 copy-start.4
  114.8 3.1 %copy-start.5 = (bf16[512,512]{0,1:T(8,128)(2,1)S(1)}, bf16[512,512]{0,1:T(8,128)(2,1)}, u32[]{:S(2)}) copy-start(bf16[512,512]{0,1:T(8,128)(2,1)} %copy-done.3) | copy-start | bytes 1572868
  157.5 3.0 copy-start.8
  157.5 3.0 copy-start.10
Sparse Core Ops, SparseCore 0:
  9.6 37.1 all-gather.5
  49.5 49.2 all-gather.7
  101.0 47.9 all-gather.9
  152.4 147.8 reduce-scatter.1
where the time goes:
time: 310 us; the launch traced here: 309 us
  waiting for transfers between devices  245 us (79%)
  matrix products  28.8 us (9%)
  between operations  13.9 us (4%)
  local copies, waits for them, and re-layouts  11.1 us (4%)
  other arithmetic  10.4 us (3%)
    reduce_scatter x1, waiting for transfers between devices, per_device(): lax.psum_scatter(product * factor, 'seq', scatter_dimension=0, tiled=True)  139 us
    all_gather x1, waiting for transfers between devices, per_device(): piece = lax.all_gather(kv_term[None], 'seq', axis=0, tiled=True)  39.5 us
    all_gather x1, waiting for transfers between devices, per_device(): full_grad = lax.all_gather(out_grad, 'head', axis=1, tiled=True)  36.4 us
    all_gather x1, waiting for transfers between devices, prefix(): everything = lax.all_gather(shard, axis)  29.6 us
    unnamed x26, local copies, waits for them, and re-layouts  8.98 us
    select_n x8, other arithmetic, turn(): return jnp.where(reached, new, before)  8.32 us
  transfers between devices with their start and end apart: 4, of which 4 were waited for; matrix products, arithmetic and copies ran while one was open for 15% of the time, Pallas kernels for 0%

commit v1 on v0

v1 whole, which is shorter than its diff:
```python
import functools
import math

import jax
import jax.numpy as jnp
from jax import lax
from jax.experimental import pallas as pl
from jax.experimental.pallas import tpu as pltpu
from jax.sharding import PartitionSpec as P

HD = 128
BF16 = jnp.bfloat16
F32 = jnp.float32


def dot(a, b, on_a=1, on_b=0):
    return lax.dot_general(a, b, (((on_a,), (on_b,)), ((), ())), preferred_element_type=F32)


def call(body, outs, *args, scalars=0, vmem=48):
    specs = [pl.BlockSpec(memory_space=pltpu.SMEM)] * scalars
    specs += [pl.BlockSpec(memory_space=pltpu.VMEM)] * (len(args) - scalars)
    return pl.pallas_call(
        body,
        out_shape=outs,
        in_specs=specs,
        out_specs=jax.tree.map(lambda _: pl.BlockSpec(memory_space=pltpu.VMEM), outs),
        compiler_params=pltpu.CompilerParams(vmem_limit_bytes=vmem << 20),
    )(*args)


def head(h):
    return slice(h * HD, (h + 1) * HD)


def state_body(scale, a_ref, b_ref, out_ref):
    for h in range(a_ref.shape[1] // HD):
        term = dot(a_ref[:, head(h)], b_ref[:, head(h)], 0, 0)
        out_ref[head(h), :] = (scale * term).astype(BF16)


def masked(scale, a, b, row):
    scores = scale * dot(a, b, 1, 1)
    rows = row + lax.broadcasted_iota(jnp.int32, scores.shape, 0)
    return jnp.where(lax.broadcasted_iota(jnp.int32, scores.shape, 1) <= rows, scores, 0.0).astype(BF16)


def inner_body(scale, part, q_ref, k_ref, v_ref, out_ref):
    for h in range(q_ref.shape[1] // HD):
        for row in range(0, q_ref.shape[0], part):
            end = row + part
            probs = masked(scale, q_ref[row:end, head(h)], k_ref[:end, head(h)], row)
            out_ref[row:end, head(h)] = dot(probs, v_ref[:end, head(h)])


def outputs_body(first, pv_ref, q_ref, prior_ref, out_ref):
    for i in range(out_ref.shape[1] // HD):
        h = first + i
        total = pv_ref[:, head(h)] + dot(q_ref[:, head(h)], prior_ref[head(h), :])
        out_ref[:, head(i)] = total.astype(BF16)


def attn_grad_body(row_ref, *refs):
    pieces, w_ref, out_ref = refs[:-2], refs[-2], refs[-1]
    total = None
    for i, piece in enumerate(pieces):
        depth = piece.shape[1]
        rows = pl.ds(pl.multiple_of(row_ref[i], depth), depth)
        term = dot(piece[...], w_ref[rows, :])
        total = term if total is None else total + term
    out_ref[...] = total.astype(BF16)


def grads_body(scale, part, q_ref, k_ref, v_ref, d_ref, prior_ref, later_ref, dq_ref, dk_ref, dv_ref):
    rows = q_ref.shape[0]
    for h in range(q_ref.shape[1] // HD):
        at = head(h)
        dk = dot(v_ref[:, at], later_ref[at, :], 1, 1)
        dv = dot(k_ref[:, at], later_ref[at, :])
        dk_parts = [dk[r : r + part] for r in range(0, rows, part)]
        dv_parts = [dv[r : r + part] for r in range(0, rows, part)]
        for row in range(0, rows, part):
            end = row + part
            q, d = q_ref[row:end, at], d_ref[row:end, at]
            probs = masked(scale, q, k_ref[:end, at], row)
            grads = masked(scale, d, v_ref[:end, at], row)
            dq = dot(grads, k_ref[:end, at]) + dot(d, prior_ref[at, :], 1, 1)
            dq_ref[row:end, at] = dq.astype(BF16)
            for i, r in enumerate(range(0, end, part)):
                dk_parts[i] += dot(grads[:, r : r + part], q, 0, 0)
                dv_parts[i] += dot(probs[:, r : r + part], d, 0, 0)
        for i, r in enumerate(range(0, rows, part)):
            dk_ref[r : r + part, at] = dk_parts[i].astype(BF16)
            dv_ref[r : r + part, at] = dv_parts[i].astype(BF16)


def product_body(factor, count, slot_ref, *refs):
    mine, theirs = refs[:count], refs[count : 2 * count]
    o_ref, n_ref = refs[2 * count : 2 * count + 2]
    outs = refs[2 * count + 2 :]
    for s, out in enumerate(outs):
        for j in range(count):

            @pl.when(slot_ref[s] == j)
            def _():
                total = dot(mine[j][...], o_ref[...], 0, 0) + dot(theirs[j][...], n_ref[...], 0, 0)
                out[...] = (factor * total).astype(BF16)


def flip(a, axis, bit, one_way=None):
    pairs = [(i, i ^ bit) for i in range(lax.axis_size(axis))]
    if one_way is not None:
        pairs = [p for p in pairs if bool(p[0] & bit) == one_way]
    return lax.ppermute(a, axis, pairs)


def add(a, b):
    return (a.astype(F32) + b.astype(F32)).astype(BF16)


def scan(term, axis, later):
    size, mine = lax.axis_size(axis), lax.axis_index(axis)
    total, before, bit = term, None, 1
    while bit < size:
        last = 2 * bit == size
        got = flip(total, axis, bit, one_way=later if last else None)
        kept = ((mine & bit) != 0) != later
        take = jnp.where(kept, got, jnp.zeros_like(got))
        before = take if before is None else add(before, take)
        if not last:
            total = add(total, got)
        bit *= 2
    return before


def gather(blocks, axis):
    bit = lax.axis_size(axis)
    blocks = [blocks]
    while bit > 1:
        bit //= 2
        blocks = [item for b in blocks for item in (b, tuple(flip(x, axis, bit) for x in b))]
    return blocks


def line_sum(blocks, line, y, size):
    up = [(0, 1), (3, 2)]
    both = [(0, 1), (1, 0), (2, 3), (3, 2)]
    middle = [(1, 2), (2, 1)]

    def send(a, pairs):
        return lax.ppermute(a, "seq", [(2 * s + i, 2 * t + i) for s, t in pairs for i in range(2)])

    e1 = [send(b[0], up) for b in blocks]
    m2 = [send(add(b[0], r), middle) for b, r in zip(blocks, e1)]
    e2 = [send(b[1], up) for b in blocks]
    m3 = [send(add(b[1], r), middle) for b, r in zip(blocks, e2)]
    e3 = [send(add(b[2], r), both) for b, r in zip(blocks, m2)]
    parts = [
        b[3].astype(F32) + r.astype(F32) + s.astype(F32) for b, r, s in zip(blocks, e3, m3)
    ]
    return jnp.concatenate(parts, axis=1)


ORDER = ((3, 2, 1, 0), (3, 2, 0, 1), (0, 1, 3, 2), (0, 1, 2, 3))


def per_device(queries, keys, values, out_grad, out_weight):
    rows, width = queries.shape
    n_seq, n_head = lax.axis_size("seq"), lax.axis_size("head")
    seq, mine = lax.axis_index("seq"), lax.axis_index("head")
    y, z = seq % 2, seq // 2
    line = n_seq // 2
    total = n_seq * rows
    scale = 1.0 / math.sqrt(HD * total)
    factor = 1.0 / math.sqrt(total)
    part = 256
    shaped = lambda dims, dtype=BF16: jax.ShapeDtypeStruct(dims, dtype)
    state = lambda a, b: call(functools.partial(state_body, scale), shaped((width, HD)), a, b)

    cols = out_grad.shape[1]
    block = cols * n_head // n_seq
    cut = out_grad.reshape(rows, cols // (2 * block), 2, block)
    half = lambda i: lax.dynamic_index_in_dim(cut, i, 2, keepdims=False).reshape(rows, cols // 2)
    own, other = half(y), half(1 - y)

    kv_term = state(keys, values)
    prior = scan(kv_term, "seq", False)
    pv = call(functools.partial(inner_body, scale, part), shaped((rows, width), F32), queries, keys, values)

    pieces = gather((other, own), "head")
    theirs = gather((flip(other, "seq", 1),), "head")

    halves = []
    heads = width // HD
    chunks = 2
    for c in range(chunks):
        o = call(
            functools.partial(outputs_body, c * heads // chunks),
            shaped((rows, width // chunks)),
            pv,
            queries,
            prior,
        )
        halves.append((o, flip(o, "seq", 1)))

    if line == 4 and n_head == 4:
        slots = jnp.asarray(ORDER, jnp.int32)[z] ^ mine
    else:
        slots = jnp.arange(n_head, dtype=jnp.int32) ^ mine
    products = [
        call(
            functools.partial(product_body, factor, n_head),
            [shaped((cols // 2, width // chunks))] * n_head,
            slots,
            *[p[1] for p in pieces],
            *[t[0] for t in theirs],
            o,
            n,
            scalars=1,
        )
        for o, n in halves
    ]
    if line == 4 and n_head == 4:
        weight_grad = line_sum(products, z, y, line)
    else:
        groups = [[2 * p + i for p in range(line)] for i in range(2)]
        whole = jnp.concatenate([jnp.concatenate(p, axis=0) for p in products], axis=1)
        weight_grad = lax.psum_scatter(
            whole.astype(F32), "seq", scatter_dimension=0, axis_index_groups=groups, tiled=True
        )

    flat, starts = [], []
    for j, (n_half, m_half) in enumerate(pieces):
        first = (mine ^ j) * cols
        for i in range(cols // (2 * block)):
            for at, piece in ((1 - y, n_half), (y, m_half)):
                flat.append(piece[:, i * block : (i + 1) * block])
                starts.append(first + (2 * i + at) * block)
    attn_grad = call(
        attn_grad_body,
        shaped((rows, width)),
        jnp.stack(starts).astype(jnp.int32),
        *flat,
        out_weight,
        scalars=1,
    )
    back_term = state(queries, attn_grad)
    later = scan(back_term, "seq", True)
    grads = call(
        functools.partial(grads_body, scale, part),
        [shaped((rows, width))] * 3,
        queries,
        keys,
        values,
        attn_grad,
        prior,
        later,
    )
    return (*grads, weight_grad)


def solution(mesh):
    return jax.shard_map(
        per_device,
        mesh=mesh,
        in_specs=(
            P("seq", "head"),
            P("seq", "head"),
            P("seq", "head"),
            P("seq", "head"),
            P(None, "head"),
        ),
        out_specs=(P("seq", "head"), P("seq", "head"), P("seq", "head"), P("seq", "head")),
        check_vma=False,
    )
```

time: 310 us -> 117 us (0.38)
  waiting for transfers between devices: 245 us -> 26.8 us
  starting transfers between devices: 0.16 us -> 47.4 us
  matrix products: 28.8 us -> 0 us
  Pallas kernels: 0 us -> 20.4 us
  between operations: 13.9 us -> 1.08 us
    reduce_scatter x1 -> x0, waiting for transfers between devices: 139 us -> none  [per_device(): lax.psum_scatter(product * factor, 'seq', scatter_dimension=0, tiled=True)]
    all_gather x3 -> x0, waiting for transfers between devices: 105 us -> none  [the longest x1 39.5 us: per_device(): piece = lax.all_gather(kv_term[None], 'seq', axis=0, tiled=True)]
    ppermute x0 -> x28, starting transfers between devices: none -> 47.4 us  [the longest x10 26.1 us: send(): lax.ppermute(a, 'seq', [(2 * s + i, 2 * t + i) for s, t in pairs for i in...]
    dot_general x14 -> x0, matrix products: 28.8 us -> none  [the longest x1 5.84 us: per_device(): jnp.dot(full_grad, out_weight, preferred_element_type=jnp.float32)]
    ppermute x0 -> x28, waiting for transfers between devices: none -> 26.8 us  [the longest x18 21.9 us: flip(): return lax.ppermute(a, axis, pairs)]
    pallas_call x0 -> x9, Pallas kernels: none -> 20.4 us  [call(): pl.pallas_call(body, out_shape=outs, in_specs=specs, out_specs=jax.tree.m...]
    select_n x8 -> x0, other arithmetic: 8.32 us -> none  [turn(): return jnp.where(reached, new, before)]
    convert_element_type x1 -> x12, other arithmetic: 0.01 us -> 5.93 us  [add(): return (a.astype(F32) + b.astype(F32)).astype(BF16)]
  transfers between devices with their start and end apart: 4 -> 28, of which waited for: 4 -> 7; matrix products, arithmetic and copies ran while one was open for 15% -> 7% of each run, Pallas kernels for 0% -> 18%
where the time goes in v1:
time: 117 us; the launch traced here: 116 us
  starting transfers between devices  47.4 us (41%)
  waiting for transfers between devices  26.8 us (23%)
  Pallas kernels  20.4 us (17%)
  local copies, waits for them, and re-layouts  12.6 us (11%)
  other arithmetic  7.92 us (7%)
    ppermute x10, starting transfers between devices, send(): lax.ppermute(a, 'seq', [(2 * s + i, 2 * t + i) for s, t in pairs for i in...  26.1 us
    ppermute x18, waiting for transfers between devices, flip(): return lax.ppermute(a, axis, pairs)  21.9 us
    ppermute x18, starting transfers between devices, flip(): return lax.ppermute(a, axis, pairs)  21.3 us
    pallas_call x9, Pallas kernels, call(): pl.pallas_call(body, out_shape=outs, in_specs=specs, out_specs=jax.tree.m...  20.4 us
    unnamed x36, local copies, waits for them, and re-layouts  8.48 us
    convert_element_type x12, other arithmetic, add(): return (a.astype(F32) + b.astype(F32)).astype(BF16)  5.93 us
    ppermute x10, waiting for transfers between devices, send(): lax.ppermute(a, 'seq', [(2 * s + i, 2 * t + i) for s, t in pairs for i in...  4.92 us
  transfers between devices with their start and end apart: 28, of which 7 were waited for; matrix products, arithmetic and copies ran while one was open for 7% of the time, Pallas kernels for 18%

profile of v1, /device:TPU:0, one launch (start us, length us, event | category | flops | bytes accessed | tf_op | source)
XLA Modules:
  0.0 116.2 jit_solution(3627974684142648939)
XLA Ops:
  0.7 1.8 %reshape.21 = bf16[512,1,2,512]{3,2,0,1:T(2,128)(2,1)S(1)} reshape(bf16[512,1024]{1,0:T(8,128)(2,1)} %param.9) | data formatting | bytes 2097152 | tf_op jit(solution)/shard_map/reshape | solution.py:182
  2.5 2.2 %constant_dynamic-slice_fusion.1 = (bf16[512,1,1,512]{3,2,0,1:T(2,128)(2,1)S(1)}, bf16[512,1,1,512]{3,2,0,1:T(2,128)(2,1)S(1)}) fusion(bf16[512,1,2,512]{3,2,0,1:T(2,128)(2,1)S(1)} %reshape.21, s32[]{:T(128)S(6)} %select_n.61, s32[]{:T(128)S(6)} %select_n.60), kind=kLoop, calls=%fused_computation.20 | loop fusion | bytes 2097160 | tf_op jit(solution)/shard_map/jit(dynamic_index_in_dim)/dynamic_slice | solution.py:183
  4.8 3.0 %collective-permute-start.3 = (bf16[512,512]{1,0:T(8,128)(2,1)S(1)}, bf16[512,512]{1,0:T(8,128)(2,1)S(1)}, u32[]{:S(2)}, u32[]{:S(2)}) collective-permute-start(bf16[512,512]{1,0:T(8,128)(2,1)S(1)} %bitcast.16), channel_id=1, source_target_pairs={{0,2},{1,3},{2,0},{3,1},{4,6},{5,7},{6,4},{7,5},{8,10},{9,11},{10,... | collective-permute-start | bytes 1572872 | tf_op jit(solution)/shard_map/ppermute | solution.py:114
  7.9 0.9 copy.17
  8.8 2.0 %collective-permute-start.12 = (bf16[512,512]{1,0:T(8,128)(2,1)}, bf16[512,512]{1,0:T(8,128)(2,1)}, u32[]{:S(2)}, u32[]{:S(2)}) collective-permute-start(bf16[512,512]{1,0:T(8,128)(2,1)} %bitcast.15.refs_0_), channel_id=1, source_target_pairs={{0,4},{4,0},{8,12},{12,8},{16,20},{20,16},{24,28},{28,24},{1,5},{5... | collective-permute-start | bytes 1572872 | tf_op jit(solution)/shard_map/ppermute | solution.py:114
  11.3 14.0 %collective-permute-done.6 = bf16[512,128]{1,0:T(8,128)(2,1)S(1)} collective-permute-done((bf16[512,128]{1,0:T(8,128)(2,1)S(1)}, bf16[512,128]{1,0:T(8,128)(2,1)S(1)}, u32[]{:S(2)}, u32[]{:S(2)}) %collective-permute-start.6) | collective-permute-done | bytes 131104 | tf_op jit(solution)/shard_map/ppermute | solution.py:114
  25.3 1.8 %collective-permute-start.7 = (bf16[512,128]{1,0:T(8,128)(2,1)S(1)}, bf16[512,128]{1,0:T(8,128)(2,1)S(1)}, u32[]{:S(2)}, u32[]{:S(2)}) collective-permute-start(bf16[512,128]{1,0:T(8,128)(2,1)S(1)} %add_convert_fusion.13), channel_id=1, source_target_pairs={{0,8},{4,12},{8,0},{12,4},{16,24},{20,28},{24,16},{28,20},{1,9},{5... | collective-permute-start | bytes 393224 | tf_op jit(solution)/shard_map/ppermute | solution.py:114
  27.1 3.2 %collective-permute-done.7 = bf16[512,128]{1,0:T(8,128)(2,1)S(1)} collective-permute-done((bf16[512,128]{1,0:T(8,128)(2,1)S(1)}, bf16[512,128]{1,0:T(8,128)(2,1)S(1)}, u32[]{:S(2)}, u32[]{:S(2)}) %collective-permute-start.7) | collective-permute-done | bytes 131104 | tf_op jit(solution)/shard_map/ppermute | solution.py:114
  31.1 1.7 %collective-permute-start.14 = (bf16[512,512]{1,0:T(8,128)(2,1)}, bf16[512,512]{1,0:T(8,128)(2,1)}, u32[]{:S(2)}, u32[]{:S(2)}) collective-permute-start(bf16[512,512]{1,0:T(8,128)(2,1)} %collective-permute-done.12.refs_4_), channel_id=1, source_target_pairs={{0,2},{1,3},{2,0},{3,1},{4,6},{5,7},{6,4},{7,5},{8,10},{9,11},{10,... | collective-permute-start | bytes 1572872 | tf_op jit(solution)/shard_map/ppermute | solution.py:114
  32.9 0.7 add_convert_fusion.11
  33.6 5.1 %collective-permute-start.8 = (bf16[512,128]{1,0:T(8,128)(2,1)}, bf16[512,128]{1,0:T(8,128)(2,1)}, u32[]{:S(2)}, u32[]{:S(2)}) collective-permute-start(bf16[512,128]{1,0:T(8,128)(2,1)} %add_convert_fusion.11), channel_id=1, source_target_pairs={{0,16},{4,20},{8,24},{12,28},{1,17},{5,21},{9,25},{13,29},{2,18},{... | collective-permute-start | bytes 393224 | tf_op jit(solution)/shard_map/ppermute | solution.py:114
  38.7 1.0 copy-done.2
  39.7 1.0 copy-done.5
  40.8 1.4 %shard_map.97.pv_ref = f32[512,512]{1,0:T(8,128)S(1)} custom-call(bf16[512,512]{1,0:T(8,128)(2,1)S(1)} %copy-done, bf16[512,512]{1,0:T(8,128)(2,1)S(1)} %copy-done.2, bf16[512,512]{1,0:T(8,128)(2,1)S(1)} %copy-done.5), custom_call_target="tpu_custom_call" | custom-call | tf_op jit(solution)/shard_map/pallas_call | solution.py:23
  42.4 5.3 %shard_map.93.b_ref.d_ref = bf16[512,512]{1,0:T(8,128)(2,1)S(1)} custom-call(s32[8]{0:T(128)S(1)} %stack.35.row_ref, bf16[512,512]{1,0:T(8,128)(2,1)} %bitcast.15.refs_0_, bf16[512,512]{1,0:T(8,128)(2,1)S(1)} %bitcast.18, bf16[512,512]{1,0:T(8,128)(2,1)} %collective-permute-done.refs_2_, bf16[512,512]{1,0:T(8,128)(2,1)S(1)} %collective-permute-done.1.refs_3_.refs_1_, ...), custom_call_target="tpu_custom_call" | custom-call | tf_op jit(solution)/shard_map/pallas_call | solution.py:23
  48.2 0.8 copy-done.7
  48.9 1.5 %collective-permute-start.9 = (bf16[512,128]{1,0:T(8,128)(2,1)S(1)}, bf16[512,128]{1,0:T(8,128)(2,1)S(1)}, u32[]{:S(2)}, u32[]{:S(2)}) collective-permute-start(bf16[512,128]{1,0:T(8,128)(2,1)S(1)} %shard_map.95), channel_id=1, source_target_pairs={{0,4},{4,0},{8,12},{12,8},{16,20},{20,16},{24,28},{28,24},{1,5},{5... | collective-permute-start | bytes 393224 | tf_op jit(solution)/shard_map/ppermute | solution.py:114
  51.5 3.7 %collective-permute-done.9 = bf16[512,128]{1,0:T(8,128)(2,1)S(1)} collective-permute-done((bf16[512,128]{1,0:T(8,128)(2,1)S(1)}, bf16[512,128]{1,0:T(8,128)(2,1)S(1)}, u32[]{:S(2)}, u32[]{:S(2)}) %collective-permute-start.9) | collective-permute-done | bytes 131104 | tf_op jit(solution)/shard_map/ppermute | solution.py:114
  55.2 0.7 add_convert_fusion.9
  55.9 1.6 %collective-permute-start.10 = (bf16[512,128]{1,0:T(8,128)(2,1)}, bf16[512,128]{1,0:T(8,128)(2,1)}, u32[]{:S(2)}, u32[]{:S(2)}) collective-permute-start(bf16[512,128]{1,0:T(8,128)(2,1)} %add_convert_fusion.9), channel_id=1, source_target_pairs={{0,8},{4,12},{8,0},{12,4},{16,24},{20,28},{24,16},{28,20},{1,9},{5... | collective-permute-start | bytes 393224 | tf_op jit(solution)/shard_map/ppermute | solution.py:114
  57.5 0.7 fusion.1.slot_ref
  58.4 1.6 %collective-permute-start.22 = (bf16[512,256]{1,0:T(8,128)(2,1)S(1)}, bf16[512,256]{1,0:T(8,128)(2,1)S(1)}, u32[]{:S(2)}, u32[]{:S(2)}) collective-permute-start(bf16[512,256]{1,0:T(8,128)(2,1)S(1)} %shard_map.100.refs_8_), channel_id=1, source_target_pairs={{0,4},{4,0},{8,12},{12,8},{16,20},{20,16},{24,28},{28,24},{1,5},{5... | collective-permute-start | bytes 786440 | tf_op jit(solution)/shard_map/ppermute | solution.py:114
  60.0 0.7 collective-permute-done.16.refs_9_
  60.8 4.6 %shard_map.99 = (bf16[512,256]{1,0:T(8,128)(2,1)}, bf16[512,256]{1,0:T(8,128)(2,1)}, bf16[512,256]{1,0:T(8,128)(2,1)S(1)}, bf16[512,256]{1,0:T(8,128)(2,1)S(1)}) custom-call(s32[4]{0:T(128)S(1)} %fusion.1.slot_ref, bf16[512,512]{1,0:T(8,128)(2,1)S(1)} %bitcast.19, bf16[512,512]{1,0:T(8,128)(2,1)S(1)} %collective-permute-done.1.refs_3_.refs_1_, ...), custom_call_target="tpu_custom_call" | custom-call | tf_op jit(solution)/shard_map/pallas_call | solution.py:23
  65.4 0.8 copy-done.9
  66.2 4.3 %collective-permute-start.17 = (bf16[512,256]{1,0:T(8,128)(2,1)}, bf16[512,256]{1,0:T(8,128)(2,1)}, u32[]{:S(2)}, u32[]{:S(2)}) collective-permute-start(bf16[512,256]{1,0:T(8,128)(2,1)} %get-tuple-element.20), channel_id=1, source_target_pairs={{0,8},{4,12},{24,16},{28,20},{1,9},{5,13},{25,17},{29,21},{2,10},{... | collective-permute-start | bytes 786440 | tf_op jit(solution)/shard_map/ppermute | solution.py:151
  70.5 1.3 %collective-permute-start.20 = (bf16[512,256]{1,0:T(8,128)(2,1)}, bf16[512,256]{1,0:T(8,128)(2,1)S(1)}, u32[]{:S(2)}, u32[]{:S(2)}) collective-permute-start(bf16[512,256]{1,0:T(8,128)(2,1)} %get-tuple-element.21), channel_id=1, source_target_pairs={{0,8},{4,12},{24,16},{28,20},{1,9},{5,13},{25,17},{29,21},{2,10},{... | collective-permute-start | bytes 786440 | tf_op jit(solution)/shard_map/ppermute | solution.py:151
  71.8 1.0 add_convert_fusion.7
  72.9 1.4 %collective-permute-start.11 = (bf16[512,128]{1,0:T(8,128)(2,1)S(1)}, bf16[512,128]{1,0:T(8,128)(2,1)S(1)}, u32[]{:S(2)}, u32[]{:S(2)}) collective-permute-start(bf16[512,128]{1,0:T(8,128)(2,1)S(1)} %add_convert_fusion.7), channel_id=1, source_target_pairs={{16,0},{20,4},{24,8},{28,12},{17,1},{21,5},{25,9},{29,13},{18,2},{... | collective-permute-start | bytes 393224 | tf_op jit(solution)/shard_map/ppermute | solution.py:114
  74.3 0.7 copy-done.13
  75.0 1.0 copy-done.10
  76.1 1.0 copy-done.12
  77.1 0.9 copy-done.14
  78.1 3.4 %shard_map.101 = (bf16[512,256]{1,0:T(8,128)(2,1)S(1)}, bf16[512,256]{1,0:T(8,128)(2,1)S(1)}, bf16[512,256]{1,0:T(8,128)(2,1)S(1)}, bf16[512,256]{1,0:T(8,128)(2,1)S(1)}) custom-call(s32[4]{0:T(128)S(1)} %fusion.1.slot_ref, bf16[512,512]{1,0:T(8,128)(2,1)S(1)} %bitcast.20, bf16[512,512]{1,0:T(8,128)(2,1)S(1)} %collective-permute-done.1.refs_3_.refs_1_, ...), custom_call_target="tpu_custom_call" | custom-call | tf_op jit(solution)/shard_map/pallas_call | solution.py:23
  81.5 1.3 %collective-permute-start.23 = (bf16[512,256]{1,0:T(8,128)(2,1)S(1)}, bf16[512,256]{1,0:T(8,128)(2,1)S(1)}, u32[]{:S(2)}, u32[]{:S(2)}) collective-permute-start(bf16[512,256]{1,0:T(8,128)(2,1)S(1)} %get-tuple-element.24), channel_id=1, source_target_pairs={{0,8},{4,12},{24,16},{28,20},{1,9},{5,13},{25,17},{29,21},{2,10},{... | collective-permute-start | bytes 786440 | tf_op jit(solution)/shard_map/ppermute | solution.py:151
  82.8 1.3 %collective-permute-start.26 = (bf16[512,256]{1,0:T(8,128)(2,1)S(1)}, bf16[512,256]{1,0:T(8,128)(2,1)S(1)}, u32[]{:S(2)}, u32[]{:S(2)}) collective-permute-start(bf16[512,256]{1,0:T(8,128)(2,1)S(1)} %get-tuple-element.25), channel_id=1, source_target_pairs={{0,8},{4,12},{24,16},{28,20},{1,9},{5,13},{25,17},{29,21},{2,10},{... | collective-permute-start | bytes 786440 | tf_op jit(solution)/shard_map/ppermute | solution.py:151
  84.1 1.1 add_convert_fusion.5
  85.2 0.7 collective-permute-start.18
  85.9 1.0 add_convert_fusion.3
  87.0 0.9 collective-permute-start.21
  87.9 1.7 %collective-permute-done.23 = bf16[512,256]{1,0:T(8,128)(2,1)S(1)} collective-permute-done((bf16[512,256]{1,0:T(8,128)(2,1)S(1)}, bf16[512,256]{1,0:T(8,128)(2,1)S(1)}, u32[]{:S(2)}, u32[]{:S(2)}) %collective-permute-start.23) | collective-permute-done | bytes 262176 | tf_op jit(solution)/shard_map/ppermute | solution.py:151
  90.3 3.2 %collective-permute-done.26 = bf16[512,256]{1,0:T(8,128)(2,1)S(1)} collective-permute-done((bf16[512,256]{1,0:T(8,128)(2,1)S(1)}, bf16[512,256]{1,0:T(8,128)(2,1)S(1)}, u32[]{:S(2)}, u32[]{:S(2)}) %collective-permute-start.26) | collective-permute-done | bytes 262176 | tf_op jit(solution)/shard_map/ppermute | solution.py:151
  93.6 0.7 collective-permute-start.27
  94.4 7.9 %collective-permute-start.19 = (bf16[512,256]{1,0:T(8,128)(2,1)S(1)}, bf16[512,256]{1,0:T(8,128)(2,1)S(1)}, u32[]{:S(2)}, u32[]{:S(2)}) collective-permute-start(bf16[512,256]{1,0:T(8,128)(2,1)S(1)} %add_convert_fusion.4), channel_id=1, source_target_pairs={{0,8},{4,12},{8,0},{12,4},{16,24},{20,28},{24,16},{28,20},{1,9},{5... | collective-permute-start | bytes 786440 | tf_op jit(solution)/shard_map/ppermute | solution.py:151
  102.4 7.0 %collective-permute-start.25 = (bf16[512,256]{1,0:T(8,128)(2,1)S(1)}, bf16[512,256]{1,0:T(8,128)(2,1)S(1)}, u32[]{:S(2)}, u32[]{:S(2)}) collective-permute-start(bf16[512,256]{1,0:T(8,128)(2,1)S(1)} %add_convert_fusion.1), channel_id=1, source_target_pairs={{0,8},{4,12},{8,0},{12,4},{16,24},{20,28},{24,16},{28,20},{1,9},{5... | collective-permute-start | bytes 786440 | tf_op jit(solution)/shard_map/ppermute | solution.py:151
  109.3 1.0 add_convert_fusion.6.later_ref
  110.4 4.5 %shard_map.96 = (bf16[512,512]{1,0:T(8,128)(2,1)}, bf16[512,512]{1,0:T(8,128)(2,1)}, bf16[512,512]{1,0:T(8,128)(2,1)}) custom-call(bf16[512,512]{1,0:T(8,128)(2,1)S(1)} %copy-done, bf16[512,512]{1,0:T(8,128)(2,1)S(1)} %copy-done.3, bf16[512,512]{1,0:T(8,128)(2,1)S(1)} %copy-done.6, bf16[512,512]{1,0:T(8,128)(2,1)S(1)} %copy-done.8, ...), custom_call_target="tpu_custom_call" | custom-call | tf_op jit(solution)/shard_map/pallas_call | solution.py:23
  115.1 1.1 pad_maximum_fusion
  (72 shorter events, 4.4 us)
Async XLA Ops:
  2.5 8.3 %copy-start.1 = (bf16[512,512]{1,0:T(8,128)(2,1)S(1)}, bf16[512,512]{1,0:T(8,128)(2,1)}, u32[]{:S(2)}) copy-start(bf16[512,512]{1,0:T(8,128)(2,1)} %k_ref.3) | copy-start | bytes 1572868
  2.5 8.3 %copy-start.4 = (bf16[512,512]{1,0:T(8,128)(2,1)S(1)}, bf16[512,512]{1,0:T(8,128)(2,1)}, u32[]{:S(2)}) copy-start(bf16[512,512]{1,0:T(8,128)(2,1)} %v_ref.3) | copy-start | bytes 1572868
  2.5 36.2 %copy-start = (bf16[512,512]{1,0:T(8,128)(2,1)S(1)}, bf16[512,512]{1,0:T(8,128)(2,1)}, u32[]{:S(2)}) copy-start(bf16[512,512]{1,0:T(8,128)(2,1)} %q_ref.7) | copy-start | bytes 1572868
  4.8 25.5 %collective-permute-start.3 = (bf16[512,512]{1,0:T(8,128)(2,1)S(1)}, bf16[512,512]{1,0:T(8,128)(2,1)S(1)}, u32[]{:S(2)}, u32[]{:S(2)}) collective-permute-start(bf16[512,512]{1,0:T(8,128)(2,1)S(1)} %bitcast.16), channel_id=1, source_target_pairs={{0,2},{1,3},{2,0},{3,1},{4,6},{5,7},{6,4},{7,5},{8,10},{9,11},{10,... | collective-permute-start | bytes 1572872 | tf_op jit(solution)/shard_map/ppermute | solution.py:114
  8.8 22.3 %collective-permute-start.2 = (bf16[512,512]{1,0:T(8,128)(2,1)}, bf16[512,512]{1,0:T(8,128)(2,1)}, u32[]{:S(2)}, u32[]{:S(2)}) collective-permute-start(bf16[512,512]{1,0:T(8,128)(2,1)} %bitcast.15.refs_0_), channel_id=1, source_target_pairs={{0,2},{1,3},{2,0},{3,1},{4,6},{5,7},{6,4},{7,5},{8,10},{9,11},{10,... | collective-permute-start | bytes 1572872 | tf_op jit(solution)/shard_map/ppermute | solution.py:114
  8.8 22.3 %collective-permute-start.12 = (bf16[512,512]{1,0:T(8,128)(2,1)}, bf16[512,512]{1,0:T(8,128)(2,1)}, u32[]{:S(2)}, u32[]{:S(2)}) collective-permute-start(bf16[512,512]{1,0:T(8,128)(2,1)} %bitcast.15.refs_0_), channel_id=1, source_target_pairs={{0,4},{4,0},{8,12},{12,8},{16,20},{20,16},{24,28},{28,24},{1,5},{5... | collective-permute-start | bytes 1572872 | tf_op jit(solution)/shard_map/ppermute | solution.py:114
  11.2 14.1 %collective-permute-start.6 = (bf16[512,128]{1,0:T(8,128)(2,1)S(1)}, bf16[512,128]{1,0:T(8,128)(2,1)S(1)}, u32[]{:S(2)}, u32[]{:S(2)}) collective-permute-start(bf16[512,128]{1,0:T(8,128)(2,1)S(1)} %shard_map.94), channel_id=1, source_target_pairs={{0,4},{4,0},{8,12},{12,8},{16,20},{20,16},{24,28},{28,24},{1,5},{5... | collective-permute-start | bytes 393224 | tf_op jit(solution)/shard_map/ppermute | solution.py:114
  25.3 5.0 %collective-permute-start.7 = (bf16[512,128]{1,0:T(8,128)(2,1)S(1)}, bf16[512,128]{1,0:T(8,128)(2,1)S(1)}, u32[]{:S(2)}, u32[]{:S(2)}) collective-permute-start(bf16[512,128]{1,0:T(8,128)(2,1)S(1)} %add_convert_fusion.13), channel_id=1, source_target_pairs={{0,8},{4,12},{8,0},{12,4},{16,24},{20,28},{24,16},{28,20},{1,9},{5... | collective-permute-start | bytes 393224 | tf_op jit(solution)/shard_map/ppermute | solution.py:114
  27.1 6.5 %collective-permute-start.1 = (bf16[512,512]{1,0:T(8,128)(2,1)S(1)}, bf16[512,512]{1,0:T(8,128)(2,1)S(1)}, u32[]{:S(2)}, u32[]{:S(2)}) collective-permute-start(bf16[512,512]{1,0:T(8,128)(2,1)S(1)} %bitcast.17), channel_id=1, source_target_pairs={{0,1},{1,0},{2,3},{3,2},{4,5},{5,4},{6,7},{7,6},{8,9},{9,8},{10,11... | collective-permute-start | bytes 1572872 | tf_op jit(solution)/shard_map/ppermute | solution.py:114
  30.3 12.0 %collective-permute-start = (bf16[512,512]{1,0:T(8,128)(2,1)}, bf16[512,512]{1,0:T(8,128)(2,1)}, u32[]{:S(2)}, u32[]{:S(2)}) collective-permute-start(bf16[512,512]{1,0:T(8,128)(2,1)} %bitcast.15.refs_0_), channel_id=1, source_target_pairs={{0,1},{1,0},{2,3},{3,2},{4,5},{5,4},{6,7},{7,6},{8,9},{9,8},{10,11... | collective-permute-start | bytes 1572872 | tf_op jit(solution)/shard_map/ppermute | solution.py:114
  30.3 12.1 %collective-permute-start.5 = (bf16[512,512]{1,0:T(8,128)(2,1)S(1)}, bf16[512,512]{1,0:T(8,128)(2,1)}, u32[]{:S(2)}, u32[]{:S(2)}) collective-permute-start(bf16[512,512]{1,0:T(8,128)(2,1)S(1)} %collective-permute-done.3.refs_5_.refs_2_), channel_id=1, source_target_pairs={{0,1},{1,0},{2,3},{3,2},{4,5},{5,4},{6,7},{7,6},{8,9},{9,8},{10,11... | collective-permute-start | bytes 1572872 | tf_op jit(solution)/shard_map/ppermute | solution.py:114
  31.1 11.3 %collective-permute-start.4 = (bf16[512,512]{1,0:T(8,128)(2,1)}, bf16[512,512]{1,0:T(8,128)(2,1)}, u32[]{:S(2)}, u32[]{:S(2)}) collective-permute-start(bf16[512,512]{1,0:T(8,128)(2,1)} %collective-permute-done.2.refs_4_), channel_id=1, source_target_pairs={{0,1},{1,0},{2,3},{3,2},{4,5},{5,4},{6,7},{7,6},{8,9},{9,8},{10,11... | collective-permute-start | bytes 1572872 | tf_op jit(solution)/shard_map/ppermute | solution.py:114
  31.1 19.3 %collective-permute-start.14 = (bf16[512,512]{1,0:T(8,128)(2,1)}, bf16[512,512]{1,0:T(8,128)(2,1)}, u32[]{:S(2)}, u32[]{:S(2)}) collective-permute-start(bf16[512,512]{1,0:T(8,128)(2,1)} %collective-permute-done.12.refs_4_), channel_id=1, source_target_pairs={{0,2},{1,3},{2,0},{3,1},{4,6},{5,7},{6,4},{7,5},{8,10},{9,11},{10,... | collective-permute-start | bytes 1572872 | tf_op jit(solution)/shard_map/ppermute | solution.py:114
  33.6 17.1 %collective-permute-start.8 = (bf16[512,128]{1,0:T(8,128)(2,1)}, bf16[512,128]{1,0:T(8,128)(2,1)}, u32[]{:S(2)}, u32[]{:S(2)}) collective-permute-start(bf16[512,128]{1,0:T(8,128)(2,1)} %add_convert_fusion.11), channel_id=1, source_target_pairs={{0,16},{4,20},{8,24},{12,28},{1,17},{5,21},{9,25},{13,29},{2,18},{... | collective-permute-start | bytes 393224 | tf_op jit(solution)/shard_map/ppermute | solution.py:114
  38.7 1.0 copy-start.2
  39.7 1.0 copy-start.5
  42.3 18.4 %collective-permute-start.13 = (bf16[512,512]{1,0:T(8,128)(2,1)}, bf16[512,512]{1,0:T(8,128)(2,1)S(1)}, u32[]{:S(2)}, u32[]{:S(2)}) collective-permute-start(bf16[512,512]{1,0:T(8,128)(2,1)} %collective-permute-done.12.refs_4_), channel_id=1, source_target_pairs={{0,1},{1,0},{2,3},{3,2},{4,5},{5,4},{6,7},{7,6},{8,9},{9,8},{10,11... | collective-permute-start | bytes 1572872 | tf_op jit(solution)/shard_map/ppermute | solution.py:114
  48.1 0.8 copy-start.7
  48.9 6.3 %collective-permute-start.9 = (bf16[512,128]{1,0:T(8,128)(2,1)S(1)}, bf16[512,128]{1,0:T(8,128)(2,1)S(1)}, u32[]{:S(2)}, u32[]{:S(2)}) collective-permute-start(bf16[512,128]{1,0:T(8,128)(2,1)S(1)} %shard_map.95), channel_id=1, source_target_pairs={{0,4},{4,0},{8,12},{12,8},{16,20},{20,16},{24,28},{28,24},{1,5},{5... | collective-permute-start | bytes 393224 | tf_op jit(solution)/shard_map/ppermute | solution.py:114
  50.5 10.3 %collective-permute-start.15 = (bf16[512,512]{1,0:T(8,128)(2,1)}, bf16[512,512]{1,0:T(8,128)(2,1)S(1)}, u32[]{:S(2)}, u32[]{:S(2)}) collective-permute-start(bf16[512,512]{1,0:T(8,128)(2,1)} %collective-permute-done.14.refs_6_), channel_id=1, source_target_pairs={{0,1},{1,0},{2,3},{3,2},{4,5},{5,4},{6,7},{7,6},{8,9},{9,8},{10,11... | collective-permute-start | bytes 1572872 | tf_op jit(solution)/shard_map/ppermute | solution.py:114
  51.0 9.8 %collective-permute-start.16 = (bf16[512,256]{1,0:T(8,128)(2,1)S(1)}, bf16[512,256]{1,0:T(8,128)(2,1)S(1)}, u32[]{:S(2)}, u32[]{:S(2)}) collective-permute-start(bf16[512,256]{1,0:T(8,128)(2,1)S(1)} %shard_map.98.refs_8_), channel_id=1, source_target_pairs={{0,4},{4,0},{8,12},{12,8},{16,20},{20,16},{24,28},{28,24},{1,5},{5... | collective-permute-start | bytes 786440 | tf_op jit(solution)/shard_map/ppermute | solution.py:114
  55.2 5.5 %copy-start.15 = (bf16[512,128]{1,0:T(8,128)(2,1)}, bf16[512,128]{1,0:T(8,128)(2,1)S(1)}, u32[]{:S(2)}) copy-start(bf16[512,128]{1,0:T(8,128)(2,1)S(1)} %collective-permute-done.9) | copy-start | bytes 393220
  55.9 15.9 %collective-permute-start.10 = (bf16[512,128]{1,0:T(8,128)(2,1)}, bf16[512,128]{1,0:T(8,128)(2,1)}, u32[]{:S(2)}, u32[]{:S(2)}) collective-permute-start(bf16[512,128]{1,0:T(8,128)(2,1)} %add_convert_fusion.9), channel_id=1, source_target_pairs={{0,8},{4,12},{8,0},{12,4},{16,24},{20,28},{24,16},{28,20},{1,9},{5... | collective-permute-start | bytes 393224 | tf_op jit(solution)/shard_map/ppermute | solution.py:114
  58.4 15.9 %collective-permute-start.22 = (bf16[512,256]{1,0:T(8,128)(2,1)S(1)}, bf16[512,256]{1,0:T(8,128)(2,1)S(1)}, u32[]{:S(2)}, u32[]{:S(2)}) collective-permute-start(bf16[512,256]{1,0:T(8,128)(2,1)S(1)} %shard_map.100.refs_8_), channel_id=1, source_target_pairs={{0,4},{4,0},{8,12},{12,8},{16,20},{20,16},{24,28},{28,24},{1,5},{5... | collective-permute-start | bytes 786440 | tf_op jit(solution)/shard_map/ppermute | solution.py:114
  60.8 4.6 %copy-start.11 = (bf16[512,512]{1,0:T(8,128)(2,1)}, bf16[512,512]{1,0:T(8,128)(2,1)S(1)}, u32[]{:S(2)}) copy-start(bf16[512,512]{1,0:T(8,128)(2,1)S(1)} %collective-permute-done.15.refs_7_) | copy-start | bytes 1572868
  65.4 0.8 copy-start.9
  66.2 18.0 %collective-permute-start.17 = (bf16[512,256]{1,0:T(8,128)(2,1)}, bf16[512,256]{1,0:T(8,128)(2,1)}, u32[]{:S(2)}, u32[]{:S(2)}) collective-permute-start(bf16[512,256]{1,0:T(8,128)(2,1)} %get-tuple-element.20), channel_id=1, source_target_pairs={{0,8},{4,12},{24,16},{28,20},{1,9},{5,13},{25,17},{29,21},{2,10},{... | collective-permute-start | bytes 786440 | tf_op jit(solution)/shard_map/ppermute | solution.py:151
  70.5 15.4 %collective-permute-start.20 = (bf16[512,256]{1,0:T(8,128)(2,1)}, bf16[512,256]{1,0:T(8,128)(2,1)S(1)}, u32[]{:S(2)}, u32[]{:S(2)}) collective-permute-start(bf16[512,256]{1,0:T(8,128)(2,1)} %get-tuple-element.21), channel_id=1, source_target_pairs={{0,8},{4,12},{24,16},{28,20},{1,9},{5,13},{25,17},{29,21},{2,10},{... | collective-permute-start | bytes 786440 | tf_op jit(solution)/shard_map/ppermute | solution.py:151
  71.8 37.5 %copy-start.16 = (bf16[512,128]{1,0:T(8,128)(2,1)S(1)}, bf16[512,128]{1,0:T(8,128)(2,1)}, u32[]{:S(2)}) copy-start(bf16[512,128]{1,0:T(8,128)(2,1)} %copy-done.15) | copy-start | bytes 393220
  72.9 37.5 %copy-start.3 = (bf16[512,512]{1,0:T(8,128)(2,1)S(1)}, bf16[512,512]{1,0:T(8,128)(2,1)}, u32[]{:S(2)}) copy-start(bf16[512,512]{1,0:T(8,128)(2,1)} %k_ref.3) | copy-start | bytes 1572868
  72.9 37.5 %copy-start.6 = (bf16[512,512]{1,0:T(8,128)(2,1)S(1)}, bf16[512,512]{1,0:T(8,128)(2,1)}, u32[]{:S(2)}) copy-start(bf16[512,512]{1,0:T(8,128)(2,1)} %v_ref.3) | copy-start | bytes 1572868
  72.9 37.5 %copy-start.8 = (bf16[512,512]{1,0:T(8,128)(2,1)S(1)}, bf16[512,512]{1,0:T(8,128)(2,1)}, u32[]{:S(2)}) copy-start(bf16[512,512]{1,0:T(8,128)(2,1)} %copy-done.7) | copy-start | bytes 1572868
  72.9 36.5 %collective-permute-start.11 = (bf16[512,128]{1,0:T(8,128)(2,1)S(1)}, bf16[512,128]{1,0:T(8,128)(2,1)S(1)}, u32[]{:S(2)}, u32[]{:S(2)}) collective-permute-start(bf16[512,128]{1,0:T(8,128)(2,1)S(1)} %add_convert_fusion.7), channel_id=1, source_target_pairs={{16,0},{20,4},{24,8},{28,12},{17,1},{21,5},{25,9},{29,13},{18,2},{... | collective-permute-start | bytes 393224 | tf_op jit(solution)/shard_map/ppermute | solution.py:114
  74.3 0.7 copy-start.13
  75.0 1.0 copy-start.10
  76.1 1.0 copy-start.12
  77.1 0.9 copy-start.14
  81.5 8.0 %collective-permute-start.23 = (bf16[512,256]{1,0:T(8,128)(2,1)S(1)}, bf16[512,256]{1,0:T(8,128)(2,1)S(1)}, u32[]{:S(2)}, u32[]{:S(2)}) collective-permute-start(bf16[512,256]{1,0:T(8,128)(2,1)S(1)} %get-tuple-element.24), channel_id=1, source_target_pairs={{0,8},{4,12},{24,16},{28,20},{1,9},{5,13},{25,17},{29,21},{2,10},{... | collective-permute-start | bytes 786440 | tf_op jit(solution)/shard_map/ppermute | solution.py:151
  82.8 10.7 %collective-permute-start.26 = (bf16[512,256]{1,0:T(8,128)(2,1)S(1)}, bf16[512,256]{1,0:T(8,128)(2,1)S(1)}, u32[]{:S(2)}, u32[]{:S(2)}) collective-permute-start(bf16[512,256]{1,0:T(8,128)(2,1)S(1)} %get-tuple-element.25), channel_id=1, source_target_pairs={{0,8},{4,12},{24,16},{28,20},{1,9},{5,13},{25,17},{29,21},{2,10},{... | collective-permute-start | bytes 786440 | tf_op jit(solution)/shard_map/ppermute | solution.py:151
  85.2 9.0 %collective-permute-start.18 = (bf16[512,256]{1,0:T(8,128)(2,1)S(1)}, bf16[512,256]{1,0:T(8,128)(2,1)S(1)}, u32[]{:S(2)}, u32[]{:S(2)}) collective-permute-start(bf16[512,256]{1,0:T(8,128)(2,1)S(1)} %add_convert_fusion.5), channel_id=1, source_target_pairs={{8,16},{12,20},{16,8},{20,12},{9,17},{13,21},{17,9},{21,13},{10,18... | collective-permute-start | bytes 786440 | tf_op jit(solution)/shard_map/ppermute | solution.py:151
  87.0 27.9 %collective-permute-start.21 = (bf16[512,256]{1,0:T(8,128)(2,1)S(1)}, bf16[512,256]{1,0:T(8,128)(2,1)S(1)}, u32[]{:S(2)}, u32[]{:S(2)}) collective-permute-start(bf16[512,256]{1,0:T(8,128)(2,1)S(1)} %add_convert_fusion.3), channel_id=1, source_target_pairs={{8,16},{12,20},{16,8},{20,12},{9,17},{13,21},{17,9},{21,13},{10,18... | collective-permute-start | bytes 786440 | tf_op jit(solution)/shard_map/ppermute | solution.py:151
  89.6 12.7 %collective-permute-start.24 = (bf16[512,256]{1,0:T(8,128)(2,1)S(1)}, bf16[512,256]{1,0:T(8,128)(2,1)S(1)}, u32[]{:S(2)}, u32[]{:S(2)}) collective-permute-start(bf16[512,256]{1,0:T(8,128)(2,1)S(1)} %add_convert_fusion.2), channel_id=1, source_target_pairs={{8,16},{12,20},{16,8},{20,12},{9,17},{13,21},{17,9},{21,13},{10,18... | collective-permute-start | bytes 786440 | tf_op jit(solution)/shard_map/ppermute | solution.py:151
  93.6 21.4 %collective-permute-start.27 = (bf16[512,256]{1,0:T(8,128)(2,1)S(1)}, bf16[512,256]{1,0:T(8,128)(2,1)S(1)}, u32[]{:S(2)}, u32[]{:S(2)}) collective-permute-start(bf16[512,256]{1,0:T(8,128)(2,1)S(1)} %add_convert_fusion), channel_id=1, source_target_pairs={{8,16},{12,20},{16,8},{20,12},{9,17},{13,21},{17,9},{21,13},{10,18... | collective-permute-start | bytes 786440 | tf_op jit(solution)/shard_map/ppermute | solution.py:151
  94.4 20.5 %collective-permute-start.19 = (bf16[512,256]{1,0:T(8,128)(2,1)S(1)}, bf16[512,256]{1,0:T(8,128)(2,1)S(1)}, u32[]{:S(2)}, u32[]{:S(2)}) collective-permute-start(bf16[512,256]{1,0:T(8,128)(2,1)S(1)} %add_convert_fusion.4), channel_id=1, source_target_pairs={{0,8},{4,12},{8,0},{12,4},{16,24},{20,28},{24,16},{28,20},{1,9},{5... | collective-permute-start | bytes 786440 | tf_op jit(solution)/shard_map/ppermute | solution.py:151
  102.4 12.6 %collective-permute-start.25 = (bf16[512,256]{1,0:T(8,128)(2,1)S(1)}, bf16[512,256]{1,0:T(8,128)(2,1)S(1)}, u32[]{:S(2)}, u32[]{:S(2)}) collective-permute-start(bf16[512,256]{1,0:T(8,128)(2,1)S(1)} %add_convert_fusion.1), channel_id=1, source_target_pairs={{0,8},{4,12},{8,0},{12,4},{16,24},{20,28},{24,16},{28,20},{1,9},{5... | collective-permute-start | bytes 786440 | tf_op jit(solution)/shard_map/ppermute | solution.py:151

commit v2 on v0

v2 whole, which is shorter than its diff:
```python
import functools
import math

import jax
import jax.numpy as jnp
from jax import lax
from jax.experimental import pallas as pl
from jax.experimental.pallas import tpu as pltpu
from jax.sharding import PartitionSpec as P

HD = 128
BF16 = jnp.bfloat16
F32 = jnp.float32


def dot(a, b, on_a=1, on_b=0):
    return lax.dot_general(a, b, (((on_a,), (on_b,)), ((), ())), preferred_element_type=F32)


def call(body, outs, *args, scratch=None, cost=1, vmem=12):
    scratch = [(a.shape, a.dtype) for a in args] if scratch is None else scratch
    count = len(args)

    def kernel(*refs):
        sources, results = refs[:count], refs[count : len(refs) - len(scratch) - 1]
        buffers, sems = refs[len(refs) - len(scratch) - 1 : -1], refs[-1]
        body(sources, results, buffers, sems)

    return pl.pallas_call(
        kernel,
        out_shape=outs,
        in_specs=[pl.BlockSpec(memory_space=pl.ANY)] * count,
        out_specs=jax.tree.map(lambda _: pl.BlockSpec(memory_space=pltpu.VMEM), outs),
        scratch_shapes=[pltpu.VMEM(*buffer) for buffer in scratch]
        + [pltpu.SemaphoreType.DMA((count + len(scratch),))],
        compiler_params=pltpu.CompilerParams(vmem_limit_bytes=vmem << 20),
        cost_estimate=pl.CostEstimate(flops=cost << 20, bytes_accessed=1 << 14, transcendentals=0),
    )(*args)


def fetch(sources, buffers, sems):
    copies = [
        pltpu.make_async_copy(source, buffer, sems.at[i])
        for i, (source, buffer) in enumerate(zip(sources, buffers))
    ]
    for copy in copies:
        copy.start()

    def wait(i):
        copies[i].wait()
        return buffers[i]

    return wait


def head(h):
    return slice(h * HD, (h + 1) * HD)


def state_body(scale, sources, results, buffers, sems):
    split = None
    if len(sources) > 2:
        width = results[1].shape[1]
        first = (1 - lax.rem(lax.axis_index("seq"), 2)) * width
        half = sources[2].at[:, pl.ds(pl.multiple_of(first, width), width)]
        split = pltpu.make_async_copy(half, results[1], sems.at[len(buffers)])
    wait = fetch(sources[:2], buffers, sems)
    if split is not None:
        split.start()
    a_ref, b_ref = wait(0), wait(1)
    for h in range(a_ref.shape[1] // HD):
        term = dot(a_ref[:, head(h)], b_ref[:, head(h)], 0, 0)
        results[0][head(h), :] = (scale * term).astype(BF16)
    if split is not None:
        split.wait()


def masked(scale, a, b, row):
    scores = scale * dot(a, b, 1, 1)
    rows = row + lax.broadcasted_iota(jnp.int32, scores.shape, 0)
    return jnp.where(lax.broadcasted_iota(jnp.int32, scores.shape, 1) <= rows, scores, 0.0).astype(BF16)


def inner_body(scale, part, sources, results, buffers, sems):
    wait = fetch(sources, buffers, sems)
    q_ref, k_ref, v_ref = wait(0), wait(1), wait(2)
    for h in range(q_ref.shape[1] // HD):
        for row in range(0, q_ref.shape[0], part):
            end = row + part
            probs = masked(scale, q_ref[row:end, head(h)], k_ref[:end, head(h)], row)
            results[0][row:end, head(h)] = dot(probs, v_ref[:end, head(h)])


def outputs_body(sources, results, buffers, sems):
    wait = fetch(sources, buffers, sems)
    prior_ref, q_ref, pv_ref = wait(0), wait(1), wait(2)
    for h in range(q_ref.shape[1] // HD):
        total = pv_ref[:, head(h)] + dot(q_ref[:, head(h)], prior_ref[head(h), :])
        results[0][:, head(h)] = total.astype(BF16)


def attn_grad_body(sources, results, buffers, sems):
    wait = fetch(sources, buffers, sems)
    me = lax.axis_index("head")
    w_ref = wait(0)
    total = None
    for j in range(len(sources) - 1):
        piece = wait(j + 1)
        depth = piece.shape[1]
        rows = pl.ds(pl.multiple_of((me ^ j) * depth, depth), depth)
        term = dot(piece[...], w_ref[rows, :])
        total = term if total is None else total + term
    results[0][...] = total.astype(BF16)


def grads_body(scale, part, sources, results, buffers, sems):
    wait = fetch(sources, buffers, sems)
    q_ref, k_ref, v_ref, d_ref, prior_ref, later_ref = (wait(i) for i in range(6))
    dq_ref, dk_ref, dv_ref = results
    rows = q_ref.shape[0]
    for h in range(q_ref.shape[1] // HD):
        at = head(h)
        dk = dot(v_ref[:, at], later_ref[at, :], 1, 1)
        dv = dot(k_ref[:, at], later_ref[at, :])
        dk_parts = [dk[r : r + part] for r in range(0, rows, part)]
        dv_parts = [dv[r : r + part] for r in range(0, rows, part)]
        for row in range(0, rows, part):
            end = row + part
            q, d = q_ref[row:end, at], d_ref[row:end, at]
            probs = masked(scale, q, k_ref[:end, at], row)
            grads = masked(scale, d, v_ref[:end, at], row)
            dq = dot(grads, k_ref[:end, at]) + dot(d, prior_ref[at, :], 1, 1)
            dq_ref[row:end, at] = dq.astype(BF16)
            for i, r in enumerate(range(0, end, part)):
                dk_parts[i] += dot(grads[:, r : r + part], q, 0, 0)
                dv_parts[i] += dot(probs[:, r : r + part], d, 0, 0)
        for i, r in enumerate(range(0, rows, part)):
            dk_ref[r : r + part, at] = dk_parts[i].astype(BF16)
            dv_ref[r : r + part, at] = dv_parts[i].astype(BF16)


def slot(z, i):
    at = jnp.int32(ORDER[-1][i])
    for p in range(len(ORDER) - 1):
        at = jnp.where(z == p, ORDER[p][i], at)
    return at


def product_body(factor, count, short, slots, sources, results, buffers, sems):
    used = len(slots)
    seq, me = lax.axis_index("seq"), lax.axis_index("head")
    o, n = (pltpu.make_async_copy(sources[i], buffers[i], sems.at[i]) for i in range(2))
    o.start()
    n.start()
    copies = []
    for i, s in enumerate(slots):
        which = (slot(lax.div(seq, 2), s) if short else s) ^ me
        for part in range(2):
            at = 2 + part * used + i
            for j in range(count):

                @pl.when(which == j)
                def _():
                    piece = sources[2 + part * count + j]
                    width = buffers[at].shape[1]
                    if piece.shape[1] != width:
                        first = pl.multiple_of(lax.rem(seq, 2) * width, width)
                        piece = piece.at[:, pl.ds(first, width)]
                    pltpu.make_async_copy(piece, buffers[at], sems.at[at]).start()

            copies.append(pltpu.make_async_copy(buffers[at], buffers[at], sems.at[at]))
    o.wait()
    n.wait()
    for i, out in enumerate(results):
        copies[2 * i].wait()
        copies[2 * i + 1].wait()
        total = dot(buffers[2 + i][...], buffers[0][...], 0, 0)
        total += dot(buffers[2 + used + i][...], buffers[1][...], 0, 0)
        out[...] = (factor * total).astype(out.dtype)


def phase(*values):
    return lax.optimization_barrier(values)


def flip(a, axis, bit):
    return lax.ppermute(a, axis, [(i, i ^ bit) for i in range(lax.axis_size(axis))])


def add(a, b):
    return (a.astype(F32) + b.astype(F32)).astype(BF16)


class Scan:
    def __init__(self, term, later):
        self.term, self.later, self.total, self.before = term, later, term, 0.0
        self.bits = [1 << i for i in range(lax.axis_size("seq").bit_length() - 1)]

    def inside(self, bit):
        return ((lax.axis_index("seq") & bit) != 0) != self.later

    def start(self, bit):
        return flip(self.total, "seq", bit)

    def take(self, bit, got):
        self.before += jnp.where(self.inside(bit), got, 0).astype(F32)
        self.total = add(self.total, got)

    def across(self):
        own = jnp.where(self.inside(1), 0, self.term).astype(F32)
        return flip((self.before + own).astype(BF16), "seq", 1)

    def result(self, got=0.0):
        return (self.before + got).astype(BF16)


def send(a, pairs):
    return lax.ppermute(a, "seq", [(2 * s + i, 2 * t + i) for s, t in pairs for i in range(2)])


OUTER = ((0, 1), (1, 0), (2, 3), (3, 2))
MIDDLE = ((1, 2), (2, 1))
ORDER = ((3, 2, 1, 0), (3, 2, 0, 1), (0, 1, 3, 2), (0, 1, 2, 3))


def per_device(queries, keys, values, out_grad, out_weight):
    rows, width = queries.shape
    n_seq, n_head = lax.axis_size("seq"), lax.axis_size("head")
    seq = lax.axis_index("seq")
    y = seq % 2
    line = n_seq // 2
    total = n_seq * rows
    scale = 1.0 / math.sqrt(HD * total)
    factor = 1.0 / math.sqrt(total)
    part = 256
    shaped = lambda dims, dtype=BF16: jax.ShapeDtypeStruct(dims, dtype)
    state = functools.partial(state_body, scale)
    state_shape = shaped((width, HD))

    cols = out_grad.shape[1]
    block = cols * n_head // n_seq
    short = line == 4 and n_head == 4

    def half(a, i):
        cut = a.reshape(rows, cols // (2 * block), 2, block)
        return lax.dynamic_index_in_dim(cut, i, 2, keepdims=False).reshape(rows, cols // 2)

    inner = functools.partial(inner_body, scale, part)
    outputs = outputs_body
    matrix = shaped((rows, width))

    def product(slots, kinds, *operands, cost=1):
        body = functools.partial(product_body, factor, n_head, short, slots)
        outs = [shaped((cols // 2, width), kind) for kind in kinds]
        like = [((rows, cols // 2), BF16)] * (2 * len(slots))
        scratch = [((rows, width), BF16)] * 2 + like
        return call(body, outs, *operands, scratch=scratch, cost=cost, vmem=60)

    by_x = flip(out_grad, "head", 2)
    if short:
        scratch = [((rows, width), BF16)] * 2
        outs = [state_shape, shaped((rows, cols // 2))]
        kv_term, other = call(state, outs, keys, values, out_grad, scratch=scratch)
    else:
        (kv_term,), other = call(state, [state_shape], keys, values), half(out_grad, 1 - y)
    prior = Scan(kv_term, False)
    got = prior.start(1)
    near = flip(other, "seq", 1)
    got, q, grad = phase(got, queries, out_grad)
    prior.take(1, got)
    for bit in prior.bits[1:]:
        got = prior.start(bit)
        if bit == 4:
            (pv,) = call(inner, [shaped((rows, width), F32)], q, keys, values)
            got, pv, grad, by_x, near = phase(got, pv, grad, by_x, near)
        prior.take(bit, got)
    prior = prior.result()

    (o,) = call(outputs, [matrix], prior, queries, pv)
    o, by_x, near, grad = phase(o, by_x, near, grad)
    n = flip(o, "seq", 1)
    far = flip(near, "head", 2)
    by_core, by_xc, near_c = (flip(a, "head", 1) for a in (grad, by_x, near))

    pieces = [out_grad, by_core, by_x, by_xc]
    mine = pieces if short else [half(p, y) for p in pieces]
    (attn_grad,) = call(attn_grad_body, [matrix], out_weight, *pieces)
    (back_term,) = call(state, [state_shape], queries, attn_grad)
    later = Scan(back_term, True)
    got = later.start(2)
    got, n, far = phase(got, n, far)
    far_c = flip(far, "head", 1)
    later.take(2, got)
    operands = (o, n, *mine, near, near_c, far, far_c)

    def gradients(later):
        body = functools.partial(grads_body, scale, part)
        return call(body, [matrix] * 3, queries, keys, values, attn_grad, prior, later)

    if short:
        got = later.start(4)
        (b0,) = product((0,), (BF16,), *operands)
        e1 = send(b0, OUTER)
        o, got, _ = phase(o, got, b0)
        b1, b2, b3 = product((1, 2, 3), (BF16, F32, F32), o, *operands[1:], cost=1 << 14)
        later.take(4, got)
        got = later.across()
        e2 = send(b1, OUTER)
        e1, got, b2 = phase(e1, got, b2)
        m2 = send(add(b0, e1), MIDDLE)
        grads = gradients(later.result(got))
        e2, *grads = phase(e2, *grads)
        m3 = send(add(b1, e2), MIDDLE)
        e3 = send(add(b2, m2), OUTER)
        weight_grad = b3 + e3.astype(F32) + m3.astype(F32)
    else:
        for bit in later.bits[1:]:
            later.take(bit, later.start(bit))
        grads = gradients(later.result(later.across()))
        groups = [[2 * p + i for p in range(line)] for i in range(2)]
        whole = jnp.concatenate(product(range(n_head), [F32] * n_head, *operands), axis=0)
        weight_grad = lax.psum_scatter(
            whole, "seq", scatter_dimension=0, axis_index_groups=groups, tiled=True
        )
    return (*grads, weight_grad)


def solution(mesh):
    return jax.shard_map(
        per_device,
        mesh=mesh,
        in_specs=(
            P("seq", "head"),
            P("seq", "head"),
            P("seq", "head"),
            P("seq", "head"),
            P(None, "head"),
        ),
        out_specs=(P("seq", "head"), P("seq", "head"), P("seq", "head"), P("seq", "head")),
        check_vma=False,
    )
```

time: 310 us -> 96.6 us (0.31)
  waiting for transfers between devices: 245 us -> 34.8 us
  starting transfers between devices: 0.16 us -> 29.6 us
  matrix products: 28.8 us -> 0 us
  Pallas kernels: 0 us -> 19.6 us
  between operations: 13.9 us -> 0.97 us
  other arithmetic: 10.4 us -> 3.02 us
    reduce_scatter x1 -> x0, waiting for transfers between devices: 139 us -> none  [per_device(): lax.psum_scatter(product * factor, 'seq', scatter_dimension=0, tiled=True)]
    all_gather x3 -> x0, waiting for transfers between devices: 105 us -> none  [the longest x1 39.5 us: per_device(): piece = lax.all_gather(kv_term[None], 'seq', axis=0, tiled=True)]
    ppermute x0 -> x19, waiting for transfers between devices: none -> 34.8 us  [the longest x5 18.7 us: send(): lax.ppermute(a, 'seq', [(2 * s + i, 2 * t + i) for s, t in pairs for i in...]
    ppermute x0 -> x19, starting transfers between devices: none -> 29.6 us  [the longest x14 18.8 us: flip(): lax.ppermute(a, axis, [(i, i ^ bit) for i in range(lax.axis_size(axis))])]
    dot_general x14 -> x0, matrix products: 28.8 us -> none  [the longest x1 5.84 us: per_device(): jnp.dot(full_grad, out_weight, preferred_element_type=jnp.float32)]
    pallas_call x0 -> x8, Pallas kernels: none -> 19.6 us  [call(): pl.pallas_call(kernel, out_shape=outs, in_specs=[pl.BlockSpec(memory_spac...]
    select_n x8 -> x0, other arithmetic: 8.32 us -> none  [turn(): return jnp.where(reached, new, before)]
    unnamed x26 -> x44, local copies, waits for them, and re-layouts: 8.98 us -> 8.09 us
  transfers between devices with their start and end apart: 4 -> 19, of which waited for: 4 -> 9; matrix products, arithmetic and copies ran while one was open for 15% -> 2% of each run, Pallas kernels for 0% -> 20%
where the time goes in v2:
time: 96.6 us; the launch traced here: 96 us
  waiting for transfers between devices  34.8 us (36%)
  starting transfers between devices  29.6 us (31%)
  Pallas kernels  19.6 us (20%)
  local copies, waits for them, and re-layouts  8.09 us (8%)
  other arithmetic  3.02 us (3%)
  between operations  0.97 us (1%)
    pallas_call x8, Pallas kernels, call(): pl.pallas_call(kernel, out_shape=outs, in_specs=[pl.BlockSpec(memory_spac...  19.6 us
    ppermute x14, starting transfers between devices, flip(): lax.ppermute(a, axis, [(i, i ^ bit) for i in range(lax.axis_size(axis))])  18.8 us
    ppermute x5, waiting for transfers between devices, send(): lax.ppermute(a, 'seq', [(2 * s + i, 2 * t + i) for s, t in pairs for i in...  18.7 us
    ppermute x14, waiting for transfers between devices, flip(): lax.ppermute(a, axis, [(i, i ^ bit) for i in range(lax.axis_size(axis))])  16.1 us
    ppermute x5, starting transfers between devices, send(): lax.ppermute(a, 'seq', [(2 * s + i, 2 * t + i) for s, t in pairs for i in...  10.8 us
    unnamed x44, local copies, waits for them, and re-layouts  8.09 us
  transfers between devices with their start and end apart: 19, of which 9 were waited for; matrix products, arithmetic and copies ran while one was open for 2% of the time, Pallas kernels for 20%

profile of v2, /device:TPU:0, one launch (start us, length us, event | category | flops | bytes accessed | tf_op | source)
XLA Modules:
  0.0 96.0 jit_solution(13645183917188729583)
XLA Ops:
  0.6 3.0 %collective-permute-start.3 = (bf16[512,1024]{1,0:T(8,128)(2,1)}, bf16[512,1024]{1,0:T(8,128)(2,1)S(1)}, u32[]{:S(2)}, u32[]{:S(2)}) collective-permute-start(bf16[512,1024]{1,0:T(8,128)(2,1)} %refs_2_.8), channel_id=1, source_target_pairs={{0,2},{1,3},{2,0},{3,1},{4,6},{5,7},{6,4},{7,5},{8,10},{9,11},{10,... | collective-permute-start | bytes 3145736 | tf_op jit(solution)/shard_map/ppermute | solution.py:187
  3.6 1.3 %copy-done = bf16[512,1024]{1,0:T(8,128)(2,1)S(1)} copy-done((bf16[512,1024]{1,0:T(8,128)(2,1)S(1)}, bf16[512,1024]{1,0:T(8,128)(2,1)}, u32[]{:S(2)}) %copy-start) | copy-done | bytes 1048600
  4.9 1.0 %copy-done.4 = bf16[512,512]{1,0:T(8,128)(2,1)S(1)} copy-done((bf16[512,512]{1,0:T(8,128)(2,1)S(1)}, bf16[512,512]{1,0:T(8,128)(2,1)}, u32[]{:S(2)}) %copy-start.4) | copy-done | bytes 524312
  5.9 1.0 %copy-done.7 = bf16[512,512]{1,0:T(8,128)(2,1)S(1)} copy-done((bf16[512,512]{1,0:T(8,128)(2,1)S(1)}, bf16[512,512]{1,0:T(8,128)(2,1)}, u32[]{:S(2)}) %copy-start.7) | copy-done | bytes 524312
  7.0 0.5 shard_map.84
  7.5 1.6 %collective-permute-start = (bf16[512,128]{1,0:T(8,128)(2,1)S(1)}, bf16[512,128]{1,0:T(8,128)(2,1)S(1)}, u32[]{:S(2)}, u32[]{:S(2)}) collective-permute-start(bf16[512,128]{1,0:T(8,128)(2,1)S(1)} %get-tuple-element.36), channel_id=1, source_target_pairs={{0,4},{4,0},{8,12},{12,8},{16,20},{20,16},{24,28},{28,24},{1,5},{5... | collective-permute-start | bytes 393224 | tf_op jit(solution)/shard_map/ppermute | solution.py:187
  9.1 0.5 collective-permute-start.4
  9.6 4.4 %collective-permute-done = bf16[512,128]{1,0:T(8,128)(2,1)S(1)} collective-permute-done((bf16[512,128]{1,0:T(8,128)(2,1)S(1)}, bf16[512,128]{1,0:T(8,128)(2,1)S(1)}, u32[]{:S(2)}, u32[]{:S(2)}) %collective-permute-start) | collective-permute-done | bytes 131104 | tf_op jit(solution)/shard_map/ppermute | solution.py:187
  14.1 1.6 %collective-permute-start.1 = (bf16[512,128]{1,0:T(8,128)(2,1)S(1)}, bf16[512,128]{1,0:T(8,128)(2,1)S(1)}, u32[]{:S(2)}, u32[]{:S(2)}) collective-permute-start(bf16[512,128]{1,0:T(8,128)(2,1)S(1)} %add_convert_fusion.8), channel_id=1, source_target_pairs={{0,8},{4,12},{8,0},{12,4},{16,24},{20,28},{24,16},{28,20},{1,9},{5... | collective-permute-start | bytes 393224 | tf_op jit(solution)/shard_map/ppermute | solution.py:187
  15.7 3.4 %collective-permute-done.1 = bf16[512,128]{1,0:T(8,128)(2,1)S(1)} collective-permute-done((bf16[512,128]{1,0:T(8,128)(2,1)S(1)}, bf16[512,128]{1,0:T(8,128)(2,1)S(1)}, u32[]{:S(2)}, u32[]{:S(2)}) %collective-permute-start.1) | collective-permute-done | bytes 131104 | tf_op jit(solution)/shard_map/ppermute | solution.py:187
  19.1 3.7 %collective-permute-start.2 = (bf16[512,128]{1,0:T(8,128)(2,1)S(1)}, bf16[512,128]{1,0:T(8,128)(2,1)}, u32[]{:S(2)}, u32[]{:S(2)}) collective-permute-start(bf16[512,128]{1,0:T(8,128)(2,1)S(1)} %add_convert_fusion.7), channel_id=1, source_target_pairs={{0,16},{4,20},{8,24},{12,28},{16,0},{20,4},{24,8},{28,12},{1,17},{... | collective-permute-start | bytes 393224 | tf_op jit(solution)/shard_map/ppermute | solution.py:187
  22.8 1.0 %copy-done.2 = bf16[512,512]{1,0:T(8,128)(2,1)S(1)} copy-done((bf16[512,512]{1,0:T(8,128)(2,1)S(1)}, bf16[512,512]{1,0:T(8,128)(2,1)}, u32[]{:S(2)}) %copy-start.2) | copy-done | bytes 524312
  23.8 1.0 %copy-done.5 = bf16[512,512]{1,0:T(8,128)(2,1)S(1)} copy-done((bf16[512,512]{1,0:T(8,128)(2,1)S(1)}, bf16[512,512]{1,0:T(8,128)(2,1)}, u32[]{:S(2)}) %copy-start.5) | copy-done | bytes 524312
  24.9 1.0 %copy-done.8 = bf16[512,512]{1,0:T(8,128)(2,1)S(1)} copy-done((bf16[512,512]{1,0:T(8,128)(2,1)S(1)}, bf16[512,512]{1,0:T(8,128)(2,1)}, u32[]{:S(2)}) %copy-start.8) | copy-done | bytes 524312
  25.9 1.6 %shard_map.85.refs_2_ = f32[512,512]{1,0:T(8,128)S(1)} custom-call(bf16[512,512]{1,0:T(8,128)(2,1)S(1)} %copy-done.2, bf16[512,512]{1,0:T(8,128)(2,1)S(1)} %copy-done.5, bf16[512,512]{1,0:T(8,128)(2,1)S(1)} %copy-done.8), custom_call_target="tpu_custom_call" | custom-call | flops 1048576 | bytes 16384 | tf_op jit(solution)/shard_map/pallas_call | solution.py:29
  27.6 0.1 add_convert_fusion.6.refs_0_.refs_4_
  27.7 0.6 shard_map.86.refs_0_
  28.4 0.5 collective-permute-start.6
  28.9 1.5 %collective-permute-start.8 = (bf16[512,512]{1,0:T(8,128)(2,1)S(1)}, bf16[512,512]{1,0:T(8,128)(2,1)S(1)}, u32[]{:S(2)}, u32[]{:S(2)}) collective-permute-start(bf16[512,512]{1,0:T(8,128)(2,1)S(1)} %shard_map.86.refs_0_), channel_id=1, source_target_pairs={{0,4},{4,0},{8,12},{12,8},{16,20},{20,16},{24,28},{28,24},{1,5},{5... | collective-permute-start | bytes 1572872 | tf_op jit(solution)/shard_map/ppermute | solution.py:187
  30.4 1.1 %collective-permute-start.9 = (bf16[512,512]{1,0:T(8,128)(2,1)}, bf16[512,512]{1,0:T(8,128)(2,1)}, u32[]{:S(2)}, u32[]{:S(2)}) collective-permute-start(bf16[512,512]{1,0:T(8,128)(2,1)} %collective-permute-done.4.refs_6_), channel_id=1, source_target_pairs={{0,2},{1,3},{2,0},{3,1},{4,6},{5,7},{6,4},{7,5},{8,10},{9,11},{10,... | collective-permute-start | bytes 1572872 | tf_op jit(solution)/shard_map/ppermute | solution.py:187
  31.6 1.0 %collective-permute-done.6.refs_4_.refs_5_ = bf16[512,1024]{1,0:T(8,128)(2,1)S(1)} collective-permute-done((bf16[512,1024]{1,0:T(8,128)(2,1)S(1)}, bf16[512,1024]{1,0:T(8,128)(2,1)S(1)}, u32[]{:S(2)}, u32[]{:S(2)}) %collective-permute-start.6) | collective-permute-done | bytes 1048608 | tf_op jit(solution)/shard_map/ppermute | solution.py:187
  32.6 3.2 %shard_map.87.refs_1_.refs_3_ = bf16[512,512]{1,0:T(8,128)(2,1)S(1)} custom-call(bf16[4096,512]{1,0:T(8,128)(2,1)S(1)} %copy-done.13, bf16[512,1024]{1,0:T(8,128)(2,1)S(1)} %copy-done.1, bf16[512,1024]{1,0:T(8,128)(2,1)S(1)} %collective-permute-done.5.refs_2_.refs_3_, bf16[512,1024]{1,0:T(8,128)(2,1)S(1)} %collective-permute-done.3.refs_3_.refs_4_, ...), custom_call_target="tpu_custom_call" | custom-call | flops 1048576 | bytes 16384 | tf_op jit(solution)/shard_map/pallas_call | solution.py:29
  35.8 0.5 shard_map.88
  36.3 1.3 %collective-permute-start.7 = (bf16[512,128]{1,0:T(8,128)(2,1)S(1)}, bf16[512,128]{1,0:T(8,128)(2,1)S(1)}, u32[]{:S(2)}, u32[]{:S(2)}) collective-permute-start(bf16[512,128]{1,0:T(8,128)(2,1)S(1)} %shard_map.88), channel_id=1, source_target_pairs={{0,8},{4,12},{8,0},{12,4},{16,24},{20,28},{24,16},{28,20},{1,9},{5... | collective-permute-start | bytes 393224 | tf_op jit(solution)/shard_map/ppermute | solution.py:187
  37.6 5.2 %collective-permute-done.8.refs_1_ = bf16[512,512]{1,0:T(8,128)(2,1)S(1)} collective-permute-done((bf16[512,512]{1,0:T(8,128)(2,1)S(1)}, bf16[512,512]{1,0:T(8,128)(2,1)S(1)}, u32[]{:S(2)}, u32[]{:S(2)}) %collective-permute-start.8) | collective-permute-done | bytes 524320 | tf_op jit(solution)/shard_map/ppermute | solution.py:187
  42.8 1.5 %collective-permute-done.9.refs_8_ = bf16[512,512]{1,0:T(8,128)(2,1)} collective-permute-done((bf16[512,512]{1,0:T(8,128)(2,1)}, bf16[512,512]{1,0:T(8,128)(2,1)}, u32[]{:S(2)}, u32[]{:S(2)}) %collective-permute-start.9) | collective-permute-done | bytes 524320 | tf_op jit(solution)/shard_map/ppermute | solution.py:187
  44.4 3.3 %collective-permute-start.10 = (bf16[512,128]{1,0:T(8,128)(2,1)S(1)}, bf16[512,128]{1,0:T(8,128)(2,1)S(1)}, u32[]{:S(2)}, u32[]{:S(2)}) collective-permute-start(bf16[512,128]{1,0:T(8,128)(2,1)S(1)} %add_convert_fusion.5), channel_id=1, source_target_pairs={{0,16},{4,20},{8,24},{12,28},{16,0},{20,4},{24,8},{28,12},{1,17},{... | collective-permute-start | bytes 393224 | tf_op jit(solution)/shard_map/ppermute | solution.py:187
  47.8 0.8 copy-done.20
  48.6 0.8 copy-done.21
  49.4 3.2 %shard_map.89 = bf16[512,512]{1,0:T(8,128)(2,1)} custom-call(bf16[512,512]{1,0:T(8,128)(2,1)} %copy-done.14, bf16[512,512]{1,0:T(8,128)(2,1)} %copy-done.19, bf16[512,1024]{1,0:T(8,128)(2,1)} %refs_2_.8, bf16[512,1024]{1,0:T(8,128)(2,1)} %copy-done.11, bf16[512,1024]{1,0:T(8,128)(2,1)} %copy-done.10, bf16[512,1024]{1,0:T(8,128)(2,1)} %copy-done.12, ...), custom_call_target="tpu_custom_call" | custom-call | flops 1048576 | bytes 16384 | tf_op jit(solution)/shard_map/pallas_call | solution.py:29
  52.5 1.6 %collective-permute-start.14 = (bf16[512,512]{1,0:T(8,128)(2,1)}, bf16[512,512]{1,0:T(8,128)(2,1)}, u32[]{:S(2)}, u32[]{:S(2)}) collective-permute-start(bf16[512,512]{1,0:T(8,128)(2,1)} %shard_map.89), channel_id=1, source_target_pairs={{0,8},{4,12},{8,0},{12,4},{16,24},{20,28},{24,16},{28,20},{1,9},{5... | collective-permute-start | bytes 1572872 | tf_op jit(solution)/shard_map/ppermute | solution.py:218
  54.2 0.6 collective-permute-done.10
  54.7 0.1 add_convert_fusion.4
  54.9 0.6 collective-permute-start.15
  55.4 4.9 %shard_map.90 = (bf16[512,512]{1,0:T(8,128)(2,1)}, f32[512,512]{1,0:T(8,128)}, f32[512,512]{1,0:T(8,128)}) custom-call(bf16[512,512]{1,0:T(8,128)(2,1)} %copy-done.14, bf16[512,512]{1,0:T(8,128)(2,1)} %copy-done.19, bf16[512,1024]{1,0:T(8,128)(2,1)} %refs_2_.8, bf16[512,1024]{1,0:T(8,128)(2,1)} %copy-done.11, bf16[512,1024]{1,0:T(8,128)(2,1)} %copy-done.10, ...), custom_call_target="tpu_custom_call" | custom-call | flops 17179869184 | bytes 16384 | tf_op jit(solution)/shard_map/pallas_call | solution.py:29
  60.4 0.8 collective-permute-start.13
  61.1 6.5 %collective-permute-done.14 = bf16[512,512]{1,0:T(8,128)(2,1)} collective-permute-done((bf16[512,512]{1,0:T(8,128)(2,1)}, bf16[512,512]{1,0:T(8,128)(2,1)}, u32[]{:S(2)}, u32[]{:S(2)}) %collective-permute-start.14) | collective-permute-done | bytes 524320 | tf_op jit(solution)/shard_map/ppermute | solution.py:218
  67.7 1.2 %add_convert_fusion.2 = bf16[512,512]{1,0:T(8,128)(2,1)S(1)} fusion(bf16[512,512]{1,0:T(8,128)(2,1)} %collective-permute-done.14, bf16[512,512]{1,0:T(8,128)(2,1)S(1)} %copy-done.15), kind=kLoop, calls=%fused_computation.3 | loop fusion | flops 1048576 | bytes 1572864 | tf_op jit(solution)/shard_map/convert_element_type | solution.py:191
  68.9 0.7 collective-permute-start.16
  69.6 0.1 add_convert_fusion.3.refs_5_
  69.7 5.0 %shard_map.91 = (bf16[512,512]{1,0:T(8,128)(2,1)}, bf16[512,512]{1,0:T(8,128)(2,1)}, bf16[512,512]{1,0:T(8,128)(2,1)}) custom-call(bf16[512,512]{1,0:T(8,128)(2,1)S(1)} %copy-done.3, bf16[512,512]{1,0:T(8,128)(2,1)S(1)} %copy-done.6, bf16[512,512]{1,0:T(8,128)(2,1)S(1)} %copy-done.9, bf16[512,512]{1,0:T(8,128)(2,1)S(1)} %shard_map.87.refs_1_.refs_3_, ...), custom_call_target="tpu_custom_call" | custom-call | flops 1048576 | bytes 16384 | tf_op jit(solution)/shard_map/pallas_call | solution.py:29
  74.7 3.4 %collective-permute-done.13 = bf16[512,512]{1,0:T(8,128)(2,1)S(1)} collective-permute-done((bf16[512,512]{1,0:T(8,128)(2,1)}, bf16[512,512]{1,0:T(8,128)(2,1)S(1)}, u32[]{:S(2)}, u32[]{:S(2)}) %collective-permute-start.13) | collective-permute-done | bytes 524320 | tf_op jit(solution)/shard_map/ppermute | solution.py:218
  78.1 0.1 add_convert_fusion
  78.2 0.7 collective-permute-start.18
  79.0 0.2 add_convert_fusion.1
  79.1 7.0 %collective-permute-start.17 = (bf16[512,512]{1,0:T(8,128)(2,1)S(1)}, bf16[512,512]{1,0:T(8,128)(2,1)S(1)}, u32[]{:S(2)}, u32[]{:S(2)}) collective-permute-start(bf16[512,512]{1,0:T(8,128)(2,1)S(1)} %add_convert_fusion.1), channel_id=1, source_target_pairs={{0,8},{4,12},{8,0},{12,4},{16,24},{20,28},{24,16},{28,20},{1,9},{5... | collective-permute-start | bytes 1572872 | tf_op jit(solution)/shard_map/ppermute | solution.py:218
  86.1 8.7 %collective-permute-done.17 = bf16[512,512]{1,0:T(8,128)(2,1)S(1)} collective-permute-done((bf16[512,512]{1,0:T(8,128)(2,1)S(1)}, bf16[512,512]{1,0:T(8,128)(2,1)S(1)}, u32[]{:S(2)}, u32[]{:S(2)}) %collective-permute-start.17) | collective-permute-done | bytes 524320 | tf_op jit(solution)/shard_map/ppermute | solution.py:218
  94.9 1.2 %convert_add_fusion = f32[512,512]{1,0:T(8,128)} fusion(bf16[512,512]{1,0:T(8,128)(2,1)S(1)} %collective-permute-done.18, f32[512,512]{1,0:T(8,128)S(1)} %copy-done.16, bf16[512,512]{1,0:T(8,128)(2,1)S(1)} %collective-permute-done.17), kind=kLoop, calls=%fused_computation | loop fusion | flops 1048576 | bytes 3145728 | tf_op jit(solution)/shard_map/add | solution.py:315
  (52 shorter events, 0.3 us)
Async XLA Ops:
  0.6 26.9 %collective-permute-start.3 = (bf16[512,1024]{1,0:T(8,128)(2,1)}, bf16[512,1024]{1,0:T(8,128)(2,1)S(1)}, u32[]{:S(2)}, u32[]{:S(2)}) collective-permute-start(bf16[512,1024]{1,0:T(8,128)(2,1)} %refs_2_.8), channel_id=1, source_target_pairs={{0,2},{1,3},{2,0},{3,1},{4,6},{5,7},{6,4},{7,5},{8,10},{9,11},{10,... | collective-permute-start | bytes 3145736 | tf_op jit(solution)/shard_map/ppermute | solution.py:187
  3.6 1.3 %copy-start = (bf16[512,1024]{1,0:T(8,128)(2,1)S(1)}, bf16[512,1024]{1,0:T(8,128)(2,1)}, u32[]{:S(2)}) copy-start(bf16[512,1024]{1,0:T(8,128)(2,1)} %refs_2_.8) | copy-start | bytes 3145732
  4.9 1.0 %copy-start.4 = (bf16[512,512]{1,0:T(8,128)(2,1)S(1)}, bf16[512,512]{1,0:T(8,128)(2,1)}, u32[]{:S(2)}) copy-start(bf16[512,512]{1,0:T(8,128)(2,1)} %refs_1_.9) | copy-start | bytes 1572868
  5.9 1.0 %copy-start.7 = (bf16[512,512]{1,0:T(8,128)(2,1)S(1)}, bf16[512,512]{1,0:T(8,128)(2,1)}, u32[]{:S(2)}) copy-start(bf16[512,512]{1,0:T(8,128)(2,1)} %refs_2_.9) | copy-start | bytes 1572868
  7.0 20.7 %copy-start.3 = (bf16[512,512]{1,0:T(8,128)(2,1)S(1)}, bf16[512,512]{1,0:T(8,128)(2,1)}, u32[]{:S(2)}) copy-start(bf16[512,512]{1,0:T(8,128)(2,1)} %refs_0_.8) | copy-start | bytes 1572868
  7.0 21.3 %copy-start.1 = (bf16[512,1024]{1,0:T(8,128)(2,1)S(1)}, bf16[512,1024]{1,0:T(8,128)(2,1)}, u32[]{:S(2)}) copy-start(bf16[512,1024]{1,0:T(8,128)(2,1)} %refs_2_.8) | copy-start | bytes 3145732
  7.5 6.5 %collective-permute-start = (bf16[512,128]{1,0:T(8,128)(2,1)S(1)}, bf16[512,128]{1,0:T(8,128)(2,1)S(1)}, u32[]{:S(2)}, u32[]{:S(2)}) collective-permute-start(bf16[512,128]{1,0:T(8,128)(2,1)S(1)} %get-tuple-element.36), channel_id=1, source_target_pairs={{0,4},{4,0},{8,12},{12,8},{16,20},{20,16},{24,28},{28,24},{1,5},{5... | collective-permute-start | bytes 393224 | tf_op jit(solution)/shard_map/ppermute | solution.py:187
  9.1 18.4 %collective-permute-start.4 = (bf16[512,512]{1,0:T(8,128)(2,1)S(1)}, bf16[512,512]{1,0:T(8,128)(2,1)}, u32[]{:S(2)}, u32[]{:S(2)}) collective-permute-start(bf16[512,512]{1,0:T(8,128)(2,1)S(1)} %get-tuple-element.40), channel_id=1, source_target_pairs={{0,4},{4,0},{8,12},{12,8},{16,20},{20,16},{24,28},{28,24},{1,5},{5... | collective-permute-start | bytes 1572872 | tf_op jit(solution)/shard_map/ppermute | solution.py:187
  14.1 5.0 %collective-permute-start.1 = (bf16[512,128]{1,0:T(8,128)(2,1)S(1)}, bf16[512,128]{1,0:T(8,128)(2,1)S(1)}, u32[]{:S(2)}, u32[]{:S(2)}) collective-permute-start(bf16[512,128]{1,0:T(8,128)(2,1)S(1)} %add_convert_fusion.8), channel_id=1, source_target_pairs={{0,8},{4,12},{8,0},{12,4},{16,24},{20,28},{24,16},{28,20},{1,9},{5... | collective-permute-start | bytes 393224 | tf_op jit(solution)/shard_map/ppermute | solution.py:187
  19.1 8.4 %collective-permute-start.2 = (bf16[512,128]{1,0:T(8,128)(2,1)S(1)}, bf16[512,128]{1,0:T(8,128)(2,1)}, u32[]{:S(2)}, u32[]{:S(2)}) collective-permute-start(bf16[512,128]{1,0:T(8,128)(2,1)S(1)} %add_convert_fusion.7), channel_id=1, source_target_pairs={{0,16},{4,20},{8,24},{12,28},{16,0},{20,4},{24,8},{28,12},{1,17},{... | collective-permute-start | bytes 393224 | tf_op jit(solution)/shard_map/ppermute | solution.py:187
  22.8 1.0 %copy-start.2 = (bf16[512,512]{1,0:T(8,128)(2,1)S(1)}, bf16[512,512]{1,0:T(8,128)(2,1)}, u32[]{:S(2)}) copy-start(bf16[512,512]{1,0:T(8,128)(2,1)} %refs_0_.8) | copy-start | bytes 1572868
  23.8 1.0 %copy-start.5 = (bf16[512,512]{1,0:T(8,128)(2,1)S(1)}, bf16[512,512]{1,0:T(8,128)(2,1)}, u32[]{:S(2)}) copy-start(bf16[512,512]{1,0:T(8,128)(2,1)} %refs_1_.9) | copy-start | bytes 1572868
  24.9 1.0 %copy-start.8 = (bf16[512,512]{1,0:T(8,128)(2,1)S(1)}, bf16[512,512]{1,0:T(8,128)(2,1)}, u32[]{:S(2)}) copy-start(bf16[512,512]{1,0:T(8,128)(2,1)} %refs_2_.9) | copy-start | bytes 1572868
  25.9 6.7 %copy-start.13 = (bf16[4096,512]{1,0:T(8,128)(2,1)S(1)}, bf16[4096,512]{1,0:T(8,128)(2,1)}, u32[]{:S(2)}) copy-start(bf16[4096,512]{1,0:T(8,128)(2,1)} %refs_0_.6) | copy-start | bytes 12582916
  27.6 8.2 %copy-start.10 = (bf16[512,1024]{1,0:T(8,128)(2,1)}, bf16[512,1024]{1,0:T(8,128)(2,1)S(1)}, u32[]{:S(2)}) copy-start(bf16[512,1024]{1,0:T(8,128)(2,1)S(1)} %collective-permute-done.3.refs_3_.refs_4_) | copy-start | bytes 3145732
  28.3 7.5 %copy-start.14 = (bf16[512,512]{1,0:T(8,128)(2,1)}, bf16[512,512]{1,0:T(8,128)(2,1)S(1)}, u32[]{:S(2)}) copy-start(bf16[512,512]{1,0:T(8,128)(2,1)S(1)} %shard_map.86.refs_0_) | copy-start | bytes 1572868
  28.3 3.2 %collective-permute-start.5 = (bf16[512,1024]{1,0:T(8,128)(2,1)S(1)}, bf16[512,1024]{1,0:T(8,128)(2,1)S(1)}, u32[]{:S(2)}, u32[]{:S(2)}) collective-permute-start(bf16[512,1024]{1,0:T(8,128)(2,1)S(1)} %copy-done.1), channel_id=1, source_target_pairs={{0,1},{1,0},{2,3},{3,2},{4,5},{5,4},{6,7},{7,6},{8,9},{9,8},{10,11... | collective-permute-start | bytes 3145736 | tf_op jit(solution)/shard_map/ppermute | solution.py:187
  28.4 4.1 %collective-permute-start.6 = (bf16[512,1024]{1,0:T(8,128)(2,1)S(1)}, bf16[512,1024]{1,0:T(8,128)(2,1)S(1)}, u32[]{:S(2)}, u32[]{:S(2)}) collective-permute-start(bf16[512,1024]{1,0:T(8,128)(2,1)S(1)} %collective-permute-done.3.refs_3_.refs_4_), channel_id=1, source_target_pairs={{0,1},{1,0},{2,3},{3,2},{4,5},{5,4},{6,7},{7,6},{8,9},{9,8},{10,11... | collective-permute-start | bytes 3145736 | tf_op jit(solution)/shard_map/ppermute | solution.py:187
  28.9 13.9 %collective-permute-start.8 = (bf16[512,512]{1,0:T(8,128)(2,1)S(1)}, bf16[512,512]{1,0:T(8,128)(2,1)S(1)}, u32[]{:S(2)}, u32[]{:S(2)}) collective-permute-start(bf16[512,512]{1,0:T(8,128)(2,1)S(1)} %shard_map.86.refs_0_), channel_id=1, source_target_pairs={{0,4},{4,0},{8,12},{12,8},{16,20},{20,16},{24,28},{28,24},{1,5},{5... | collective-permute-start | bytes 1572872 | tf_op jit(solution)/shard_map/ppermute | solution.py:187
  30.4 13.9 %collective-permute-start.9 = (bf16[512,512]{1,0:T(8,128)(2,1)}, bf16[512,512]{1,0:T(8,128)(2,1)}, u32[]{:S(2)}, u32[]{:S(2)}) collective-permute-start(bf16[512,512]{1,0:T(8,128)(2,1)} %collective-permute-done.4.refs_6_), channel_id=1, source_target_pairs={{0,2},{1,3},{2,0},{3,1},{4,6},{5,7},{6,4},{7,5},{8,10},{9,11},{10,... | collective-permute-start | bytes 1572872 | tf_op jit(solution)/shard_map/ppermute | solution.py:187
  31.6 4.2 %copy-start.11 = (bf16[512,1024]{1,0:T(8,128)(2,1)}, bf16[512,1024]{1,0:T(8,128)(2,1)S(1)}, u32[]{:S(2)}) copy-start(bf16[512,1024]{1,0:T(8,128)(2,1)S(1)} %collective-permute-done.5.refs_2_.refs_3_) | copy-start | bytes 3145732
  32.6 3.3 %copy-start.12 = (bf16[512,1024]{1,0:T(8,128)(2,1)}, bf16[512,1024]{1,0:T(8,128)(2,1)S(1)}, u32[]{:S(2)}) copy-start(bf16[512,1024]{1,0:T(8,128)(2,1)S(1)} %collective-permute-done.6.refs_4_.refs_5_) | copy-start | bytes 3145732
  36.3 8.1 %collective-permute-start.7 = (bf16[512,128]{1,0:T(8,128)(2,1)S(1)}, bf16[512,128]{1,0:T(8,128)(2,1)S(1)}, u32[]{:S(2)}, u32[]{:S(2)}) collective-permute-start(bf16[512,128]{1,0:T(8,128)(2,1)S(1)} %shard_map.88), channel_id=1, source_target_pairs={{0,8},{4,12},{8,0},{12,4},{16,24},{20,28},{24,16},{28,20},{1,9},{5... | collective-permute-start | bytes 393224 | tf_op jit(solution)/shard_map/ppermute | solution.py:187
  37.6 10.2 %collective-permute-start.11 = (bf16[512,512]{1,0:T(8,128)(2,1)}, bf16[512,512]{1,0:T(8,128)(2,1)S(1)}, u32[]{:S(2)}, u32[]{:S(2)}) collective-permute-start(bf16[512,512]{1,0:T(8,128)(2,1)} %collective-permute-done.4.refs_6_), channel_id=1, source_target_pairs={{0,1},{1,0},{2,3},{3,2},{4,5},{5,4},{6,7},{7,6},{8,9},{9,8},{10,11... | collective-permute-start | bytes 1572872 | tf_op jit(solution)/shard_map/ppermute | solution.py:187
  42.8 1.6 %copy-start.19 = (bf16[512,512]{1,0:T(8,128)(2,1)}, bf16[512,512]{1,0:T(8,128)(2,1)S(1)}, u32[]{:S(2)}) copy-start(bf16[512,512]{1,0:T(8,128)(2,1)S(1)} %collective-permute-done.8.refs_1_) | copy-start | bytes 1572868
  44.4 3.4 %collective-permute-start.12 = (bf16[512,512]{1,0:T(8,128)(2,1)}, bf16[512,512]{1,0:T(8,128)(2,1)S(1)}, u32[]{:S(2)}, u32[]{:S(2)}) collective-permute-start(bf16[512,512]{1,0:T(8,128)(2,1)} %collective-permute-done.9.refs_8_), channel_id=1, source_target_pairs={{0,1},{1,0},{2,3},{3,2},{4,5},{5,4},{6,7},{7,6},{8,9},{9,8},{10,11... | collective-permute-start | bytes 1572872 | tf_op jit(solution)/shard_map/ppermute | solution.py:187
  44.4 10.3 %collective-permute-start.10 = (bf16[512,128]{1,0:T(8,128)(2,1)S(1)}, bf16[512,128]{1,0:T(8,128)(2,1)S(1)}, u32[]{:S(2)}, u32[]{:S(2)}) collective-permute-start(bf16[512,128]{1,0:T(8,128)(2,1)S(1)} %add_convert_fusion.5), channel_id=1, source_target_pairs={{0,16},{4,20},{8,24},{12,28},{16,0},{20,4},{24,8},{28,12},{1,17},{... | collective-permute-start | bytes 393224 | tf_op jit(solution)/shard_map/ppermute | solution.py:187
  47.8 0.8 copy-start.20
  48.6 0.8 copy-start.21
  52.5 15.1 %collective-permute-start.14 = (bf16[512,512]{1,0:T(8,128)(2,1)}, bf16[512,512]{1,0:T(8,128)(2,1)}, u32[]{:S(2)}, u32[]{:S(2)}) collective-permute-start(bf16[512,512]{1,0:T(8,128)(2,1)} %shard_map.89), channel_id=1, source_target_pairs={{0,8},{4,12},{8,0},{12,4},{16,24},{20,28},{24,16},{28,20},{1,9},{5... | collective-permute-start | bytes 1572872 | tf_op jit(solution)/shard_map/ppermute | solution.py:218
  54.8 12.9 %copy-start.15 = (bf16[512,512]{1,0:T(8,128)(2,1)S(1)}, bf16[512,512]{1,0:T(8,128)(2,1)}, u32[]{:S(2)}) copy-start(bf16[512,512]{1,0:T(8,128)(2,1)} %shard_map.89) | copy-start | bytes 1572868
  54.8 14.8 %copy-start.6 = (bf16[512,512]{1,0:T(8,128)(2,1)S(1)}, bf16[512,512]{1,0:T(8,128)(2,1)}, u32[]{:S(2)}) copy-start(bf16[512,512]{1,0:T(8,128)(2,1)} %refs_1_.9) | copy-start | bytes 1572868
  54.9 14.8 %copy-start.9 = (bf16[512,512]{1,0:T(8,128)(2,1)S(1)}, bf16[512,512]{1,0:T(8,128)(2,1)}, u32[]{:S(2)}) copy-start(bf16[512,512]{1,0:T(8,128)(2,1)} %refs_2_.9) | copy-start | bytes 1572868
  54.9 6.3 %collective-permute-start.15 = (bf16[512,128]{1,0:T(8,128)(2,1)S(1)}, bf16[512,128]{1,0:T(8,128)(2,1)S(1)}, u32[]{:S(2)}, u32[]{:S(2)}) collective-permute-start(bf16[512,128]{1,0:T(8,128)(2,1)S(1)} %add_convert_fusion.4), channel_id=1, source_target_pairs={{0,4},{4,0},{8,12},{12,8},{16,20},{20,16},{24,28},{28,24},{1,5},{5... | collective-permute-start | bytes 393224 | tf_op jit(solution)/shard_map/ppermute | solution.py:187
  60.3 17.8 %copy-start.18 = (bf16[512,512]{1,0:T(8,128)(2,1)S(1)}, bf16[512,512]{1,0:T(8,128)(2,1)}, u32[]{:S(2)}) copy-start(bf16[512,512]{1,0:T(8,128)(2,1)} %get-tuple-element.54) | copy-start | bytes 1572868
  60.3 18.6 %copy-start.17 = (f32[512,512]{1,0:T(8,128)S(1)}, f32[512,512]{1,0:T(8,128)}, u32[]{:S(2)}) copy-start(f32[512,512]{1,0:T(8,128)} %get-tuple-element.65) | copy-start | bytes 3145732
  60.3 34.5 %copy-start.16 = (f32[512,512]{1,0:T(8,128)S(1)}, f32[512,512]{1,0:T(8,128)}, u32[]{:S(2)}) copy-start(f32[512,512]{1,0:T(8,128)} %get-tuple-element.64) | copy-start | bytes 3145732
  60.4 17.7 %collective-permute-start.13 = (bf16[512,512]{1,0:T(8,128)(2,1)}, bf16[512,512]{1,0:T(8,128)(2,1)S(1)}, u32[]{:S(2)}, u32[]{:S(2)}) collective-permute-start(bf16[512,512]{1,0:T(8,128)(2,1)} %get-tuple-element.54), channel_id=1, source_target_pairs={{0,8},{4,12},{8,0},{12,4},{16,24},{20,28},{24,16},{28,20},{1,9},{5... | collective-permute-start | bytes 1572872 | tf_op jit(solution)/shard_map/ppermute | solution.py:218
  68.9 10.1 %collective-permute-start.16 = (bf16[512,512]{1,0:T(8,128)(2,1)S(1)}, bf16[512,512]{1,0:T(8,128)(2,1)S(1)}, u32[]{:S(2)}, u32[]{:S(2)}) collective-permute-start(bf16[512,512]{1,0:T(8,128)(2,1)S(1)} %add_convert_fusion.2), channel_id=1, source_target_pairs={{8,16},{12,20},{16,8},{20,12},{9,17},{13,21},{17,9},{21,13},{10,18... | collective-permute-start | bytes 1572872 | tf_op jit(solution)/shard_map/ppermute | solution.py:218
  78.2 7.9 %collective-permute-start.18 = (bf16[512,512]{1,0:T(8,128)(2,1)S(1)}, bf16[512,512]{1,0:T(8,128)(2,1)S(1)}, u32[]{:S(2)}, u32[]{:S(2)}) collective-permute-start(bf16[512,512]{1,0:T(8,128)(2,1)S(1)} %add_convert_fusion), channel_id=1, source_target_pairs={{8,16},{12,20},{16,8},{20,12},{9,17},{13,21},{17,9},{21,13},{10,18... | collective-permute-start | bytes 1572872 | tf_op jit(solution)/shard_map/ppermute | solution.py:218
  79.1 15.7 %collective-permute-start.17 = (bf16[512,512]{1,0:T(8,128)(2,1)S(1)}, bf16[512,512]{1,0:T(8,128)(2,1)S(1)}, u32[]{:S(2)}, u32[]{:S(2)}) collective-permute-start(bf16[512,512]{1,0:T(8,128)(2,1)S(1)} %add_convert_fusion.1), channel_id=1, source_target_pairs={{0,8},{4,12},{8,0},{12,4},{16,24},{20,28},{24,16},{28,20},{1,9},{5... | collective-permute-start | bytes 1572872 | tf_op jit(solution)/shard_map/ppermute | solution.py:218

commit v3 on v2

--- a/solution.py
+++ b/solution.py
@@ -146,7 +146,7 @@
     return at
 
 
-def product_body(factor, count, short, slots, sources, results, buffers, sems):
+def product_body(factor, count, short, slots, parts, sources, results, buffers, sems):
     used = len(slots)
     seq, me = lax.axis_index("seq"), lax.axis_index("head")
     o, n = (pltpu.make_async_copy(sources[i], buffers[i], sems.at[i]) for i in range(2))
@@ -171,12 +171,18 @@
             copies.append(pltpu.make_async_copy(buffers[at], buffers[at], sems.at[at]))
     o.wait()
     n.wait()
-    for i, out in enumerate(results):
+    results = list(results)
+    for i in range(used):
         copies[2 * i].wait()
         copies[2 * i + 1].wait()
         total = dot(buffers[2 + i][...], buffers[0][...], 0, 0)
         total += dot(buffers[2 + used + i][...], buffers[1][...], 0, 0)
-        out[...] = (factor * total).astype(out.dtype)
+        total *= factor
+        first = 0
+        for _ in range(parts[i]):
+            part = results.pop(0)
+            part[...] = total[:, first : first + part.shape[1]].astype(part.dtype)
+            first += part.shape[1]
 
 
 def phase(*values):
@@ -187,8 +193,21 @@
     return lax.ppermute(a, axis, [(i, i ^ bit) for i in range(lax.axis_size(axis))])
 
 
-def add(a, b):
-    return (a.astype(F32) + b.astype(F32)).astype(BF16)
+def add_body(*refs):
+    *sources, out = refs
+    out[...] = sum(ref[...].astype(F32) for ref in sources).astype(out.dtype)
+
+
+def add(*terms, kind=BF16):
+    spec = pl.BlockSpec(memory_space=pltpu.VMEM)
+    return pl.pallas_call(
+        add_body,
+        out_shape=jax.ShapeDtypeStruct(terms[0].shape, kind),
+        in_specs=[spec] * len(terms),
+        out_specs=spec,
+        compiler_params=pltpu.CompilerParams(vmem_limit_bytes=8 << 20),
+        cost_estimate=pl.CostEstimate(flops=1 << 20, bytes_accessed=1 << 14, transcendentals=0),
+    )(*terms)
 
 
 class Scan:
@@ -250,8 +269,8 @@
     matrix = shaped((rows, width))
 
     def product(slots, kinds, *operands, cost=1):
-        body = functools.partial(product_body, factor, n_head, short, slots)
-        outs = [shaped((cols // 2, width), kind) for kind in kinds]
+        body = functools.partial(product_body, factor, n_head, short, slots, [len(k) for k in kinds])
+        outs = [shaped((cols // 2, width // len(k)), kind) for k in kinds for kind in k]
         like = [((rows, cols // 2), BF16)] * (2 * len(slots))
         scratch = [((rows, width), BF16)] * 2 + like
         return call(body, outs, *operands, scratch=scratch, cost=cost, vmem=60)
@@ -260,13 +279,13 @@
     if short:
         scratch = [((rows, width), BF16)] * 2
         outs = [state_shape, shaped((rows, cols // 2))]
-        kv_term, other = call(state, outs, keys, values, out_grad, scratch=scratch)
+        kv_term, other = call(state, outs, keys, values, out_grad, scratch=scratch, vmem=60)
     else:
         (kv_term,), other = call(state, [state_shape], keys, values), half(out_grad, 1 - y)
     prior = Scan(kv_term, False)
     got = prior.start(1)
+    got, other, q, grad = phase(got, other, queries, out_grad)
     near = flip(other, "seq", 1)
-    got, q, grad = phase(got, queries, out_grad)
     prior.take(1, got)
     for bit in prior.bits[1:]:
         got = prior.start(bit)
@@ -299,26 +318,25 @@
 
     if short:
         got = later.start(4)
-        (b0,) = product((0,), (BF16,), *operands)
-        e1 = send(b0, OUTER)
-        o, got, _ = phase(o, got, b0)
-        b1, b2, b3 = product((1, 2, 3), (BF16, F32, F32), o, *operands[1:], cost=1 << 14)
+        *b0, b1 = product((0, 1), ((BF16,) * 2, (BF16,)), *operands)
+        e1, e2 = [send(b, OUTER) for b in b0], send(b1, OUTER)
+        o, got, *b0 = phase(o, got, *b0)
+        b2, b3 = product((2, 3), ((F32,), (F32,)), o, *operands[1:], cost=1 << 14)
         later.take(4, got)
         got = later.across()
-        e2 = send(b1, OUTER)
-        e1, got, b2 = phase(e1, got, b2)
-        m2 = send(add(b0, e1), MIDDLE)
+        e1[0], got, b2 = phase(e1[0], got, b2)
+        m2 = [send(add(b, e), MIDDLE) for b, e in zip(b0, e1)]
+        e2, got, *m2 = phase(e2, got, *m2)
         grads = gradients(later.result(got))
-        e2, *grads = phase(e2, *grads)
         m3 = send(add(b1, e2), MIDDLE)
-        e3 = send(add(b2, m2), OUTER)
-        weight_grad = b3 + e3.astype(F32) + m3.astype(F32)
+        e3 = send(add(b2, jnp.concatenate(m2, axis=1)), OUTER)
+        weight_grad = add(b3, e3, m3, kind=F32)
     else:
         for bit in later.bits[1:]:
             later.take(bit, later.start(bit))
         grads = gradients(later.result(later.across()))
         groups = [[2 * p + i for p in range(line)] for i in range(2)]
-        whole = jnp.concatenate(product(range(n_head), [F32] * n_head, *operands), axis=0)
+        whole = jnp.concatenate(product(range(n_head), [(F32,)] * n_head, *operands), axis=0)
         weight_grad = lax.psum_scatter(
             whole, "seq", scatter_dimension=0, axis_index_groups=groups, tiled=True
         )

time: 96.6 us -> 93.5 us (0.968)
  Pallas kernels: 19.6 us -> 23 us
  other arithmetic: 3.02 us -> 0.27 us
  local copies, waits for them, and re-layouts: 8.09 us -> 5.7 us
  starting transfers between devices: 29.6 us -> 27.3 us
    ppermute x5 -> x7, starting transfers between devices: 10.8 us -> 7.73 us  [send(): lax.ppermute(a, 'seq', [(2 * s + i, 2 * t + i) for s, t in pairs for i in...]
    unnamed x44 -> x46, local copies, waits for them, and re-layouts: 8.09 us -> 5.7 us
    ppermute x5 -> x7, waiting for transfers between devices: 18.7 us -> 20.7 us  [send(): lax.ppermute(a, 'seq', [(2 * s + i, 2 * t + i) for s, t in pairs for i in...]
    pallas_call x8, Pallas kernels: 19.6 us -> 21.4 us  [call(): pl.pallas_call(kernel, out_shape=outs, in_specs=[pl.BlockSpec(memory_spac...]
    convert_element_type x6 -> x0, other arithmetic: 1.58 us -> none  [add(): return (a.astype(F32) + b.astype(F32)).astype(BF16)]
    pallas_call x0 -> x8, Pallas kernels: none -> 1.55 us  [add(): pl.pallas_call(add_body, out_shape=jax.ShapeDtypeStruct(terms[0].shape, k...]
    ppermute x14, waiting for transfers between devices: 16.1 us -> 14.6 us  [flip(): lax.ppermute(a, axis, [(i, i ^ bit) for i in range(lax.axis_size(axis))])]
    add x1 -> x0, other arithmetic: 1.18 us -> none  [per_device(): weight_grad = b3 + e3.astype(F32) + m3.astype(F32)]
  transfers between devices with their start and end apart: 19 -> 21, of which waited for: 9 -> 10; matrix products, arithmetic and copies ran while one was open for 2% -> 0% of each run, Pallas kernels for 20% -> 23%
where the time goes in v3:
time: 93.5 us; the launch traced here: 92.6 us
  waiting for transfers between devices  35.3 us (38%)
  starting transfers between devices  27.3 us (29%)
  Pallas kernels  23 us (25%)
  local copies, waits for them, and re-layouts  5.7 us (6%)
  between operations  1 us (1%)
    pallas_call x8, Pallas kernels, call(): pl.pallas_call(kernel, out_shape=outs, in_specs=[pl.BlockSpec(memory_spac...  21.4 us
    ppermute x7, waiting for transfers between devices, send(): lax.ppermute(a, 'seq', [(2 * s + i, 2 * t + i) for s, t in pairs for i in...  20.7 us
    ppermute x14, starting transfers between devices, flip(): lax.ppermute(a, axis, [(i, i ^ bit) for i in range(lax.axis_size(axis))])  19.6 us
    ppermute x14, waiting for transfers between devices, flip(): lax.ppermute(a, axis, [(i, i ^ bit) for i in range(lax.axis_size(axis))])  14.6 us
    ppermute x7, starting transfers between devices, send(): lax.ppermute(a, 'seq', [(2 * s + i, 2 * t + i) for s, t in pairs for i in...  7.73 us
    unnamed x46, local copies, waits for them, and re-layouts  5.7 us
  transfers between devices with their start and end apart: 21, of which 10 were waited for; matrix products, arithmetic and copies ran while one was open for 0% of the time, Pallas kernels for 23%

profile of v3, /device:TPU:0, one launch (start us, length us, event | category | flops | bytes accessed | tf_op | source)
XLA Modules:
  0.0 92.6 jit_solution(15590294335661623686)
XLA Ops:
  0.7 3.0 %collective-permute-start.3 = (bf16[512,1024]{1,0:T(8,128)(2,1)}, bf16[512,1024]{1,0:T(8,128)(2,1)S(1)}, u32[]{:S(2)}, u32[]{:S(2)}) collective-permute-start(bf16[512,1024]{1,0:T(8,128)(2,1)} %refs_2_.8), channel_id=1, source_target_pairs={{0,2},{1,3},{2,0},{3,1},{4,6},{5,7},{6,4},{7,5},{8,10},{9,11},{10,... | collective-permute-start | bytes 3145736 | tf_op jit(solution)/shard_map/ppermute | solution.py:193
  3.7 2.4 %shard_map.84 = (bf16[512,128]{1,0:T(8,128)(2,1)}, bf16[512,512]{1,0:T(8,128)(2,1)}) custom-call(bf16[512,512]{1,0:T(8,128)(2,1)} %refs_1_.9, bf16[512,512]{1,0:T(8,128)(2,1)} %refs_2_.9, bf16[512,1024]{1,0:T(8,128)(2,1)} %refs_2_.8), custom_call_target="tpu_custom_call" | custom-call | flops 1048576 | bytes 16384 | tf_op jit(solution)/shard_map/pallas_call | solution.py:29
  6.1 1.6 %collective-permute-start = (bf16[512,128]{1,0:T(8,128)(2,1)}, bf16[512,128]{1,0:T(8,128)(2,1)S(1)}, u32[]{:S(2)}, u32[]{:S(2)}) collective-permute-start(bf16[512,128]{1,0:T(8,128)(2,1)} %get-tuple-element.41.refs_0_), channel_id=1, source_target_pairs={{0,4},{4,0},{8,12},{12,8},{16,20},{20,16},{24,28},{28,24},{1,5},{5... | collective-permute-start | bytes 393224 | tf_op jit(solution)/shard_map/ppermute | solution.py:193
  7.7 3.7 %collective-permute-done.refs_1_ = bf16[512,128]{1,0:T(8,128)(2,1)S(1)} collective-permute-done((bf16[512,128]{1,0:T(8,128)(2,1)}, bf16[512,128]{1,0:T(8,128)(2,1)S(1)}, u32[]{:S(2)}, u32[]{:S(2)}) %collective-permute-start) | collective-permute-done | bytes 131104 | tf_op jit(solution)/shard_map/ppermute | solution.py:193
  11.3 1.5 %collective-permute-start.4 = (bf16[512,512]{1,0:T(8,128)(2,1)}, bf16[512,512]{1,0:T(8,128)(2,1)}, u32[]{:S(2)}, u32[]{:S(2)}) collective-permute-start(bf16[512,512]{1,0:T(8,128)(2,1)} %get-tuple-element.46), channel_id=1, source_target_pairs={{0,4},{4,0},{8,12},{12,8},{16,20},{20,16},{24,28},{28,24},{1,5},{5... | collective-permute-start | bytes 1572872 | tf_op jit(solution)/shard_map/ppermute | solution.py:193
  12.9 0.9 copy-done.17
  13.8 1.6 %collective-permute-start.1 = (bf16[512,128]{1,0:T(8,128)(2,1)S(1)}, bf16[512,128]{1,0:T(8,128)(2,1)S(1)}, u32[]{:S(2)}, u32[]{:S(2)}) collective-permute-start(bf16[512,128]{1,0:T(8,128)(2,1)S(1)} %shard_map.85.refs_0_), channel_id=1, source_target_pairs={{0,8},{4,12},{8,0},{12,4},{16,24},{20,28},{24,16},{28,20},{1,9},{5... | collective-permute-start | bytes 393224 | tf_op jit(solution)/shard_map/ppermute | solution.py:193
  15.4 3.4 %collective-permute-done.1.refs_1_ = bf16[512,128]{1,0:T(8,128)(2,1)S(1)} collective-permute-done((bf16[512,128]{1,0:T(8,128)(2,1)S(1)}, bf16[512,128]{1,0:T(8,128)(2,1)S(1)}, u32[]{:S(2)}, u32[]{:S(2)}) %collective-permute-start.1) | collective-permute-done | bytes 131104 | tf_op jit(solution)/shard_map/ppermute | solution.py:193
  18.9 2.7 %collective-permute-start.2 = (bf16[512,128]{1,0:T(8,128)(2,1)S(1)}, bf16[512,128]{1,0:T(8,128)(2,1)S(1)}, u32[]{:S(2)}, u32[]{:S(2)}) collective-permute-start(bf16[512,128]{1,0:T(8,128)(2,1)S(1)} %shard_map.86), channel_id=1, source_target_pairs={{0,16},{4,20},{8,24},{12,28},{16,0},{20,4},{24,8},{28,12},{1,17},{... | collective-permute-start | bytes 393224 | tf_op jit(solution)/shard_map/ppermute | solution.py:193
  21.5 1.0 %copy-done.1 = bf16[512,512]{1,0:T(8,128)(2,1)S(1)} copy-done((bf16[512,512]{1,0:T(8,128)(2,1)S(1)}, bf16[512,512]{1,0:T(8,128)(2,1)}, u32[]{:S(2)}) %copy-start.1) | copy-done | bytes 524312
  22.6 1.0 %copy-done.3 = bf16[512,512]{1,0:T(8,128)(2,1)S(1)} copy-done((bf16[512,512]{1,0:T(8,128)(2,1)S(1)}, bf16[512,512]{1,0:T(8,128)(2,1)}, u32[]{:S(2)}) %copy-start.3) | copy-done | bytes 524312
  23.6 1.0 %copy-done.5 = bf16[512,512]{1,0:T(8,128)(2,1)S(1)} copy-done((bf16[512,512]{1,0:T(8,128)(2,1)S(1)}, bf16[512,512]{1,0:T(8,128)(2,1)}, u32[]{:S(2)}) %copy-start.5) | copy-done | bytes 524312
  24.7 1.6 %shard_map.87.refs_2_ = f32[512,512]{1,0:T(8,128)S(1)} custom-call(bf16[512,512]{1,0:T(8,128)(2,1)S(1)} %copy-done.1, bf16[512,512]{1,0:T(8,128)(2,1)S(1)} %copy-done.3, bf16[512,512]{1,0:T(8,128)(2,1)S(1)} %copy-done.5), custom_call_target="tpu_custom_call" | custom-call | flops 1048576 | bytes 16384 | tf_op jit(solution)/shard_map/pallas_call | solution.py:29
  26.3 0.7 collective-permute-done.3.refs_3_.refs_4_
  27.0 0.1 add_convert_fusion.2.refs_0_.refs_4_
  27.1 0.6 shard_map.88.refs_0_
  27.9 0.5 collective-permute-start.6
  28.4 1.8 %collective-permute-start.8 = (bf16[512,512]{1,0:T(8,128)(2,1)S(1)}, bf16[512,512]{1,0:T(8,128)(2,1)S(1)}, u32[]{:S(2)}, u32[]{:S(2)}) collective-permute-start(bf16[512,512]{1,0:T(8,128)(2,1)S(1)} %shard_map.88.refs_0_), channel_id=1, source_target_pairs={{0,4},{4,0},{8,12},{12,8},{16,20},{20,16},{24,28},{28,24},{1,5},{5... | collective-permute-start | bytes 1572872 | tf_op jit(solution)/shard_map/ppermute | solution.py:193
  30.1 1.5 %collective-permute-start.9 = (bf16[512,512]{1,0:T(8,128)(2,1)}, bf16[512,512]{1,0:T(8,128)(2,1)}, u32[]{:S(2)}, u32[]{:S(2)}) collective-permute-start(bf16[512,512]{1,0:T(8,128)(2,1)} %collective-permute-done.4.refs_6_), channel_id=1, source_target_pairs={{0,2},{1,3},{2,0},{3,1},{4,6},{5,7},{6,4},{7,5},{8,10},{9,11},{10,... | collective-permute-start | bytes 1572872 | tf_op jit(solution)/shard_map/ppermute | solution.py:193
  31.6 0.4 collective-permute-done.6.refs_4_.refs_5_
  32.0 3.2 %shard_map.89.refs_1_.refs_3_ = bf16[512,512]{1,0:T(8,128)(2,1)S(1)} custom-call(bf16[4096,512]{1,0:T(8,128)(2,1)S(1)} %copy-done.10, bf16[512,1024]{1,0:T(8,128)(2,1)S(1)} %copy-done, bf16[512,1024]{1,0:T(8,128)(2,1)S(1)} %collective-permute-done.5.refs_2_.refs_3_, bf16[512,1024]{1,0:T(8,128)(2,1)S(1)} %collective-permute-done.3.refs_3_.refs_4_, ...), custom_call_target="tpu_custom_call" | custom-call | flops 1048576 | bytes 16384 | tf_op jit(solution)/shard_map/pallas_call | solution.py:29
  35.3 0.5 shard_map.90.refs_0_
  35.7 1.9 %collective-permute-start.7 = (bf16[512,128]{1,0:T(8,128)(2,1)S(1)}, bf16[512,128]{1,0:T(8,128)(2,1)S(1)}, u32[]{:S(2)}, u32[]{:S(2)}) collective-permute-start(bf16[512,128]{1,0:T(8,128)(2,1)S(1)} %shard_map.90.refs_0_), channel_id=1, source_target_pairs={{0,8},{4,12},{8,0},{12,4},{16,24},{20,28},{24,16},{28,20},{1,9},{5... | collective-permute-start | bytes 393224 | tf_op jit(solution)/shard_map/ppermute | solution.py:193
  37.6 4.6 %collective-permute-done.8.refs_1_ = bf16[512,512]{1,0:T(8,128)(2,1)S(1)} collective-permute-done((bf16[512,512]{1,0:T(8,128)(2,1)S(1)}, bf16[512,512]{1,0:T(8,128)(2,1)S(1)}, u32[]{:S(2)}, u32[]{:S(2)}) %collective-permute-start.8) | collective-permute-done | bytes 524320 | tf_op jit(solution)/shard_map/ppermute | solution.py:193
  42.3 1.8 %collective-permute-done.9.refs_8_ = bf16[512,512]{1,0:T(8,128)(2,1)} collective-permute-done((bf16[512,512]{1,0:T(8,128)(2,1)}, bf16[512,512]{1,0:T(8,128)(2,1)}, u32[]{:S(2)}, u32[]{:S(2)}) %collective-permute-start.9) | collective-permute-done | bytes 524320 | tf_op jit(solution)/shard_map/ppermute | solution.py:193
  44.1 2.7 %collective-permute-start.10 = (bf16[512,128]{1,0:T(8,128)(2,1)S(1)}, bf16[512,128]{1,0:T(8,128)(2,1)S(1)}, u32[]{:S(2)}, u32[]{:S(2)}) collective-permute-start(bf16[512,128]{1,0:T(8,128)(2,1)S(1)} %shard_map.91), channel_id=1, source_target_pairs={{0,16},{4,20},{8,24},{12,28},{16,0},{20,4},{24,8},{28,12},{1,17},{... | collective-permute-start | bytes 393224 | tf_op jit(solution)/shard_map/ppermute | solution.py:193
  46.8 0.8 copy-done.19
  47.6 0.8 copy-done.20
  48.4 3.9 %shard_map.92 = (bf16[512,256]{1,0:T(8,128)(2,1)}, bf16[512,256]{1,0:T(8,128)(2,1)}, bf16[512,512]{1,0:T(8,128)(2,1)}) custom-call(bf16[512,512]{1,0:T(8,128)(2,1)} %copy-done.11, bf16[512,512]{1,0:T(8,128)(2,1)} %copy-done.18, bf16[512,1024]{1,0:T(8,128)(2,1)} %refs_2_.8, bf16[512,1024]{1,0:T(8,128)(2,1)} %copy-done.8, bf16[512,1024]{1,0:T(8,128)(2,1)} %copy-done.7, ...), custom_call_target="tpu_custom_call" | custom-call | flops 1048576 | bytes 16384 | tf_op jit(solution)/shard_map/pallas_call | solution.py:29
  52.3 1.7 %collective-permute-start.14 = (bf16[512,256]{1,0:T(8,128)(2,1)}, bf16[512,256]{1,0:T(8,128)(2,1)S(1)}, u32[]{:S(2)}, u32[]{:S(2)}) collective-permute-start(bf16[512,256]{1,0:T(8,128)(2,1)} %get-tuple-element.66.refs_0_), channel_id=1, source_target_pairs={{0,8},{4,12},{8,0},{12,4},{16,24},{20,28},{24,16},{28,20},{1,9},{5... | collective-permute-start | bytes 786440 | tf_op jit(solution)/shard_map/ppermute | solution.py:237
  54.0 0.4 collective-permute-start.17
  54.4 0.1 add_convert_fusion.1
  54.5 0.8 collective-permute-start.15
  55.3 1.6 %collective-permute-start.13 = (bf16[512,512]{1,0:T(8,128)(2,1)}, bf16[512,512]{1,0:T(8,128)(2,1)S(1)}, u32[]{:S(2)}, u32[]{:S(2)}) collective-permute-start(bf16[512,512]{1,0:T(8,128)(2,1)} %get-tuple-element.62.refs_0_), channel_id=1, source_target_pairs={{0,8},{4,12},{8,0},{12,4},{16,24},{20,28},{24,16},{28,20},{1,9},{5... | collective-permute-start | bytes 1572872 | tf_op jit(solution)/shard_map/ppermute | solution.py:237
  57.0 4.1 %shard_map.93 = (f32[512,512]{1,0:T(8,128)}, f32[512,512]{1,0:T(8,128)}) custom-call(bf16[512,512]{1,0:T(8,128)(2,1)} %copy-done.11, bf16[512,512]{1,0:T(8,128)(2,1)} %copy-done.18, bf16[512,1024]{1,0:T(8,128)(2,1)} %refs_2_.8, bf16[512,1024]{1,0:T(8,128)(2,1)} %copy-done.8, bf16[512,1024]{1,0:T(8,128)(2,1)} %copy-done.7, bf16[512,1024]{1,0:T(8,128)(2,1)} %copy-done.9, ...), custom_call_target="tpu_custom_call" | custom-call | flops 17179869184 | bytes 16384 | tf_op jit(solution)/shard_map/pallas_call | solution.py:29
  61.1 0.6 collective-permute-done.14.refs_1_
  61.8 0.8 collective-permute-start.16
  62.6 4.7 %collective-permute-done.17.refs_1_ = bf16[512,256]{1,0:T(8,128)(2,1)S(1)} collective-permute-done((bf16[512,256]{1,0:T(8,128)(2,1)}, bf16[512,256]{1,0:T(8,128)(2,1)S(1)}, u32[]{:S(2)}, u32[]{:S(2)}) %collective-permute-start.17) | collective-permute-done | bytes 262176 | tf_op jit(solution)/shard_map/ppermute | solution.py:237
  67.4 0.7 collective-permute-start.18
  68.1 9.7 %collective-permute-done.13.refs_1_ = bf16[512,512]{1,0:T(8,128)(2,1)S(1)} collective-permute-done((bf16[512,512]{1,0:T(8,128)(2,1)}, bf16[512,512]{1,0:T(8,128)(2,1)S(1)}, u32[]{:S(2)}, u32[]{:S(2)}) %collective-permute-start.13) | collective-permute-done | bytes 524320 | tf_op jit(solution)/shard_map/ppermute | solution.py:237
  77.9 0.1 shard_map.98
  78.1 0.1 shard_map.97
  78.2 1.6 %collective-permute-start.19 = (bf16[512,512]{1,0:T(8,128)(2,1)S(1)}, bf16[512,512]{1,0:T(8,128)(2,1)S(1)}, u32[]{:S(2)}, u32[]{:S(2)}) collective-permute-start(bf16[512,512]{1,0:T(8,128)(2,1)S(1)} %shard_map.97), channel_id=1, source_target_pairs={{0,8},{4,12},{8,0},{12,4},{16,24},{20,28},{24,16},{28,20},{1,9},{5... | collective-permute-start | bytes 1572872 | tf_op jit(solution)/shard_map/ppermute | solution.py:237
  79.8 0.9 collective-permute-start.20
  80.7 0.1 add_convert_fusion.refs_5_
  80.8 5.0 %shard_map.96 = (bf16[512,512]{1,0:T(8,128)(2,1)}, bf16[512,512]{1,0:T(8,128)(2,1)}, bf16[512,512]{1,0:T(8,128)(2,1)}) custom-call(bf16[512,512]{1,0:T(8,128)(2,1)S(1)} %copy-done.2, bf16[512,512]{1,0:T(8,128)(2,1)S(1)} %copy-done.4, bf16[512,512]{1,0:T(8,128)(2,1)S(1)} %copy-done.6, bf16[512,512]{1,0:T(8,128)(2,1)S(1)} %shard_map.89.refs_1_.refs_3_, ...), custom_call_target="tpu_custom_call" | custom-call | flops 1048576 | bytes 16384 | tf_op jit(solution)/shard_map/pallas_call | solution.py:29
  85.8 5.6 %collective-permute-done.19.refs_1_ = bf16[512,512]{1,0:T(8,128)(2,1)S(1)} collective-permute-done((bf16[512,512]{1,0:T(8,128)(2,1)S(1)}, bf16[512,512]{1,0:T(8,128)(2,1)S(1)}, u32[]{:S(2)}, u32[]{:S(2)}) %collective-permute-start.19) | collective-permute-done | bytes 524320 | tf_op jit(solution)/shard_map/ppermute | solution.py:237
  91.5 1.1 %shard_map.99 = f32[512,512]{1,0:T(8,128)} custom-call(f32[512,512]{1,0:T(8,128)S(1)} %copy-done.12, bf16[512,512]{1,0:T(8,128)(2,1)S(1)} %collective-permute-done.19.refs_1_, bf16[512,512]{1,0:T(8,128)(2,1)S(1)} %collective-permute-done.20.refs_2_), custom_call_target="tpu_custom_call" | custom-call | flops 1048576 | bytes 16384 | tf_op jit(solution)/shard_map/pallas_call | solution.py:203
  (60 shorter events, 0.5 us)
Async XLA Ops:
  0.6 27.1 %copy-start = (bf16[512,1024]{1,0:T(8,128)(2,1)S(1)}, bf16[512,1024]{1,0:T(8,128)(2,1)}, u32[]{:S(2)}) copy-start(bf16[512,1024]{1,0:T(8,128)(2,1)} %refs_2_.8) | copy-start | bytes 3145732
  0.6 26.5 %copy-start.2 = (bf16[512,512]{1,0:T(8,128)(2,1)S(1)}, bf16[512,512]{1,0:T(8,128)(2,1)}, u32[]{:S(2)}) copy-start(bf16[512,512]{1,0:T(8,128)(2,1)} %refs_0_.8) | copy-start | bytes 1572868
  0.7 26.4 %collective-permute-start.3 = (bf16[512,1024]{1,0:T(8,128)(2,1)}, bf16[512,1024]{1,0:T(8,128)(2,1)S(1)}, u32[]{:S(2)}, u32[]{:S(2)}) collective-permute-start(bf16[512,1024]{1,0:T(8,128)(2,1)} %refs_2_.8), channel_id=1, source_target_pairs={{0,2},{1,3},{2,0},{3,1},{4,6},{5,7},{6,4},{7,5},{8,10},{9,11},{10,... | collective-permute-start | bytes 3145736 | tf_op jit(solution)/shard_map/ppermute | solution.py:193
  6.1 5.2 %collective-permute-start = (bf16[512,128]{1,0:T(8,128)(2,1)}, bf16[512,128]{1,0:T(8,128)(2,1)S(1)}, u32[]{:S(2)}, u32[]{:S(2)}) collective-permute-start(bf16[512,128]{1,0:T(8,128)(2,1)} %get-tuple-element.41.refs_0_), channel_id=1, source_target_pairs={{0,4},{4,0},{8,12},{12,8},{16,20},{20,16},{24,28},{28,24},{1,5},{5... | collective-permute-start | bytes 393224 | tf_op jit(solution)/shard_map/ppermute | solution.py:193
  11.3 15.0 %collective-permute-start.4 = (bf16[512,512]{1,0:T(8,128)(2,1)}, bf16[512,512]{1,0:T(8,128)(2,1)}, u32[]{:S(2)}, u32[]{:S(2)}) collective-permute-start(bf16[512,512]{1,0:T(8,128)(2,1)} %get-tuple-element.46), channel_id=1, source_target_pairs={{0,4},{4,0},{8,12},{12,8},{16,20},{20,16},{24,28},{28,24},{1,5},{5... | collective-permute-start | bytes 1572872 | tf_op jit(solution)/shard_map/ppermute | solution.py:193
  12.9 0.9 copy-start.17
  13.8 5.0 %collective-permute-start.1 = (bf16[512,128]{1,0:T(8,128)(2,1)S(1)}, bf16[512,128]{1,0:T(8,128)(2,1)S(1)}, u32[]{:S(2)}, u32[]{:S(2)}) collective-permute-start(bf16[512,128]{1,0:T(8,128)(2,1)S(1)} %shard_map.85.refs_0_), channel_id=1, source_target_pairs={{0,8},{4,12},{8,0},{12,4},{16,24},{20,28},{24,16},{28,20},{1,9},{5... | collective-permute-start | bytes 393224 | tf_op jit(solution)/shard_map/ppermute | solution.py:193
  18.9 7.4 %collective-permute-start.2 = (bf16[512,128]{1,0:T(8,128)(2,1)S(1)}, bf16[512,128]{1,0:T(8,128)(2,1)S(1)}, u32[]{:S(2)}, u32[]{:S(2)}) collective-permute-start(bf16[512,128]{1,0:T(8,128)(2,1)S(1)} %shard_map.86), channel_id=1, source_target_pairs={{0,16},{4,20},{8,24},{12,28},{16,0},{20,4},{24,8},{28,12},{1,17},{... | collective-permute-start | bytes 393224 | tf_op jit(solution)/shard_map/ppermute | solution.py:193
  21.5 1.0 %copy-start.1 = (bf16[512,512]{1,0:T(8,128)(2,1)S(1)}, bf16[512,512]{1,0:T(8,128)(2,1)}, u32[]{:S(2)}) copy-start(bf16[512,512]{1,0:T(8,128)(2,1)} %refs_0_.8) | copy-start | bytes 1572868
  22.6 1.0 %copy-start.3 = (bf16[512,512]{1,0:T(8,128)(2,1)S(1)}, bf16[512,512]{1,0:T(8,128)(2,1)}, u32[]{:S(2)}) copy-start(bf16[512,512]{1,0:T(8,128)(2,1)} %refs_1_.9) | copy-start | bytes 1572868
  23.6 1.0 %copy-start.5 = (bf16[512,512]{1,0:T(8,128)(2,1)S(1)}, bf16[512,512]{1,0:T(8,128)(2,1)}, u32[]{:S(2)}) copy-start(bf16[512,512]{1,0:T(8,128)(2,1)} %refs_2_.9) | copy-start | bytes 1572868
  24.7 7.4 %copy-start.10 = (bf16[4096,512]{1,0:T(8,128)(2,1)S(1)}, bf16[4096,512]{1,0:T(8,128)(2,1)}, u32[]{:S(2)}) copy-start(bf16[4096,512]{1,0:T(8,128)(2,1)} %refs_0_.6) | copy-start | bytes 12582916
  27.0 8.2 %copy-start.7 = (bf16[512,1024]{1,0:T(8,128)(2,1)}, bf16[512,1024]{1,0:T(8,128)(2,1)S(1)}, u32[]{:S(2)}) copy-start(bf16[512,1024]{1,0:T(8,128)(2,1)S(1)} %collective-permute-done.3.refs_3_.refs_4_) | copy-start | bytes 3145732
  27.8 7.5 %copy-start.11 = (bf16[512,512]{1,0:T(8,128)(2,1)}, bf16[512,512]{1,0:T(8,128)(2,1)S(1)}, u32[]{:S(2)}) copy-start(bf16[512,512]{1,0:T(8,128)(2,1)S(1)} %shard_map.88.refs_0_) | copy-start | bytes 1572868
  27.8 3.8 %collective-permute-start.5 = (bf16[512,1024]{1,0:T(8,128)(2,1)S(1)}, bf16[512,1024]{1,0:T(8,128)(2,1)S(1)}, u32[]{:S(2)}, u32[]{:S(2)}) collective-permute-start(bf16[512,1024]{1,0:T(8,128)(2,1)S(1)} %copy-done), channel_id=1, source_target_pairs={{0,1},{1,0},{2,3},{3,2},{4,5},{5,4},{6,7},{7,6},{8,9},{9,8},{10,11... | collective-permute-start | bytes 3145736 | tf_op jit(solution)/shard_map/ppermute | solution.py:193
  27.9 4.1 %collective-permute-start.6 = (bf16[512,1024]{1,0:T(8,128)(2,1)S(1)}, bf16[512,1024]{1,0:T(8,128)(2,1)S(1)}, u32[]{:S(2)}, u32[]{:S(2)}) collective-permute-start(bf16[512,1024]{1,0:T(8,128)(2,1)S(1)} %collective-permute-done.3.refs_3_.refs_4_), channel_id=1, source_target_pairs={{0,1},{1,0},{2,3},{3,2},{4,5},{5,4},{6,7},{7,6},{8,9},{9,8},{10,11... | collective-permute-start | bytes 3145736 | tf_op jit(solution)/shard_map/ppermute | solution.py:193
  28.4 13.9 %collective-permute-start.8 = (bf16[512,512]{1,0:T(8,128)(2,1)S(1)}, bf16[512,512]{1,0:T(8,128)(2,1)S(1)}, u32[]{:S(2)}, u32[]{:S(2)}) collective-permute-start(bf16[512,512]{1,0:T(8,128)(2,1)S(1)} %shard_map.88.refs_0_), channel_id=1, source_target_pairs={{0,4},{4,0},{8,12},{12,8},{16,20},{20,16},{24,28},{28,24},{1,5},{5... | collective-permute-start | bytes 1572872 | tf_op jit(solution)/shard_map/ppermute | solution.py:193
  30.1 13.9 %collective-permute-start.9 = (bf16[512,512]{1,0:T(8,128)(2,1)}, bf16[512,512]{1,0:T(8,128)(2,1)}, u32[]{:S(2)}, u32[]{:S(2)}) collective-permute-start(bf16[512,512]{1,0:T(8,128)(2,1)} %collective-permute-done.4.refs_6_), channel_id=1, source_target_pairs={{0,2},{1,3},{2,0},{3,1},{4,6},{5,7},{6,4},{7,5},{8,10},{9,11},{10,... | collective-permute-start | bytes 1572872 | tf_op jit(solution)/shard_map/ppermute | solution.py:193
  31.6 3.6 %copy-start.8 = (bf16[512,1024]{1,0:T(8,128)(2,1)}, bf16[512,1024]{1,0:T(8,128)(2,1)S(1)}, u32[]{:S(2)}) copy-start(bf16[512,1024]{1,0:T(8,128)(2,1)S(1)} %collective-permute-done.5.refs_2_.refs_3_) | copy-start | bytes 3145732
  32.0 3.3 %copy-start.9 = (bf16[512,1024]{1,0:T(8,128)(2,1)}, bf16[512,1024]{1,0:T(8,128)(2,1)S(1)}, u32[]{:S(2)}) copy-start(bf16[512,1024]{1,0:T(8,128)(2,1)S(1)} %collective-permute-done.6.refs_4_.refs_5_) | copy-start | bytes 3145732
  35.7 8.3 %collective-permute-start.7 = (bf16[512,128]{1,0:T(8,128)(2,1)S(1)}, bf16[512,128]{1,0:T(8,128)(2,1)S(1)}, u32[]{:S(2)}, u32[]{:S(2)}) collective-permute-start(bf16[512,128]{1,0:T(8,128)(2,1)S(1)} %shard_map.90.refs_0_), channel_id=1, source_target_pairs={{0,8},{4,12},{8,0},{12,4},{16,24},{20,28},{24,16},{28,20},{1,9},{5... | collective-permute-start | bytes 393224 | tf_op jit(solution)/shard_map/ppermute | solution.py:193
  37.6 9.1 %collective-permute-start.11 = (bf16[512,512]{1,0:T(8,128)(2,1)}, bf16[512,512]{1,0:T(8,128)(2,1)S(1)}, u32[]{:S(2)}, u32[]{:S(2)}) collective-permute-start(bf16[512,512]{1,0:T(8,128)(2,1)} %collective-permute-done.4.refs_6_), channel_id=1, source_target_pairs={{0,1},{1,0},{2,3},{3,2},{4,5},{5,4},{6,7},{7,6},{8,9},{9,8},{10,11... | collective-permute-start | bytes 1572872 | tf_op jit(solution)/shard_map/ppermute | solution.py:193
  42.3 1.8 %copy-start.18 = (bf16[512,512]{1,0:T(8,128)(2,1)}, bf16[512,512]{1,0:T(8,128)(2,1)S(1)}, u32[]{:S(2)}) copy-start(bf16[512,512]{1,0:T(8,128)(2,1)S(1)} %collective-permute-done.8.refs_1_) | copy-start | bytes 1572868
  44.1 2.7 %collective-permute-start.12 = (bf16[512,512]{1,0:T(8,128)(2,1)}, bf16[512,512]{1,0:T(8,128)(2,1)S(1)}, u32[]{:S(2)}, u32[]{:S(2)}) collective-permute-start(bf16[512,512]{1,0:T(8,128)(2,1)} %collective-permute-done.9.refs_8_), channel_id=1, source_target_pairs={{0,1},{1,0},{2,3},{3,2},{4,5},{5,4},{6,7},{7,6},{8,9},{9,8},{10,11... | collective-permute-start | bytes 1572872 | tf_op jit(solution)/shard_map/ppermute | solution.py:193
  44.1 10.3 %collective-permute-start.10 = (bf16[512,128]{1,0:T(8,128)(2,1)S(1)}, bf16[512,128]{1,0:T(8,128)(2,1)S(1)}, u32[]{:S(2)}, u32[]{:S(2)}) collective-permute-start(bf16[512,128]{1,0:T(8,128)(2,1)S(1)} %shard_map.91), channel_id=1, source_target_pairs={{0,16},{4,20},{8,24},{12,28},{16,0},{20,4},{24,8},{28,12},{1,17},{... | collective-permute-start | bytes 393224 | tf_op jit(solution)/shard_map/ppermute | solution.py:193
  46.8 0.8 copy-start.19
  47.6 0.8 copy-start.20
  52.3 9.4 %collective-permute-start.14 = (bf16[512,256]{1,0:T(8,128)(2,1)}, bf16[512,256]{1,0:T(8,128)(2,1)S(1)}, u32[]{:S(2)}, u32[]{:S(2)}) collective-permute-start(bf16[512,256]{1,0:T(8,128)(2,1)} %get-tuple-element.66.refs_0_), channel_id=1, source_target_pairs={{0,8},{4,12},{8,0},{12,4},{16,24},{20,28},{24,16},{28,20},{1,9},{5... | collective-permute-start | bytes 786440 | tf_op jit(solution)/shard_map/ppermute | solution.py:237
  54.0 13.4 %collective-permute-start.17 = (bf16[512,256]{1,0:T(8,128)(2,1)}, bf16[512,256]{1,0:T(8,128)(2,1)S(1)}, u32[]{:S(2)}, u32[]{:S(2)}) collective-permute-start(bf16[512,256]{1,0:T(8,128)(2,1)} %get-tuple-element.68.refs_0_), channel_id=1, source_target_pairs={{0,8},{4,12},{8,0},{12,4},{16,24},{20,28},{24,16},{28,20},{1,9},{5... | collective-permute-start | bytes 786440 | tf_op jit(solution)/shard_map/ppermute | solution.py:237
  54.4 0.9 copy-start.21
  54.5 6.6 %collective-permute-start.15 = (bf16[512,128]{1,0:T(8,128)(2,1)S(1)}, bf16[512,128]{1,0:T(8,128)(2,1)S(1)}, u32[]{:S(2)}, u32[]{:S(2)}) collective-permute-start(bf16[512,128]{1,0:T(8,128)(2,1)S(1)} %add_convert_fusion.1), channel_id=1, source_target_pairs={{0,4},{4,0},{8,12},{12,8},{16,20},{20,16},{24,28},{28,24},{1,5},{5... | collective-permute-start | bytes 393224 | tf_op jit(solution)/shard_map/ppermute | solution.py:193
  55.3 6.4 %copy-start.16 = (bf16[512,256]{1,0:T(8,128)(2,1)S(1)}, bf16[512,256]{1,0:T(8,128)(2,1)}, u32[]{:S(2)}) copy-start(bf16[512,256]{1,0:T(8,128)(2,1)} %get-tuple-element.66.refs_0_) | copy-start | bytes 786436
  55.3 12.1 %copy-start.15 = (bf16[512,256]{1,0:T(8,128)(2,1)S(1)}, bf16[512,256]{1,0:T(8,128)(2,1)}, u32[]{:S(2)}) copy-start(bf16[512,256]{1,0:T(8,128)(2,1)} %get-tuple-element.68.refs_0_) | copy-start | bytes 786436
  55.3 22.6 %copy-start.14 = (bf16[512,512]{1,0:T(8,128)(2,1)S(1)}, bf16[512,512]{1,0:T(8,128)(2,1)}, u32[]{:S(2)}) copy-start(bf16[512,512]{1,0:T(8,128)(2,1)} %get-tuple-element.62.refs_0_) | copy-start | bytes 1572868
  55.3 22.6 %collective-permute-start.13 = (bf16[512,512]{1,0:T(8,128)(2,1)}, bf16[512,512]{1,0:T(8,128)(2,1)S(1)}, u32[]{:S(2)}, u32[]{:S(2)}) collective-permute-start(bf16[512,512]{1,0:T(8,128)(2,1)} %get-tuple-element.62.refs_0_), channel_id=1, source_target_pairs={{0,8},{4,12},{8,0},{12,4},{16,24},{20,28},{24,16},{28,20},{1,9},{5... | collective-permute-start | bytes 1572872 | tf_op jit(solution)/shard_map/ppermute | solution.py:237
  61.1 17.0 %copy-start.13 = (f32[512,512]{1,0:T(8,128)S(1)}, f32[512,512]{1,0:T(8,128)}, u32[]{:S(2)}) copy-start(f32[512,512]{1,0:T(8,128)} %get-tuple-element.74.refs_0_) | copy-start | bytes 3145732
  61.1 19.6 %copy-start.22 = (bf16[512,128]{1,0:T(8,128)(2,1)S(1)}, bf16[512,128]{1,0:T(8,128)(2,1)}, u32[]{:S(2)}) copy-start(bf16[512,128]{1,0:T(8,128)(2,1)} %copy-done.21) | copy-start | bytes 393220
  61.1 19.7 %copy-start.4 = (bf16[512,512]{1,0:T(8,128)(2,1)S(1)}, bf16[512,512]{1,0:T(8,128)(2,1)}, u32[]{:S(2)}) copy-start(bf16[512,512]{1,0:T(8,128)(2,1)} %refs_1_.9) | copy-start | bytes 1572868
  61.1 19.7 %copy-start.6 = (bf16[512,512]{1,0:T(8,128)(2,1)S(1)}, bf16[512,512]{1,0:T(8,128)(2,1)}, u32[]{:S(2)}) copy-start(bf16[512,512]{1,0:T(8,128)(2,1)} %refs_2_.9) | copy-start | bytes 1572868
  61.8 29.6 %copy-start.12 = (f32[512,512]{1,0:T(8,128)S(1)}, f32[512,512]{1,0:T(8,128)}, u32[]{:S(2)}) copy-start(f32[512,512]{1,0:T(8,128)} %get-tuple-element.73.refs_0_) | copy-start | bytes 3145732
  61.8 6.3 %collective-permute-start.16 = (bf16[512,256]{1,0:T(8,128)(2,1)S(1)}, bf16[512,256]{1,0:T(8,128)(2,1)S(1)}, u32[]{:S(2)}, u32[]{:S(2)}) collective-permute-start(bf16[512,256]{1,0:T(8,128)(2,1)S(1)} %shard_map.94), channel_id=1, source_target_pairs={{8,16},{12,20},{16,8},{20,12},{9,17},{13,21},{17,9},{21,13},{10,18... | collective-permute-start | bytes 786440 | tf_op jit(solution)/shard_map/ppermute | solution.py:237
  67.4 0.7 collective-permute-start.18
  78.2 13.3 %collective-permute-start.19 = (bf16[512,512]{1,0:T(8,128)(2,1)S(1)}, bf16[512,512]{1,0:T(8,128)(2,1)S(1)}, u32[]{:S(2)}, u32[]{:S(2)}) collective-permute-start(bf16[512,512]{1,0:T(8,128)(2,1)S(1)} %shard_map.97), channel_id=1, source_target_pairs={{0,8},{4,12},{8,0},{12,4},{16,24},{20,28},{24,16},{28,20},{1,9},{5... | collective-permute-start | bytes 1572872 | tf_op jit(solution)/shard_map/ppermute | solution.py:237
  79.8 11.6 %collective-permute-start.20 = (bf16[512,512]{1,0:T(8,128)(2,1)S(1)}, bf16[512,512]{1,0:T(8,128)(2,1)S(1)}, u32[]{:S(2)}, u32[]{:S(2)}) collective-permute-start(bf16[512,512]{1,0:T(8,128)(2,1)S(1)} %shard_map.98), channel_id=1, source_target_pairs={{8,16},{12,20},{16,8},{20,12},{9,17},{13,21},{17,9},{21,13},{10,18... | collective-permute-start | bytes 1572872 | tf_op jit(solution)/shard_map/ppermute | solution.py:237

commit v4 on v3

--- a/solution.py
+++ b/solution.py
@@ -198,10 +198,38 @@
     out[...] = sum(ref[...].astype(F32) for ref in sources).astype(out.dtype)
 
 
-def add(*terms, kind=BF16):
+def add(*terms, kind=BF16, cost=1):
     spec = pl.BlockSpec(memory_space=pltpu.VMEM)
     return pl.pallas_call(
         add_body,
+        out_shape=jax.ShapeDtypeStruct(terms[0].shape, kind),
+        in_specs=[spec] * len(terms),
+        out_specs=spec,
+        compiler_params=pltpu.CompilerParams(vmem_limit_bytes=8 << 20),
+        cost_estimate=pl.CostEstimate(flops=cost << 20, bytes_accessed=1 << 14, transcendentals=0),
+    )(*terms)
+
+
+def total_body(b_ref, e_ref, *refs):
+    *m_refs, out_ref = refs
+    width = out_ref.shape[1] // len(m_refs)
+    for i, m_ref in enumerate(m_refs):
+        at = slice(i * width, (i + 1) * width)
+        out_ref[:, at] = b_ref[:, at] + e_ref[:, at].astype(F32) + m_ref[...].astype(F32)
+
+
+def joined_body(b_ref, *refs):
+    *m_refs, out_ref = refs
+    width = out_ref.shape[1] // len(m_refs)
+    for i, m_ref in enumerate(m_refs):
+        at = slice(i * width, (i + 1) * width)
+        out_ref[:, at] = (b_ref[:, at] + m_ref[...].astype(F32)).astype(BF16)
+
+
+def small(body, kind, *terms):
+    spec = pl.BlockSpec(memory_space=pltpu.VMEM)
+    return pl.pallas_call(
+        body,
         out_shape=jax.ShapeDtypeStruct(terms[0].shape, kind),
         in_specs=[spec] * len(terms),
         out_specs=spec,
@@ -318,19 +346,28 @@
 
     if short:
         got = later.start(4)
-        *b0, b1 = product((0, 1), ((BF16,) * 2, (BF16,)), *operands)
-        e1, e2 = [send(b, OUTER) for b in b0], send(b1, OUTER)
+        pair = (BF16, BF16)
+        outs = product((0, 1), (pair, pair), *operands)
+        b0, b1 = list(outs[:2]), list(outs[2:])
+        e1, e2 = [send(b, OUTER) for b in b0], [send(b1[0], OUTER)]
         o, got, *b0 = phase(o, got, *b0)
         b2, b3 = product((2, 3), ((F32,), (F32,)), o, *operands[1:], cost=1 << 14)
         later.take(4, got)
         got = later.across()
-        e1[0], got, b2 = phase(e1[0], got, b2)
-        m2 = [send(add(b, e), MIDDLE) for b, e in zip(b0, e1)]
-        e2, got, *m2 = phase(e2, got, *m2)
+        e1[0], b1[1], got, b2 = phase(e1[0], b1[1], got, b2)
+        m2 = [send(add(b0[0], e1[0]), MIDDLE)]
+        e2 += [send(b1[1], OUTER)]
+        e1[1], m2[0] = phase(e1[1], m2[0])
+        m2 += [send(add(b0[1], e1[1], cost=1 << 14), MIDDLE)]
+        sent = add(b1[0], e2[0])
+        m3 = [send(sent, MIDDLE)]
+        m2[1], got, _ = phase(m2[1], got, sent)
+        sent = small(joined_body, BF16, b2, *m2)
+        e3 = send(sent, OUTER)
+        e2[1], _ = phase(e2[1], sent)
+        m3 += [send(add(b1[1], e2[1]), MIDDLE)]
         grads = gradients(later.result(got))
-        m3 = send(add(b1, e2), MIDDLE)
-        e3 = send(add(b2, jnp.concatenate(m2, axis=1)), OUTER)
-        weight_grad = add(b3, e3, m3, kind=F32)
+        weight_grad = small(total_body, F32, b3, e3, *m3)
     else:
         for bit in later.bits[1:]:
             later.take(bit, later.start(bit))

time: 93.5 us -> 91.8 us (0.982)
  waiting for transfers between devices: 35.3 us -> 21.3 us
  starting transfers between devices: 27.3 us -> 40.1 us
    ppermute x7 -> x9, waiting for transfers between devices: 20.7 us -> 6.48 us  [send(): lax.ppermute(a, 'seq', [(2 * s + i, 2 * t + i) for s, t in pairs for i in...]
    ppermute x7 -> x9, starting transfers between devices: 7.73 us -> 20.5 us  [send(): lax.ppermute(a, 'seq', [(2 * s + i, 2 * t + i) for s, t in pairs for i in...]
    pallas_call x0 -> x2, Pallas kernels: none -> 1.2 us  [small(): pl.pallas_call(body, out_shape=jax.ShapeDtypeStruct(terms[0].shape, kind)...]
    pallas_call x8 -> x7, Pallas kernels: 1.55 us -> 0.35 us  [add(): pl.pallas_call(add_body, out_shape=jax.ShapeDtypeStruct(terms[0].shape, k...]
    unnamed x46 -> x52, local copies, waits for them, and re-layouts: 5.7 us -> 5.71 us
  transfers between devices with their start and end apart: 21 -> 23, of which waited for: 10 -> 10; matrix products, arithmetic and copies ran while one was open for 0% -> 0% of each run, Pallas kernels for 23% -> 23%
where the time goes in v4:
time: 91.8 us; the launch traced here: 91.4 us
  starting transfers between devices  40.1 us (44%)
  Pallas kernels  23 us (25%)
  waiting for transfers between devices  21.3 us (23%)
  local copies, waits for them, and re-layouts  5.71 us (6%)
  between operations  1.09 us (1%)
    pallas_call x8, Pallas kernels, call(): pl.pallas_call(kernel, out_shape=outs, in_specs=[pl.BlockSpec(memory_spac...  21.4 us
    ppermute x9, starting transfers between devices, send(): lax.ppermute(a, 'seq', [(2 * s + i, 2 * t + i) for s, t in pairs for i in...  20.5 us
    ppermute x14, starting transfers between devices, flip(): lax.ppermute(a, axis, [(i, i ^ bit) for i in range(lax.axis_size(axis))])  19.6 us
    ppermute x14, waiting for transfers between devices, flip(): lax.ppermute(a, axis, [(i, i ^ bit) for i in range(lax.axis_size(axis))])  14.8 us
    ppermute x9, waiting for transfers between devices, send(): lax.ppermute(a, 'seq', [(2 * s + i, 2 * t + i) for s, t in pairs for i in...  6.48 us
    unnamed x52, local copies, waits for them, and re-layouts  5.71 us
  transfers between devices with their start and end apart: 23, of which 10 were waited for; matrix products, arithmetic and copies ran while one was open for 0% of the time, Pallas kernels for 23%

profile of v4, /device:TPU:0, one launch (start us, length us, event | category | flops | bytes accessed | tf_op | source)
XLA Modules:
  0.0 91.4 jit_solution(11357917613611124907)
XLA Ops:
  0.7 3.0 %collective-permute-start.3 = (bf16[512,1024]{1,0:T(8,128)(2,1)}, bf16[512,1024]{1,0:T(8,128)(2,1)S(1)}, u32[]{:S(2)}, u32[]{:S(2)}) collective-permute-start(bf16[512,1024]{1,0:T(8,128)(2,1)} %refs_2_.8), channel_id=1, source_target_pairs={{0,2},{1,3},{2,0},{3,1},{4,6},{5,7},{6,4},{7,5},{8,10},{9,11},{10,... | collective-permute-start | bytes 3145736 | tf_op jit(solution)/shard_map/ppermute | solution.py:193
  3.7 2.4 %shard_map.84 = (bf16[512,128]{1,0:T(8,128)(2,1)}, bf16[512,512]{1,0:T(8,128)(2,1)}) custom-call(bf16[512,512]{1,0:T(8,128)(2,1)} %refs_1_.9, bf16[512,512]{1,0:T(8,128)(2,1)} %refs_2_.9, bf16[512,1024]{1,0:T(8,128)(2,1)} %refs_2_.8), custom_call_target="tpu_custom_call" | custom-call | flops 1048576 | bytes 16384 | tf_op jit(solution)/shard_map/pallas_call | solution.py:29
  6.1 1.6 %collective-permute-start = (bf16[512,128]{1,0:T(8,128)(2,1)}, bf16[512,128]{1,0:T(8,128)(2,1)S(1)}, u32[]{:S(2)}, u32[]{:S(2)}) collective-permute-start(bf16[512,128]{1,0:T(8,128)(2,1)} %get-tuple-element.44.refs_0_), channel_id=1, source_target_pairs={{0,4},{4,0},{8,12},{12,8},{16,20},{20,16},{24,28},{28,24},{1,5},{5... | collective-permute-start | bytes 393224 | tf_op jit(solution)/shard_map/ppermute | solution.py:193
  7.7 3.7 %collective-permute-done.refs_1_ = bf16[512,128]{1,0:T(8,128)(2,1)S(1)} collective-permute-done((bf16[512,128]{1,0:T(8,128)(2,1)}, bf16[512,128]{1,0:T(8,128)(2,1)S(1)}, u32[]{:S(2)}, u32[]{:S(2)}) %collective-permute-start) | collective-permute-done | bytes 131104 | tf_op jit(solution)/shard_map/ppermute | solution.py:193
  11.3 1.5 %collective-permute-start.4 = (bf16[512,512]{1,0:T(8,128)(2,1)}, bf16[512,512]{1,0:T(8,128)(2,1)}, u32[]{:S(2)}, u32[]{:S(2)}) collective-permute-start(bf16[512,512]{1,0:T(8,128)(2,1)} %get-tuple-element.49), channel_id=1, source_target_pairs={{0,4},{4,0},{8,12},{12,8},{16,20},{20,16},{24,28},{28,24},{1,5},{5... | collective-permute-start | bytes 1572872 | tf_op jit(solution)/shard_map/ppermute | solution.py:193
  12.9 0.9 copy-done.17
  13.8 1.6 %collective-permute-start.1 = (bf16[512,128]{1,0:T(8,128)(2,1)S(1)}, bf16[512,128]{1,0:T(8,128)(2,1)S(1)}, u32[]{:S(2)}, u32[]{:S(2)}) collective-permute-start(bf16[512,128]{1,0:T(8,128)(2,1)S(1)} %shard_map.85.refs_0_), channel_id=1, source_target_pairs={{0,8},{4,12},{8,0},{12,4},{16,24},{20,28},{24,16},{28,20},{1,9},{5... | collective-permute-start | bytes 393224 | tf_op jit(solution)/shard_map/ppermute | solution.py:193
  15.4 3.4 %collective-permute-done.1.refs_1_ = bf16[512,128]{1,0:T(8,128)(2,1)S(1)} collective-permute-done((bf16[512,128]{1,0:T(8,128)(2,1)S(1)}, bf16[512,128]{1,0:T(8,128)(2,1)S(1)}, u32[]{:S(2)}, u32[]{:S(2)}) %collective-permute-start.1) | collective-permute-done | bytes 131104 | tf_op jit(solution)/shard_map/ppermute | solution.py:193
  18.9 2.7 %collective-permute-start.2 = (bf16[512,128]{1,0:T(8,128)(2,1)S(1)}, bf16[512,128]{1,0:T(8,128)(2,1)S(1)}, u32[]{:S(2)}, u32[]{:S(2)}) collective-permute-start(bf16[512,128]{1,0:T(8,128)(2,1)S(1)} %shard_map.86), channel_id=1, source_target_pairs={{0,16},{4,20},{8,24},{12,28},{16,0},{20,4},{24,8},{28,12},{1,17},{... | collective-permute-start | bytes 393224 | tf_op jit(solution)/shard_map/ppermute | solution.py:193
  21.5 1.0 %copy-done.1 = bf16[512,512]{1,0:T(8,128)(2,1)S(1)} copy-done((bf16[512,512]{1,0:T(8,128)(2,1)S(1)}, bf16[512,512]{1,0:T(8,128)(2,1)}, u32[]{:S(2)}) %copy-start.1) | copy-done | bytes 524312
  22.6 1.0 %copy-done.3 = bf16[512,512]{1,0:T(8,128)(2,1)S(1)} copy-done((bf16[512,512]{1,0:T(8,128)(2,1)S(1)}, bf16[512,512]{1,0:T(8,128)(2,1)}, u32[]{:S(2)}) %copy-start.3) | copy-done | bytes 524312
  23.6 1.0 %copy-done.5 = bf16[512,512]{1,0:T(8,128)(2,1)S(1)} copy-done((bf16[512,512]{1,0:T(8,128)(2,1)S(1)}, bf16[512,512]{1,0:T(8,128)(2,1)}, u32[]{:S(2)}) %copy-start.5) | copy-done | bytes 524312
  24.7 1.6 %shard_map.87.refs_2_ = f32[512,512]{1,0:T(8,128)S(1)} custom-call(bf16[512,512]{1,0:T(8,128)(2,1)S(1)} %copy-done.1, bf16[512,512]{1,0:T(8,128)(2,1)S(1)} %copy-done.3, bf16[512,512]{1,0:T(8,128)(2,1)S(1)} %copy-done.5), custom_call_target="tpu_custom_call" | custom-call | flops 1048576 | bytes 16384 | tf_op jit(solution)/shard_map/pallas_call | solution.py:29
  26.3 0.7 collective-permute-done.3.refs_3_.refs_4_
  27.0 0.1 add_convert_fusion.2.refs_0_.refs_4_
  27.1 0.6 shard_map.88.refs_0_
  27.9 0.5 collective-permute-start.6
  28.4 1.8 %collective-permute-start.8 = (bf16[512,512]{1,0:T(8,128)(2,1)S(1)}, bf16[512,512]{1,0:T(8,128)(2,1)S(1)}, u32[]{:S(2)}, u32[]{:S(2)}) collective-permute-start(bf16[512,512]{1,0:T(8,128)(2,1)S(1)} %shard_map.88.refs_0_), channel_id=1, source_target_pairs={{0,4},{4,0},{8,12},{12,8},{16,20},{20,16},{24,28},{28,24},{1,5},{5... | collective-permute-start | bytes 1572872 | tf_op jit(solution)/shard_map/ppermute | solution.py:193
  30.1 1.5 %collective-permute-start.9 = (bf16[512,512]{1,0:T(8,128)(2,1)}, bf16[512,512]{1,0:T(8,128)(2,1)}, u32[]{:S(2)}, u32[]{:S(2)}) collective-permute-start(bf16[512,512]{1,0:T(8,128)(2,1)} %collective-permute-done.4.refs_6_), channel_id=1, source_target_pairs={{0,2},{1,3},{2,0},{3,1},{4,6},{5,7},{6,4},{7,5},{8,10},{9,11},{10,... | collective-permute-start | bytes 1572872 | tf_op jit(solution)/shard_map/ppermute | solution.py:193
  31.6 0.4 collective-permute-done.6.refs_4_.refs_5_
  32.0 3.2 %shard_map.89.refs_1_.refs_3_ = bf16[512,512]{1,0:T(8,128)(2,1)S(1)} custom-call(bf16[4096,512]{1,0:T(8,128)(2,1)S(1)} %copy-done.10, bf16[512,1024]{1,0:T(8,128)(2,1)S(1)} %copy-done, bf16[512,1024]{1,0:T(8,128)(2,1)S(1)} %collective-permute-done.5.refs_2_.refs_3_, bf16[512,1024]{1,0:T(8,128)(2,1)S(1)} %collective-permute-done.3.refs_3_.refs_4_, ...), custom_call_target="tpu_custom_call" | custom-call | flops 1048576 | bytes 16384 | tf_op jit(solution)/shard_map/pallas_call | solution.py:29
  35.3 0.5 shard_map.90.refs_0_
  35.7 1.9 %collective-permute-start.7 = (bf16[512,128]{1,0:T(8,128)(2,1)S(1)}, bf16[512,128]{1,0:T(8,128)(2,1)S(1)}, u32[]{:S(2)}, u32[]{:S(2)}) collective-permute-start(bf16[512,128]{1,0:T(8,128)(2,1)S(1)} %shard_map.90.refs_0_), channel_id=1, source_target_pairs={{0,8},{4,12},{8,0},{12,4},{16,24},{20,28},{24,16},{28,20},{1,9},{5... | collective-permute-start | bytes 393224 | tf_op jit(solution)/shard_map/ppermute | solution.py:193
  37.6 4.6 %collective-permute-done.8.refs_1_ = bf16[512,512]{1,0:T(8,128)(2,1)S(1)} collective-permute-done((bf16[512,512]{1,0:T(8,128)(2,1)S(1)}, bf16[512,512]{1,0:T(8,128)(2,1)S(1)}, u32[]{:S(2)}, u32[]{:S(2)}) %collective-permute-start.8) | collective-permute-done | bytes 524320 | tf_op jit(solution)/shard_map/ppermute | solution.py:193
  42.3 1.8 %collective-permute-done.9.refs_8_ = bf16[512,512]{1,0:T(8,128)(2,1)} collective-permute-done((bf16[512,512]{1,0:T(8,128)(2,1)}, bf16[512,512]{1,0:T(8,128)(2,1)}, u32[]{:S(2)}, u32[]{:S(2)}) %collective-permute-start.9) | collective-permute-done | bytes 524320 | tf_op jit(solution)/shard_map/ppermute | solution.py:193
  44.1 2.7 %collective-permute-start.10 = (bf16[512,128]{1,0:T(8,128)(2,1)S(1)}, bf16[512,128]{1,0:T(8,128)(2,1)S(1)}, u32[]{:S(2)}, u32[]{:S(2)}) collective-permute-start(bf16[512,128]{1,0:T(8,128)(2,1)S(1)} %shard_map.91), channel_id=1, source_target_pairs={{0,16},{4,20},{8,24},{12,28},{16,0},{20,4},{24,8},{28,12},{1,17},{... | collective-permute-start | bytes 393224 | tf_op jit(solution)/shard_map/ppermute | solution.py:193
  46.8 0.8 copy-done.20
  47.6 0.8 copy-done.21
  48.4 4.0 %shard_map.92 = (bf16[512,256]{1,0:T(8,128)(2,1)}, bf16[512,256]{1,0:T(8,128)(2,1)}, bf16[512,256]{1,0:T(8,128)(2,1)}, bf16[512,256]{1,0:T(8,128)(2,1)}) custom-call(bf16[512,512]{1,0:T(8,128)(2,1)} %copy-done.11, bf16[512,512]{1,0:T(8,128)(2,1)} %copy-done.19, bf16[512,1024]{1,0:T(8,128)(2,1)} %refs_2_.8, bf16[512,1024]{1,0:T(8,128)(2,1)} %copy-done.8, ...), custom_call_target="tpu_custom_call" | custom-call | flops 1048576 | bytes 16384 | tf_op jit(solution)/shard_map/pallas_call | solution.py:29
  52.3 1.7 %collective-permute-start.14 = (bf16[512,256]{1,0:T(8,128)(2,1)}, bf16[512,256]{1,0:T(8,128)(2,1)S(1)}, u32[]{:S(2)}, u32[]{:S(2)}) collective-permute-start(bf16[512,256]{1,0:T(8,128)(2,1)} %get-tuple-element.66.refs_0_), channel_id=1, source_target_pairs={{0,8},{4,12},{8,0},{12,4},{16,24},{20,28},{24,16},{28,20},{1,9},{5... | collective-permute-start | bytes 786440 | tf_op jit(solution)/shard_map/ppermute | solution.py:265
  54.0 0.4 collective-permute-start.13
  54.4 0.1 add_convert_fusion.1
  54.5 0.8 collective-permute-start.15
  55.3 4.1 %shard_map.93 = (f32[512,512]{1,0:T(8,128)}, f32[512,512]{1,0:T(8,128)}) custom-call(bf16[512,512]{1,0:T(8,128)(2,1)} %copy-done.11, bf16[512,512]{1,0:T(8,128)(2,1)} %copy-done.19, bf16[512,1024]{1,0:T(8,128)(2,1)} %refs_2_.8, bf16[512,1024]{1,0:T(8,128)(2,1)} %copy-done.8, bf16[512,1024]{1,0:T(8,128)(2,1)} %copy-done.7, bf16[512,1024]{1,0:T(8,128)(2,1)} %copy-done.9, ...), custom_call_target="tpu_custom_call" | custom-call | flops 17179869184 | bytes 16384 | tf_op jit(solution)/shard_map/pallas_call | solution.py:29
  59.4 0.2 collective-permute-done.15
  59.7 2.1 %collective-permute-done.14.refs_1_ = bf16[512,256]{1,0:T(8,128)(2,1)S(1)} collective-permute-done((bf16[512,256]{1,0:T(8,128)(2,1)}, bf16[512,256]{1,0:T(8,128)(2,1)S(1)}, u32[]{:S(2)}, u32[]{:S(2)}) %collective-permute-start.14) | collective-permute-done | bytes 262176 | tf_op jit(solution)/shard_map/ppermute | solution.py:265
  61.8 0.7 collective-permute-start.16
  62.6 3.1 %collective-permute-start.18 = (bf16[512,256]{1,0:T(8,128)(2,1)S(1)}, bf16[512,256]{1,0:T(8,128)(2,1)S(1)}, u32[]{:S(2)}, u32[]{:S(2)}) collective-permute-start(bf16[512,256]{1,0:T(8,128)(2,1)S(1)} %copy-done.15), channel_id=1, source_target_pairs={{0,8},{4,12},{8,0},{12,4},{16,24},{20,28},{24,16},{28,20},{1,9},{5... | collective-permute-start | bytes 786440 | tf_op jit(solution)/shard_map/ppermute | solution.py:265
  65.6 1.7 %collective-permute-done.13.refs_1_ = bf16[512,256]{1,0:T(8,128)(2,1)S(1)} collective-permute-done((bf16[512,256]{1,0:T(8,128)(2,1)}, bf16[512,256]{1,0:T(8,128)(2,1)S(1)}, u32[]{:S(2)}, u32[]{:S(2)}) %collective-permute-start.13) | collective-permute-done | bytes 262176 | tf_op jit(solution)/shard_map/ppermute | solution.py:265
  67.5 0.8 collective-permute-start.17
  68.3 6.4 %collective-permute-start.21 = (bf16[512,256]{1,0:T(8,128)(2,1)S(1)}, bf16[512,256]{1,0:T(8,128)(2,1)S(1)}, u32[]{:S(2)}, u32[]{:S(2)}) collective-permute-start(bf16[512,256]{1,0:T(8,128)(2,1)S(1)} %copy-done.14), channel_id=1, source_target_pairs={{0,8},{4,12},{8,0},{12,4},{16,24},{20,28},{24,16},{28,20},{1,9},{5... | collective-permute-start | bytes 786440 | tf_op jit(solution)/shard_map/ppermute | solution.py:265
  74.8 0.1 shard_map.98
  74.9 6.0 %collective-permute-start.19 = (bf16[512,512]{1,0:T(8,128)(2,1)S(1)}, bf16[512,512]{1,0:T(8,128)(2,1)S(1)}, u32[]{:S(2)}, u32[]{:S(2)}) collective-permute-start(bf16[512,512]{1,0:T(8,128)(2,1)S(1)} %shard_map.98), channel_id=1, source_target_pairs={{0,8},{4,12},{8,0},{12,4},{16,24},{20,28},{24,16},{28,20},{1,9},{5... | collective-permute-start | bytes 1572872 | tf_op jit(solution)/shard_map/ppermute | solution.py:265
  80.8 0.7 collective-permute-start.20
  81.6 0.9 collective-permute-start.22
  82.6 5.0 %shard_map.97 = (bf16[512,512]{1,0:T(8,128)(2,1)}, bf16[512,512]{1,0:T(8,128)(2,1)}, bf16[512,512]{1,0:T(8,128)(2,1)}) custom-call(bf16[512,512]{1,0:T(8,128)(2,1)S(1)} %copy-done.2, bf16[512,512]{1,0:T(8,128)(2,1)S(1)} %copy-done.4, bf16[512,512]{1,0:T(8,128)(2,1)S(1)} %copy-done.6, bf16[512,512]{1,0:T(8,128)(2,1)S(1)} %shard_map.89.refs_1_.refs_3_, ...), custom_call_target="tpu_custom_call" | custom-call | flops 1048576 | bytes 16384 | tf_op jit(solution)/shard_map/pallas_call | solution.py:29
  87.6 2.6 %collective-permute-done.19.e_ref = bf16[512,512]{1,0:T(8,128)(2,1)S(1)} collective-permute-done((bf16[512,512]{1,0:T(8,128)(2,1)S(1)}, bf16[512,512]{1,0:T(8,128)(2,1)S(1)}, u32[]{:S(2)}, u32[]{:S(2)}) %collective-permute-start.19) | collective-permute-done | bytes 524320 | tf_op jit(solution)/shard_map/ppermute | solution.py:265
  90.3 1.1 %shard_map.100 = f32[512,512]{1,0:T(8,128)} custom-call(f32[512,512]{1,0:T(8,128)S(1)} %copy-done.12, bf16[512,512]{1,0:T(8,128)(2,1)S(1)} %collective-permute-done.19.e_ref, bf16[512,256]{1,0:T(8,128)(2,1)S(1)} %collective-permute-done.20.refs_0_, bf16[512,256]{1,0:T(8,128)(2,1)S(1)} %collective-permute-done.22.refs_1_), custom_call_target="tpu_custom_call" | custom-call | flops 1048576 | bytes 16384 | tf_op jit(solution)/shard_map/pallas_call | solution.py:231
  (70 shorter events, 0.6 us)
Async XLA Ops:
  0.6 27.1 %copy-start = (bf16[512,1024]{1,0:T(8,128)(2,1)S(1)}, bf16[512,1024]{1,0:T(8,128)(2,1)}, u32[]{:S(2)}) copy-start(bf16[512,1024]{1,0:T(8,128)(2,1)} %refs_2_.8) | copy-start | bytes 3145732
  0.6 26.5 %copy-start.2 = (bf16[512,512]{1,0:T(8,128)(2,1)S(1)}, bf16[512,512]{1,0:T(8,128)(2,1)}, u32[]{:S(2)}) copy-start(bf16[512,512]{1,0:T(8,128)(2,1)} %refs_0_.8) | copy-start | bytes 1572868
  0.7 26.4 %collective-permute-start.3 = (bf16[512,1024]{1,0:T(8,128)(2,1)}, bf16[512,1024]{1,0:T(8,128)(2,1)S(1)}, u32[]{:S(2)}, u32[]{:S(2)}) collective-permute-start(bf16[512,1024]{1,0:T(8,128)(2,1)} %refs_2_.8), channel_id=1, source_target_pairs={{0,2},{1,3},{2,0},{3,1},{4,6},{5,7},{6,4},{7,5},{8,10},{9,11},{10,... | collective-permute-start | bytes 3145736 | tf_op jit(solution)/shard_map/ppermute | solution.py:193
  6.1 5.2 %collective-permute-start = (bf16[512,128]{1,0:T(8,128)(2,1)}, bf16[512,128]{1,0:T(8,128)(2,1)S(1)}, u32[]{:S(2)}, u32[]{:S(2)}) collective-permute-start(bf16[512,128]{1,0:T(8,128)(2,1)} %get-tuple-element.44.refs_0_), channel_id=1, source_target_pairs={{0,4},{4,0},{8,12},{12,8},{16,20},{20,16},{24,28},{28,24},{1,5},{5... | collective-permute-start | bytes 393224 | tf_op jit(solution)/shard_map/ppermute | solution.py:193
  11.3 15.0 %collective-permute-start.4 = (bf16[512,512]{1,0:T(8,128)(2,1)}, bf16[512,512]{1,0:T(8,128)(2,1)}, u32[]{:S(2)}, u32[]{:S(2)}) collective-permute-start(bf16[512,512]{1,0:T(8,128)(2,1)} %get-tuple-element.49), channel_id=1, source_target_pairs={{0,4},{4,0},{8,12},{12,8},{16,20},{20,16},{24,28},{28,24},{1,5},{5... | collective-permute-start | bytes 1572872 | tf_op jit(solution)/shard_map/ppermute | solution.py:193
  12.9 0.9 copy-start.17
  13.8 5.0 %collective-permute-start.1 = (bf16[512,128]{1,0:T(8,128)(2,1)S(1)}, bf16[512,128]{1,0:T(8,128)(2,1)S(1)}, u32[]{:S(2)}, u32[]{:S(2)}) collective-permute-start(bf16[512,128]{1,0:T(8,128)(2,1)S(1)} %shard_map.85.refs_0_), channel_id=1, source_target_pairs={{0,8},{4,12},{8,0},{12,4},{16,24},{20,28},{24,16},{28,20},{1,9},{5... | collective-permute-start | bytes 393224 | tf_op jit(solution)/shard_map/ppermute | solution.py:193
  18.9 7.4 %collective-permute-start.2 = (bf16[512,128]{1,0:T(8,128)(2,1)S(1)}, bf16[512,128]{1,0:T(8,128)(2,1)S(1)}, u32[]{:S(2)}, u32[]{:S(2)}) collective-permute-start(bf16[512,128]{1,0:T(8,128)(2,1)S(1)} %shard_map.86), channel_id=1, source_target_pairs={{0,16},{4,20},{8,24},{12,28},{16,0},{20,4},{24,8},{28,12},{1,17},{... | collective-permute-start | bytes 393224 | tf_op jit(solution)/shard_map/ppermute | solution.py:193
  21.5 1.0 %copy-start.1 = (bf16[512,512]{1,0:T(8,128)(2,1)S(1)}, bf16[512,512]{1,0:T(8,128)(2,1)}, u32[]{:S(2)}) copy-start(bf16[512,512]{1,0:T(8,128)(2,1)} %refs_0_.8) | copy-start | bytes 1572868
  22.6 1.0 %copy-start.3 = (bf16[512,512]{1,0:T(8,128)(2,1)S(1)}, bf16[512,512]{1,0:T(8,128)(2,1)}, u32[]{:S(2)}) copy-start(bf16[512,512]{1,0:T(8,128)(2,1)} %refs_1_.9) | copy-start | bytes 1572868
  23.6 1.0 %copy-start.5 = (bf16[512,512]{1,0:T(8,128)(2,1)S(1)}, bf16[512,512]{1,0:T(8,128)(2,1)}, u32[]{:S(2)}) copy-start(bf16[512,512]{1,0:T(8,128)(2,1)} %refs_2_.9) | copy-start | bytes 1572868
  24.7 7.4 %copy-start.10 = (bf16[4096,512]{1,0:T(8,128)(2,1)S(1)}, bf16[4096,512]{1,0:T(8,128)(2,1)}, u32[]{:S(2)}) copy-start(bf16[4096,512]{1,0:T(8,128)(2,1)} %refs_0_.6) | copy-start | bytes 12582916
  27.0 8.2 %copy-start.7 = (bf16[512,1024]{1,0:T(8,128)(2,1)}, bf16[512,1024]{1,0:T(8,128)(2,1)S(1)}, u32[]{:S(2)}) copy-start(bf16[512,1024]{1,0:T(8,128)(2,1)S(1)} %collective-permute-done.3.refs_3_.refs_4_) | copy-start | bytes 3145732
  27.8 7.5 %copy-start.11 = (bf16[512,512]{1,0:T(8,128)(2,1)}, bf16[512,512]{1,0:T(8,128)(2,1)S(1)}, u32[]{:S(2)}) copy-start(bf16[512,512]{1,0:T(8,128)(2,1)S(1)} %shard_map.88.refs_0_) | copy-start | bytes 1572868
  27.8 3.8 %collective-permute-start.5 = (bf16[512,1024]{1,0:T(8,128)(2,1)S(1)}, bf16[512,1024]{1,0:T(8,128)(2,1)S(1)}, u32[]{:S(2)}, u32[]{:S(2)}) collective-permute-start(bf16[512,1024]{1,0:T(8,128)(2,1)S(1)} %copy-done), channel_id=1, source_target_pairs={{0,1},{1,0},{2,3},{3,2},{4,5},{5,4},{6,7},{7,6},{8,9},{9,8},{10,11... | collective-permute-start | bytes 3145736 | tf_op jit(solution)/shard_map/ppermute | solution.py:193
  27.9 4.1 %collective-permute-start.6 = (bf16[512,1024]{1,0:T(8,128)(2,1)S(1)}, bf16[512,1024]{1,0:T(8,128)(2,1)S(1)}, u32[]{:S(2)}, u32[]{:S(2)}) collective-permute-start(bf16[512,1024]{1,0:T(8,128)(2,1)S(1)} %collective-permute-done.3.refs_3_.refs_4_), channel_id=1, source_target_pairs={{0,1},{1,0},{2,3},{3,2},{4,5},{5,4},{6,7},{7,6},{8,9},{9,8},{10,11... | collective-permute-start | bytes 3145736 | tf_op jit(solution)/shard_map/ppermute | solution.py:193
  28.4 13.9 %collective-permute-start.8 = (bf16[512,512]{1,0:T(8,128)(2,1)S(1)}, bf16[512,512]{1,0:T(8,128)(2,1)S(1)}, u32[]{:S(2)}, u32[]{:S(2)}) collective-permute-start(bf16[512,512]{1,0:T(8,128)(2,1)S(1)} %shard_map.88.refs_0_), channel_id=1, source_target_pairs={{0,4},{4,0},{8,12},{12,8},{16,20},{20,16},{24,28},{28,24},{1,5},{5... | collective-permute-start | bytes 1572872 | tf_op jit(solution)/shard_map/ppermute | solution.py:193
  30.1 13.9 %collective-permute-start.9 = (bf16[512,512]{1,0:T(8,128)(2,1)}, bf16[512,512]{1,0:T(8,128)(2,1)}, u32[]{:S(2)}, u32[]{:S(2)}) collective-permute-start(bf16[512,512]{1,0:T(8,128)(2,1)} %collective-permute-done.4.refs_6_), channel_id=1, source_target_pairs={{0,2},{1,3},{2,0},{3,1},{4,6},{5,7},{6,4},{7,5},{8,10},{9,11},{10,... | collective-permute-start | bytes 1572872 | tf_op jit(solution)/shard_map/ppermute | solution.py:193
  31.6 3.6 %copy-start.8 = (bf16[512,1024]{1,0:T(8,128)(2,1)}, bf16[512,1024]{1,0:T(8,128)(2,1)S(1)}, u32[]{:S(2)}) copy-start(bf16[512,1024]{1,0:T(8,128)(2,1)S(1)} %collective-permute-done.5.refs_2_.refs_3_) | copy-start | bytes 3145732
  32.0 3.3 %copy-start.9 = (bf16[512,1024]{1,0:T(8,128)(2,1)}, bf16[512,1024]{1,0:T(8,128)(2,1)S(1)}, u32[]{:S(2)}) copy-start(bf16[512,1024]{1,0:T(8,128)(2,1)S(1)} %collective-permute-done.6.refs_4_.refs_5_) | copy-start | bytes 3145732
  35.7 8.3 %collective-permute-start.7 = (bf16[512,128]{1,0:T(8,128)(2,1)S(1)}, bf16[512,128]{1,0:T(8,128)(2,1)S(1)}, u32[]{:S(2)}, u32[]{:S(2)}) collective-permute-start(bf16[512,128]{1,0:T(8,128)(2,1)S(1)} %shard_map.90.refs_0_), channel_id=1, source_target_pairs={{0,8},{4,12},{8,0},{12,4},{16,24},{20,28},{24,16},{28,20},{1,9},{5... | collective-permute-start | bytes 393224 | tf_op jit(solution)/shard_map/ppermute | solution.py:193
  37.6 9.1 %collective-permute-start.11 = (bf16[512,512]{1,0:T(8,128)(2,1)}, bf16[512,512]{1,0:T(8,128)(2,1)S(1)}, u32[]{:S(2)}, u32[]{:S(2)}) collective-permute-start(bf16[512,512]{1,0:T(8,128)(2,1)} %collective-permute-done.4.refs_6_), channel_id=1, source_target_pairs={{0,1},{1,0},{2,3},{3,2},{4,5},{5,4},{6,7},{7,6},{8,9},{9,8},{10,11... | collective-permute-start | bytes 1572872 | tf_op jit(solution)/shard_map/ppermute | solution.py:193
  42.3 1.8 %copy-start.19 = (bf16[512,512]{1,0:T(8,128)(2,1)}, bf16[512,512]{1,0:T(8,128)(2,1)S(1)}, u32[]{:S(2)}) copy-start(bf16[512,512]{1,0:T(8,128)(2,1)S(1)} %collective-permute-done.8.refs_1_) | copy-start | bytes 1572868
  44.1 2.7 %collective-permute-start.12 = (bf16[512,512]{1,0:T(8,128)(2,1)}, bf16[512,512]{1,0:T(8,128)(2,1)S(1)}, u32[]{:S(2)}, u32[]{:S(2)}) collective-permute-start(bf16[512,512]{1,0:T(8,128)(2,1)} %collective-permute-done.9.refs_8_), channel_id=1, source_target_pairs={{0,1},{1,0},{2,3},{3,2},{4,5},{5,4},{6,7},{7,6},{8,9},{9,8},{10,11... | collective-permute-start | bytes 1572872 | tf_op jit(solution)/shard_map/ppermute | solution.py:193
  44.1 10.3 %collective-permute-start.10 = (bf16[512,128]{1,0:T(8,128)(2,1)S(1)}, bf16[512,128]{1,0:T(8,128)(2,1)S(1)}, u32[]{:S(2)}, u32[]{:S(2)}) collective-permute-start(bf16[512,128]{1,0:T(8,128)(2,1)S(1)} %shard_map.91), channel_id=1, source_target_pairs={{0,16},{4,20},{8,24},{12,28},{16,0},{20,4},{24,8},{28,12},{1,17},{... | collective-permute-start | bytes 393224 | tf_op jit(solution)/shard_map/ppermute | solution.py:193
  47.6 0.8 copy-start.21
  52.3 9.4 %collective-permute-start.14 = (bf16[512,256]{1,0:T(8,128)(2,1)}, bf16[512,256]{1,0:T(8,128)(2,1)S(1)}, u32[]{:S(2)}, u32[]{:S(2)}) collective-permute-start(bf16[512,256]{1,0:T(8,128)(2,1)} %get-tuple-element.66.refs_0_), channel_id=1, source_target_pairs={{0,8},{4,12},{8,0},{12,4},{16,24},{20,28},{24,16},{28,20},{1,9},{5... | collective-permute-start | bytes 786440 | tf_op jit(solution)/shard_map/ppermute | solution.py:265
  54.0 13.4 %collective-permute-start.13 = (bf16[512,256]{1,0:T(8,128)(2,1)}, bf16[512,256]{1,0:T(8,128)(2,1)S(1)}, u32[]{:S(2)}, u32[]{:S(2)}) collective-permute-start(bf16[512,256]{1,0:T(8,128)(2,1)} %get-tuple-element.65.refs_0_), channel_id=1, source_target_pairs={{0,8},{4,12},{8,0},{12,4},{16,24},{20,28},{24,16},{28,20},{1,9},{5... | collective-permute-start | bytes 786440 | tf_op jit(solution)/shard_map/ppermute | solution.py:265
  54.4 5.0 %copy-start.22 = (bf16[512,128]{1,0:T(8,128)(2,1)}, bf16[512,128]{1,0:T(8,128)(2,1)S(1)}, u32[]{:S(2)}) copy-start(bf16[512,128]{1,0:T(8,128)(2,1)S(1)} %collective-permute-done.10) | copy-start | bytes 393220
  54.5 7.2 %copy-start.16 = (bf16[512,256]{1,0:T(8,128)(2,1)S(1)}, bf16[512,256]{1,0:T(8,128)(2,1)}, u32[]{:S(2)}) copy-start(bf16[512,256]{1,0:T(8,128)(2,1)} %get-tuple-element.66.refs_0_) | copy-start | bytes 786436
  54.5 8.0 %copy-start.15 = (bf16[512,256]{1,0:T(8,128)(2,1)S(1)}, bf16[512,256]{1,0:T(8,128)(2,1)}, u32[]{:S(2)}) copy-start(bf16[512,256]{1,0:T(8,128)(2,1)} %get-tuple-element.73.refs_0_) | copy-start | bytes 786436
  54.5 12.8 %copy-start.18 = (bf16[512,256]{1,0:T(8,128)(2,1)S(1)}, bf16[512,256]{1,0:T(8,128)(2,1)}, u32[]{:S(2)}) copy-start(bf16[512,256]{1,0:T(8,128)(2,1)} %get-tuple-element.65.refs_0_) | copy-start | bytes 786436
  54.5 5.1 %collective-permute-start.15 = (bf16[512,128]{1,0:T(8,128)(2,1)S(1)}, bf16[512,128]{1,0:T(8,128)(2,1)S(1)}, u32[]{:S(2)}, u32[]{:S(2)}) collective-permute-start(bf16[512,128]{1,0:T(8,128)(2,1)S(1)} %add_convert_fusion.1), channel_id=1, source_target_pairs={{0,4},{4,0},{8,12},{12,8},{16,20},{20,16},{24,28},{28,24},{1,5},{5... | collective-permute-start | bytes 393224 | tf_op jit(solution)/shard_map/ppermute | solution.py:193
  59.7 2.8 %copy-start.24 = (bf16[512,128]{1,0:T(8,128)(2,1)}, bf16[512,128]{1,0:T(8,128)(2,1)S(1)}, u32[]{:S(2)}) copy-start(bf16[512,128]{1,0:T(8,128)(2,1)S(1)} %collective-permute-done.15) | copy-start | bytes 393220
  61.8 5.6 %collective-permute-start.16 = (bf16[512,256]{1,0:T(8,128)(2,1)S(1)}, bf16[512,256]{1,0:T(8,128)(2,1)S(1)}, u32[]{:S(2)}, u32[]{:S(2)}) collective-permute-start(bf16[512,256]{1,0:T(8,128)(2,1)S(1)} %shard_map.94), channel_id=1, source_target_pairs={{8,16},{12,20},{16,8},{20,12},{9,17},{13,21},{17,9},{21,13},{10,18... | collective-permute-start | bytes 786440 | tf_op jit(solution)/shard_map/ppermute | solution.py:265
  62.5 5.8 %copy-start.14 = (bf16[512,256]{1,0:T(8,128)(2,1)S(1)}, bf16[512,256]{1,0:T(8,128)(2,1)}, u32[]{:S(2)}) copy-start(bf16[512,256]{1,0:T(8,128)(2,1)} %get-tuple-element.82.refs_0_) | copy-start | bytes 786436
  62.5 12.2 %copy-start.13 = (f32[512,512]{1,0:T(8,128)S(1)}, f32[512,512]{1,0:T(8,128)}, u32[]{:S(2)}) copy-start(f32[512,512]{1,0:T(8,128)} %get-tuple-element.79.b_ref) | copy-start | bytes 3145732
  62.5 19.9 %copy-start.23 = (bf16[512,128]{1,0:T(8,128)(2,1)S(1)}, bf16[512,128]{1,0:T(8,128)(2,1)}, u32[]{:S(2)}) copy-start(bf16[512,128]{1,0:T(8,128)(2,1)} %copy-done.22) | copy-start | bytes 393220
  62.6 19.9 %copy-start.25 = (bf16[512,128]{1,0:T(8,128)(2,1)S(1)}, bf16[512,128]{1,0:T(8,128)(2,1)}, u32[]{:S(2)}) copy-start(bf16[512,128]{1,0:T(8,128)(2,1)} %copy-done.24) | copy-start | bytes 393220
  62.6 12.1 %collective-permute-start.18 = (bf16[512,256]{1,0:T(8,128)(2,1)S(1)}, bf16[512,256]{1,0:T(8,128)(2,1)S(1)}, u32[]{:S(2)}, u32[]{:S(2)}) collective-permute-start(bf16[512,256]{1,0:T(8,128)(2,1)S(1)} %copy-done.15), channel_id=1, source_target_pairs={{0,8},{4,12},{8,0},{12,4},{16,24},{20,28},{24,16},{28,20},{1,9},{5... | collective-permute-start | bytes 786440 | tf_op jit(solution)/shard_map/ppermute | solution.py:265
  67.4 15.1 %copy-start.4 = (bf16[512,512]{1,0:T(8,128)(2,1)S(1)}, bf16[512,512]{1,0:T(8,128)(2,1)}, u32[]{:S(2)}) copy-start(bf16[512,512]{1,0:T(8,128)(2,1)} %refs_1_.9) | copy-start | bytes 1572868
  67.5 15.1 %copy-start.6 = (bf16[512,512]{1,0:T(8,128)(2,1)S(1)}, bf16[512,512]{1,0:T(8,128)(2,1)}, u32[]{:S(2)}) copy-start(bf16[512,512]{1,0:T(8,128)(2,1)} %refs_2_.9) | copy-start | bytes 1572868
  67.5 22.8 %copy-start.12 = (f32[512,512]{1,0:T(8,128)S(1)}, f32[512,512]{1,0:T(8,128)}, u32[]{:S(2)}) copy-start(f32[512,512]{1,0:T(8,128)} %get-tuple-element.78.b_ref) | copy-start | bytes 3145732
  67.5 7.3 %collective-permute-start.17 = (bf16[512,256]{1,0:T(8,128)(2,1)S(1)}, bf16[512,256]{1,0:T(8,128)(2,1)S(1)}, u32[]{:S(2)}, u32[]{:S(2)}) collective-permute-start(bf16[512,256]{1,0:T(8,128)(2,1)S(1)} %shard_map.95), channel_id=1, source_target_pairs={{8,16},{12,20},{16,8},{20,12},{9,17},{13,21},{17,9},{21,13},{10,18... | collective-permute-start | bytes 786440 | tf_op jit(solution)/shard_map/ppermute | solution.py:265
  68.3 13.2 %collective-permute-start.21 = (bf16[512,256]{1,0:T(8,128)(2,1)S(1)}, bf16[512,256]{1,0:T(8,128)(2,1)S(1)}, u32[]{:S(2)}, u32[]{:S(2)}) collective-permute-start(bf16[512,256]{1,0:T(8,128)(2,1)S(1)} %copy-done.14), channel_id=1, source_target_pairs={{0,8},{4,12},{8,0},{12,4},{16,24},{20,28},{24,16},{28,20},{1,9},{5... | collective-permute-start | bytes 786440 | tf_op jit(solution)/shard_map/ppermute | solution.py:265
  74.9 15.4 %collective-permute-start.19 = (bf16[512,512]{1,0:T(8,128)(2,1)S(1)}, bf16[512,512]{1,0:T(8,128)(2,1)S(1)}, u32[]{:S(2)}, u32[]{:S(2)}) collective-permute-start(bf16[512,512]{1,0:T(8,128)(2,1)S(1)} %shard_map.98), channel_id=1, source_target_pairs={{0,8},{4,12},{8,0},{12,4},{16,24},{20,28},{24,16},{28,20},{1,9},{5... | collective-permute-start | bytes 1572872 | tf_op jit(solution)/shard_map/ppermute | solution.py:265
  80.8 6.8 %collective-permute-start.20 = (bf16[512,256]{1,0:T(8,128)(2,1)S(1)}, bf16[512,256]{1,0:T(8,128)(2,1)S(1)}, u32[]{:S(2)}, u32[]{:S(2)}) collective-permute-start(bf16[512,256]{1,0:T(8,128)(2,1)S(1)} %shard_map.96), channel_id=1, source_target_pairs={{8,16},{12,20},{16,8},{20,12},{9,17},{13,21},{17,9},{21,13},{10,18... | collective-permute-start | bytes 786440 | tf_op jit(solution)/shard_map/ppermute | solution.py:265
  81.6 6.0 %collective-permute-start.22 = (bf16[512,256]{1,0:T(8,128)(2,1)S(1)}, bf16[512,256]{1,0:T(8,128)(2,1)S(1)}, u32[]{:S(2)}, u32[]{:S(2)}) collective-permute-start(bf16[512,256]{1,0:T(8,128)(2,1)S(1)} %shard_map.99), channel_id=1, source_target_pairs={{8,16},{12,20},{16,8},{20,12},{9,17},{13,21},{17,9},{21,13},{10,18... | collective-permute-start | bytes 786440 | tf_op jit(solution)/shard_map/ppermute | solution.py:265
  (1 other events, 0.8 us)

commit v5 on v3

--- a/solution.py
+++ b/solution.py
@@ -17,7 +17,7 @@
     return lax.dot_general(a, b, (((on_a,), (on_b,)), ((), ())), preferred_element_type=F32)
 
 
-def call(body, outs, *args, scratch=None, cost=1, vmem=12):
+def call(body, outs, *args, scratch=None, cost=1, vmem=12, direct=()):
     scratch = [(a.shape, a.dtype) for a in args] if scratch is None else scratch
     count = len(args)
 
@@ -29,7 +29,9 @@
     return pl.pallas_call(
         kernel,
         out_shape=outs,
-        in_specs=[pl.BlockSpec(memory_space=pl.ANY)] * count,
+        in_specs=[
+            pl.BlockSpec(memory_space=pltpu.VMEM if i in direct else pl.ANY) for i in range(count)
+        ],
         out_specs=jax.tree.map(lambda _: pl.BlockSpec(memory_space=pltpu.VMEM), outs),
         scratch_shapes=[pltpu.VMEM(*buffer) for buffer in scratch]
         + [pltpu.SemaphoreType.DMA((count + len(scratch),))],
@@ -185,6 +187,36 @@
             first += part.shape[1]
 
 
+def first_body(factor, count, loaded, sources, results, buffers, sems):
+    seq, me = lax.axis_index("seq"), lax.axis_index("head")
+    which = slot(lax.div(seq, 2), 0) ^ me
+    for j in range(count):
+
+        @pl.when(which == j)
+        def _():
+            piece = sources[1 + j]
+            width = buffers[0].shape[1]
+            if piece.shape[1] != width:
+                first = pl.multiple_of(lax.rem(seq, 2) * width, width)
+                piece = piece.at[:, pl.ds(first, width)]
+            pltpu.make_async_copy(piece, buffers[0], sems.at[0]).start()
+
+    o_ref = sources[0]
+    if loaded:
+        load = pltpu.make_async_copy(o_ref, buffers[1], sems.at[1])
+        load.start()
+        load.wait()
+        o_ref = buffers[1]
+    pltpu.make_async_copy(buffers[0], buffers[0], sems.at[0]).wait()
+    total = factor * dot(buffers[0][...], o_ref[...], 0, 0)
+    if len(sources) > count + 1:
+        total += sources[-1][...]
+    first = 0
+    for out in results:
+        out[...] = total[:, first : first + out.shape[1]].astype(out.dtype)
+        first += out.shape[1]
+
+
 def phase(*values):
     return lax.optimization_barrier(values)
 
@@ -198,11 +230,29 @@
     out[...] = sum(ref[...].astype(F32) for ref in sources).astype(out.dtype)
 
 
-def add(*terms, kind=BF16):
+def add(*terms, kind=BF16, cost=1):
     spec = pl.BlockSpec(memory_space=pltpu.VMEM)
     return pl.pallas_call(
         add_body,
         out_shape=jax.ShapeDtypeStruct(terms[0].shape, kind),
+        in_specs=[spec] * len(terms),
+        out_specs=spec,
+        compiler_params=pltpu.CompilerParams(vmem_limit_bytes=8 << 20),
+        cost_estimate=pl.CostEstimate(flops=cost << 20, bytes_accessed=1 << 14, transcendentals=0),
+    )(*terms)
+
+
+def total_body(front_ref, back_ref, m_ref, e_ref, out_ref):
+    width = front_ref.shape[1]
+    out_ref[:, :width] = front_ref[...]
+    out_ref[:, width:] = back_ref[...] + m_ref[...].astype(F32) + e_ref[...].astype(F32)
+
+
+def small(body, kind, *terms, wide=1):
+    spec = pl.BlockSpec(memory_space=pltpu.VMEM)
+    return pl.pallas_call(
+        body,
+        out_shape=jax.ShapeDtypeStruct((terms[0].shape[0], terms[0].shape[1] * wide), kind),
         in_specs=[spec] * len(terms),
         out_specs=spec,
         compiler_params=pltpu.CompilerParams(vmem_limit_bytes=8 << 20),
@@ -307,7 +357,15 @@
     (back_term,) = call(state, [state_shape], queries, attn_grad)
     later = Scan(back_term, True)
     got = later.start(2)
-    got, n, far = phase(got, n, far)
+    if short:
+        first = functools.partial(first_body, factor, n_head)
+        scratch = [((rows, cols // 2), BF16), ((rows, width), BF16)]
+        outs = [shaped((cols // 2, width), F32)]
+        o, _ = phase(o, back_term)
+        (begun,) = call(functools.partial(first, True), outs, o, *mine, scratch=scratch, vmem=60)
+        got, n, far, begun = phase(got, n, far, begun)
+    else:
+        got, n, far = phase(got, n, far)
     far_c = flip(far, "head", 1)
     later.take(2, got)
     operands = (o, n, *mine, near, near_c, far, far_c)
@@ -318,19 +376,33 @@
 
     if short:
         got = later.start(4)
-        *b0, b1 = product((0, 1), ((BF16,) * 2, (BF16,)), *operands)
-        e1, e2 = [send(b, OUTER) for b in b0], send(b1, OUTER)
+        pair = (BF16, BF16)
+        outs = [shaped((cols // 2, width // 2))] * 2
+        theirs = (near, near_c, far, far_c)
+        first = functools.partial(first, False)
+        b0 = call(first, outs, n, *theirs, begun, scratch=scratch[:1], vmem=8, direct=(0, n_head + 1))
+        e1 = [send(b, OUTER) for b in b0]
         o, got, *b0 = phase(o, got, *b0)
-        b2, b3 = product((2, 3), ((F32,), (F32,)), o, *operands[1:], cost=1 << 14)
+        outs = product((1, 2, 3), (pair, (F32, F32), (F32, F32)), o, *operands[1:], cost=1 << 14)
+        b1, b2, (b3, b3_back) = list(outs[:2]), outs[2:4], outs[4:]
+        e2 = [send(b1[0], OUTER)]
         later.take(4, got)
         got = later.across()
-        e1[0], got, b2 = phase(e1[0], got, b2)
-        m2 = [send(add(b, e), MIDDLE) for b, e in zip(b0, e1)]
-        e2, got, *m2 = phase(e2, got, *m2)
+        e1[0], b1[1], got, *b2 = phase(e1[0], b1[1], got, *b2)
+        m2 = [send(add(b0[0], e1[0]), MIDDLE)]
+        e2 += [send(b1[1], OUTER)]
+        m2 += [send(add(b0[1], e1[1], cost=1024), MIDDLE)]
+        e2[0], m2[0] = phase(e2[0], m2[0])
+        sent = add(b1[0], e2[0], cost=2048)
+        m3 = [send(sent, MIDDLE)]
+        m2[1], got, _ = phase(m2[1], got, sent)
+        parts = [add(b, m) for b, m in zip(b2, m2)]
+        e3 = [send(p, OUTER) for p in parts]
+        e2[1], _, _ = phase(e2[1], *parts)
+        m3 += [send(add(b1[1], e2[1]), MIDDLE)]
         grads = gradients(later.result(got))
-        m3 = send(add(b1, e2), MIDDLE)
-        e3 = send(add(b2, jnp.concatenate(m2, axis=1)), OUTER)
-        weight_grad = add(b3, e3, m3, kind=F32)
+        front = add(b3, m3[0], e3[0], kind=F32, cost=2048)
+        weight_grad = small(total_body, F32, front, b3_back, m3[1], e3[1], wide=2)
     else:
         for bit in later.bits[1:]:
             later.take(bit, later.start(bit))

time: 93.5 us -> 89.1 us (0.953)
  waiting for transfers between devices: 35.3 us -> 20.8 us
  starting transfers between devices: 27.3 us -> 36.6 us
  Pallas kernels: 23 us -> 24.4 us
    ppermute x7 -> x10, waiting for transfers between devices: 20.7 us -> 7.16 us  [send(): lax.ppermute(a, 'seq', [(2 * s + i, 2 * t + i) for s, t in pairs for i in...]
    ppermute x7 -> x10, starting transfers between devices: 7.73 us -> 17.3 us  [send(): lax.ppermute(a, 'seq', [(2 * s + i, 2 * t + i) for s, t in pairs for i in...]
    pallas_call x8 -> x9, Pallas kernels: 21.4 us -> 22.8 us  [call(): pl.pallas_call(kernel, out_shape=outs, in_specs=[pl.BlockSpec(memory_spac...]
    pallas_call x0 -> x1, Pallas kernels: none -> 1.08 us  [small(): pl.pallas_call(body, out_shape=jax.ShapeDtypeStruct((terms[0].shape[0], t...]
    pallas_call x8 -> x10, Pallas kernels: 1.55 us -> 0.52 us  [add(): pl.pallas_call(add_body, out_shape=jax.ShapeDtypeStruct(terms[0].shape, k...]
    ppermute x14, waiting for transfers between devices: 14.6 us -> 13.6 us  [flip(): lax.ppermute(a, axis, [(i, i ^ bit) for i in range(lax.axis_size(axis))])]
    unnamed x46 -> x44, local copies, waits for them, and re-layouts: 5.7 us -> 5.51 us
  transfers between devices with their start and end apart: 21 -> 24, of which waited for: 10 -> 10; matrix products, arithmetic and copies ran while one was open for 0% -> 0% of each run, Pallas kernels for 23% -> 26%
where the time goes in v5:
time: 89.1 us; the launch traced here: 88.6 us
  starting transfers between devices  36.6 us (41%)
  Pallas kernels  24.4 us (27%)
  waiting for transfers between devices  20.8 us (23%)
  local copies, waits for them, and re-layouts  5.51 us (6%)
  between operations  1.05 us (1%)
    pallas_call x9, Pallas kernels, call(): pl.pallas_call(kernel, out_shape=outs, in_specs=[pl.BlockSpec(memory_spac...  22.8 us
    ppermute x14, starting transfers between devices, flip(): lax.ppermute(a, axis, [(i, i ^ bit) for i in range(lax.axis_size(axis))])  19.3 us
    ppermute x10, starting transfers between devices, send(): lax.ppermute(a, 'seq', [(2 * s + i, 2 * t + i) for s, t in pairs for i in...  17.3 us
    ppermute x14, waiting for transfers between devices, flip(): lax.ppermute(a, axis, [(i, i ^ bit) for i in range(lax.axis_size(axis))])  13.6 us
    ppermute x10, waiting for transfers between devices, send(): lax.ppermute(a, 'seq', [(2 * s + i, 2 * t + i) for s, t in pairs for i in...  7.16 us
    unnamed x44, local copies, waits for them, and re-layouts  5.51 us
  transfers between devices with their start and end apart: 24, of which 10 were waited for; matrix products, arithmetic and copies ran while one was open for 0% of the time, Pallas kernels for 26%

profile of v5, /device:TPU:0, one launch (start us, length us, event | category | flops | bytes accessed | tf_op | source)
XLA Modules:
  0.0 88.6 jit_solution(11903154174678586606)
XLA Ops:
  0.7 3.0 %collective-permute-start.3 = (bf16[512,1024]{1,0:T(8,128)(2,1)}, bf16[512,1024]{1,0:T(8,128)(2,1)S(1)}, u32[]{:S(2)}, u32[]{:S(2)}) collective-permute-start(bf16[512,1024]{1,0:T(8,128)(2,1)} %refs_2_.6), channel_id=1, source_target_pairs={{0,2},{1,3},{2,0},{3,1},{4,6},{5,7},{6,4},{7,5},{8,10},{9,11},{10,... | collective-permute-start | bytes 3145736 | tf_op jit(solution)/shard_map/ppermute | solution.py:225
  3.7 2.4 %shard_map.84 = (bf16[512,128]{1,0:T(8,128)(2,1)}, bf16[512,512]{1,0:T(8,128)(2,1)}) custom-call(bf16[512,512]{1,0:T(8,128)(2,1)} %refs_1_.11, bf16[512,512]{1,0:T(8,128)(2,1)} %refs_2_.7, bf16[512,1024]{1,0:T(8,128)(2,1)} %refs_2_.6), custom_call_target="tpu_custom_call" | custom-call | flops 1048576 | bytes 16384 | tf_op jit(solution)/shard_map/pallas_call | solution.py:29
  6.1 1.6 %collective-permute-start = (bf16[512,128]{1,0:T(8,128)(2,1)}, bf16[512,128]{1,0:T(8,128)(2,1)S(1)}, u32[]{:S(2)}, u32[]{:S(2)}) collective-permute-start(bf16[512,128]{1,0:T(8,128)(2,1)} %get-tuple-element.49.refs_0_), channel_id=1, source_target_pairs={{0,4},{4,0},{8,12},{12,8},{16,20},{20,16},{24,28},{28,24},{1,5},{5... | collective-permute-start | bytes 393224 | tf_op jit(solution)/shard_map/ppermute | solution.py:225
  7.7 3.7 %collective-permute-done.refs_1_ = bf16[512,128]{1,0:T(8,128)(2,1)S(1)} collective-permute-done((bf16[512,128]{1,0:T(8,128)(2,1)}, bf16[512,128]{1,0:T(8,128)(2,1)S(1)}, u32[]{:S(2)}, u32[]{:S(2)}) %collective-permute-start) | collective-permute-done | bytes 131104 | tf_op jit(solution)/shard_map/ppermute | solution.py:225
  11.3 1.5 %collective-permute-start.4 = (bf16[512,512]{1,0:T(8,128)(2,1)}, bf16[512,512]{1,0:T(8,128)(2,1)}, u32[]{:S(2)}, u32[]{:S(2)}) collective-permute-start(bf16[512,512]{1,0:T(8,128)(2,1)} %get-tuple-element.54), channel_id=1, source_target_pairs={{0,4},{4,0},{8,12},{12,8},{16,20},{20,16},{24,28},{28,24},{1,5},{5... | collective-permute-start | bytes 1572872 | tf_op jit(solution)/shard_map/ppermute | solution.py:225
  12.9 0.9 %copy-done.19 = bf16[512,128]{1,0:T(8,128)(2,1)S(1)} copy-done((bf16[512,128]{1,0:T(8,128)(2,1)S(1)}, bf16[512,128]{1,0:T(8,128)(2,1)}, u32[]{:S(2)}) %copy-start.19) | copy-done | bytes 131096
  13.8 1.6 %collective-permute-start.1 = (bf16[512,128]{1,0:T(8,128)(2,1)S(1)}, bf16[512,128]{1,0:T(8,128)(2,1)S(1)}, u32[]{:S(2)}, u32[]{:S(2)}) collective-permute-start(bf16[512,128]{1,0:T(8,128)(2,1)S(1)} %shard_map.85.refs_0_), channel_id=1, source_target_pairs={{0,8},{4,12},{8,0},{12,4},{16,24},{20,28},{24,16},{28,20},{1,9},{5... | collective-permute-start | bytes 393224 | tf_op jit(solution)/shard_map/ppermute | solution.py:225
  15.4 3.4 %collective-permute-done.1.refs_1_ = bf16[512,128]{1,0:T(8,128)(2,1)S(1)} collective-permute-done((bf16[512,128]{1,0:T(8,128)(2,1)S(1)}, bf16[512,128]{1,0:T(8,128)(2,1)S(1)}, u32[]{:S(2)}, u32[]{:S(2)}) %collective-permute-start.1) | collective-permute-done | bytes 131104 | tf_op jit(solution)/shard_map/ppermute | solution.py:225
  18.9 2.7 %collective-permute-start.2 = (bf16[512,128]{1,0:T(8,128)(2,1)S(1)}, bf16[512,128]{1,0:T(8,128)(2,1)S(1)}, u32[]{:S(2)}, u32[]{:S(2)}) collective-permute-start(bf16[512,128]{1,0:T(8,128)(2,1)S(1)} %shard_map.86), channel_id=1, source_target_pairs={{0,16},{4,20},{8,24},{12,28},{16,0},{20,4},{24,8},{28,12},{1,17},{... | collective-permute-start | bytes 393224 | tf_op jit(solution)/shard_map/ppermute | solution.py:225
  21.5 1.0 %copy-done.1 = bf16[512,512]{1,0:T(8,128)(2,1)S(1)} copy-done((bf16[512,512]{1,0:T(8,128)(2,1)S(1)}, bf16[512,512]{1,0:T(8,128)(2,1)}, u32[]{:S(2)}) %copy-start.1) | copy-done | bytes 524312
  22.6 1.0 %copy-done.3 = bf16[512,512]{1,0:T(8,128)(2,1)S(1)} copy-done((bf16[512,512]{1,0:T(8,128)(2,1)S(1)}, bf16[512,512]{1,0:T(8,128)(2,1)}, u32[]{:S(2)}) %copy-start.3) | copy-done | bytes 524312
  23.6 1.0 %copy-done.5 = bf16[512,512]{1,0:T(8,128)(2,1)S(1)} copy-done((bf16[512,512]{1,0:T(8,128)(2,1)S(1)}, bf16[512,512]{1,0:T(8,128)(2,1)}, u32[]{:S(2)}) %copy-start.5) | copy-done | bytes 524312
  24.7 1.6 %shard_map.87.refs_2_ = f32[512,512]{1,0:T(8,128)S(1)} custom-call(bf16[512,512]{1,0:T(8,128)(2,1)S(1)} %copy-done.1, bf16[512,512]{1,0:T(8,128)(2,1)S(1)} %copy-done.3, bf16[512,512]{1,0:T(8,128)(2,1)S(1)} %copy-done.5), custom_call_target="tpu_custom_call" | custom-call | flops 1048576 | bytes 16384 | tf_op jit(solution)/shard_map/pallas_call | solution.py:29
  26.3 0.7 collective-permute-done.3.refs_3_.refs_4_
  27.0 0.1 add_convert_fusion.2.refs_0_.refs_4_
  27.1 0.6 shard_map.88.refs_0_
  27.9 0.5 collective-permute-start.6
  28.4 1.8 %collective-permute-start.8 = (bf16[512,512]{1,0:T(8,128)(2,1)S(1)}, bf16[512,512]{1,0:T(8,128)(2,1)}, u32[]{:S(2)}, u32[]{:S(2)}) collective-permute-start(bf16[512,512]{1,0:T(8,128)(2,1)S(1)} %shard_map.88.refs_0_), channel_id=1, source_target_pairs={{0,4},{4,0},{8,12},{12,8},{16,20},{20,16},{24,28},{28,24},{1,5},{5... | collective-permute-start | bytes 1572872 | tf_op jit(solution)/shard_map/ppermute | solution.py:225
  30.1 1.5 %collective-permute-start.9 = (bf16[512,512]{1,0:T(8,128)(2,1)}, bf16[512,512]{1,0:T(8,128)(2,1)}, u32[]{:S(2)}, u32[]{:S(2)}) collective-permute-start(bf16[512,512]{1,0:T(8,128)(2,1)} %collective-permute-done.4.refs_1_.refs_6_), channel_id=1, source_target_pairs={{0,2},{1,3},{2,0},{3,1},{4,6},{5,7},{6,4},{7,5},{8,10},{9,11},{10,... | collective-permute-start | bytes 1572872 | tf_op jit(solution)/shard_map/ppermute | solution.py:225
  31.6 0.4 collective-permute-done.6.refs_4_.refs_5_
  32.0 3.2 %shard_map.89.refs_1_.refs_3_ = bf16[512,512]{1,0:T(8,128)(2,1)S(1)} custom-call(bf16[4096,512]{1,0:T(8,128)(2,1)S(1)} %copy-done.7, bf16[512,1024]{1,0:T(8,128)(2,1)S(1)} %copy-done, bf16[512,1024]{1,0:T(8,128)(2,1)S(1)} %collective-permute-done.5.refs_2_.refs_3_, bf16[512,1024]{1,0:T(8,128)(2,1)S(1)} %collective-permute-done.3.refs_3_.refs_4_, ...), custom_call_target="tpu_custom_call" | custom-call | flops 1048576 | bytes 16384 | tf_op jit(solution)/shard_map/pallas_call | solution.py:29
  35.3 0.5 shard_map.90.refs_0_
  35.7 1.9 %collective-permute-start.7 = (bf16[512,128]{1,0:T(8,128)(2,1)S(1)}, bf16[512,128]{1,0:T(8,128)(2,1)S(1)}, u32[]{:S(2)}, u32[]{:S(2)}) collective-permute-start(bf16[512,128]{1,0:T(8,128)(2,1)S(1)} %shard_map.90.refs_0_), channel_id=1, source_target_pairs={{0,8},{4,12},{8,0},{12,4},{16,24},{20,28},{24,16},{28,20},{1,9},{5... | collective-permute-start | bytes 393224 | tf_op jit(solution)/shard_map/ppermute | solution.py:225
  37.6 2.7 %shard_map.91.refs_5_ = f32[512,512]{1,0:T(8,128)} custom-call(bf16[512,512]{1,0:T(8,128)(2,1)} %copy-done.12, bf16[512,1024]{1,0:T(8,128)(2,1)} %refs_2_.6, bf16[512,1024]{1,0:T(8,128)(2,1)} %copy-done.9, bf16[512,1024]{1,0:T(8,128)(2,1)} %copy-done.8, bf16[512,1024]{1,0:T(8,128)(2,1)} %copy-done.10), custom_call_target="tpu_custom_call" | custom-call | flops 1048576 | bytes 16384 | tf_op jit(solution)/shard_map/pallas_call | solution.py:29
  40.3 2.0 %collective-permute-done.8.refs_0_.refs_1_ = bf16[512,512]{1,0:T(8,128)(2,1)} collective-permute-done((bf16[512,512]{1,0:T(8,128)(2,1)S(1)}, bf16[512,512]{1,0:T(8,128)(2,1)}, u32[]{:S(2)}, u32[]{:S(2)}) %collective-permute-start.8) | collective-permute-done | bytes 524320 | tf_op jit(solution)/shard_map/ppermute | solution.py:225
  42.4 1.7 %collective-permute-done.9.refs_3_.refs_8_ = bf16[512,512]{1,0:T(8,128)(2,1)} collective-permute-done((bf16[512,512]{1,0:T(8,128)(2,1)}, bf16[512,512]{1,0:T(8,128)(2,1)}, u32[]{:S(2)}, u32[]{:S(2)}) %collective-permute-start.9) | collective-permute-done | bytes 524320 | tf_op jit(solution)/shard_map/ppermute | solution.py:225
  44.1 2.7 %collective-permute-start.10 = (bf16[512,128]{1,0:T(8,128)(2,1)S(1)}, bf16[512,128]{1,0:T(8,128)(2,1)S(1)}, u32[]{:S(2)}, u32[]{:S(2)}) collective-permute-start(bf16[512,128]{1,0:T(8,128)(2,1)S(1)} %shard_map.92), channel_id=1, source_target_pairs={{0,16},{4,20},{8,24},{12,28},{16,0},{20,4},{24,8},{28,12},{1,17},{... | collective-permute-start | bytes 393224 | tf_op jit(solution)/shard_map/ppermute | solution.py:225
  46.8 1.4 %copy-done.11 = f32[512,512]{1,0:T(8,128)S(1)} copy-done((f32[512,512]{1,0:T(8,128)S(1)}, f32[512,512]{1,0:T(8,128)}, u32[]{:S(2)}) %copy-start.11) | copy-done | bytes 1048600
  48.2 1.8 %shard_map.93 = (bf16[512,256]{1,0:T(8,128)(2,1)S(1)}, bf16[512,256]{1,0:T(8,128)(2,1)S(1)}) custom-call(bf16[512,512]{1,0:T(8,128)(2,1)} %collective-permute-done.8.refs_0_.refs_1_, bf16[512,512]{1,0:T(8,128)(2,1)} %collective-permute-done.4.refs_1_.refs_6_, bf16[512,512]{1,0:T(8,128)(2,1)S(1)} %collective-permute-done.11.refs_2_.refs_7_, ...), custom_call_target="tpu_custom_call" | custom-call | flops 1048576 | bytes 16384 | tf_op jit(solution)/shard_map/pallas_call | solution.py:29
  50.0 1.6 %collective-permute-start.15 = (bf16[512,256]{1,0:T(8,128)(2,1)S(1)}, bf16[512,256]{1,0:T(8,128)(2,1)S(1)}, u32[]{:S(2)}, u32[]{:S(2)}) collective-permute-start(bf16[512,256]{1,0:T(8,128)(2,1)S(1)} %get-tuple-element.79.refs_0_), channel_id=1, source_target_pairs={{0,8},{4,12},{8,0},{12,4},{16,24},{20,28},{24,16},{28,20},{1,9},{5... | collective-permute-start | bytes 786440 | tf_op jit(solution)/shard_map/ppermute | solution.py:287
  51.6 0.4 collective-permute-start.13
  52.1 1.7 %collective-permute-done.10 = bf16[512,128]{1,0:T(8,128)(2,1)S(1)} collective-permute-done((bf16[512,128]{1,0:T(8,128)(2,1)S(1)}, bf16[512,128]{1,0:T(8,128)(2,1)S(1)}, u32[]{:S(2)}, u32[]{:S(2)}) %collective-permute-start.10) | collective-permute-done | bytes 131104 | tf_op jit(solution)/shard_map/ppermute | solution.py:225
  53.8 0.1 add_convert_fusion.1
  53.9 0.5 collective-permute-start.16
  54.4 4.9 %shard_map.95 = (bf16[512,256]{1,0:T(8,128)(2,1)}, bf16[512,256]{1,0:T(8,128)(2,1)}, f32[512,256]{1,0:T(8,128)}, f32[512,256]{1,0:T(8,128)}, f32[512,256]{1,0:T(8,128)}, /*index=5*/f32[512,256]{1,0:T(8,128)}) custom-call(bf16[512,512]{1,0:T(8,128)(2,1)} %copy-done.12, bf16[512,512]{1,0:T(8,128)(2,1)} %collective-permute-done.8.refs_0_.refs_1_, ...), custom_call_target="tpu_custom_call" | custom-call | flops 17179869184 | bytes 16384 | tf_op jit(solution)/shard_map/pallas_call | solution.py:29
  59.3 0.8 collective-permute-start.17
  60.2 0.7 collective-permute-start.18
  60.9 4.0 %collective-permute-done.13.refs_1_ = bf16[512,256]{1,0:T(8,128)(2,1)S(1)} collective-permute-done((bf16[512,256]{1,0:T(8,128)(2,1)S(1)}, bf16[512,256]{1,0:T(8,128)(2,1)S(1)}, u32[]{:S(2)}, u32[]{:S(2)}) %collective-permute-start.13) | collective-permute-done | bytes 262176 | tf_op jit(solution)/shard_map/ppermute | solution.py:287
  65.0 0.8 collective-permute-start.14
  65.9 4.2 %collective-permute-start.21 = (bf16[512,256]{1,0:T(8,128)(2,1)S(1)}, bf16[512,256]{1,0:T(8,128)(2,1)S(1)}, u32[]{:S(2)}, u32[]{:S(2)}) collective-permute-start(bf16[512,256]{1,0:T(8,128)(2,1)S(1)} %copy-done.18), channel_id=1, source_target_pairs={{0,8},{4,12},{8,0},{12,4},{16,24},{20,28},{24,16},{28,20},{1,9},{5... | collective-permute-start | bytes 786440 | tf_op jit(solution)/shard_map/ppermute | solution.py:287
  70.0 0.5 collective-permute-done.17.refs_1_
  70.6 0.8 collective-permute-start.19
  71.5 6.1 %collective-permute-start.20 = (bf16[512,256]{1,0:T(8,128)(2,1)S(1)}, bf16[512,256]{1,0:T(8,128)(2,1)S(1)}, u32[]{:S(2)}, u32[]{:S(2)}) collective-permute-start(bf16[512,256]{1,0:T(8,128)(2,1)S(1)} %shard_map.99), channel_id=1, source_target_pairs={{0,8},{4,12},{8,0},{12,4},{16,24},{20,28},{24,16},{28,20},{1,9},{5... | collective-permute-start | bytes 786440 | tf_op jit(solution)/shard_map/ppermute | solution.py:287
  77.7 0.9 %collective-permute-start.23 = (bf16[512,256]{1,0:T(8,128)(2,1)S(1)}, bf16[512,256]{1,0:T(8,128)(2,1)S(1)}, u32[]{:S(2)}, u32[]{:S(2)}) collective-permute-start(bf16[512,256]{1,0:T(8,128)(2,1)S(1)} %shard_map.101), channel_id=1, source_target_pairs={{0,8},{4,12},{8,0},{12,4},{16,24},{20,28},{24,16},{28,20},{1,9},{5... | collective-permute-start | bytes 786440 | tf_op jit(solution)/shard_map/ppermute | solution.py:287
  78.7 0.9 collective-permute-start.22
  79.7 5.0 %shard_map.98 = (bf16[512,512]{1,0:T(8,128)(2,1)}, bf16[512,512]{1,0:T(8,128)(2,1)}, bf16[512,512]{1,0:T(8,128)(2,1)}) custom-call(bf16[512,512]{1,0:T(8,128)(2,1)S(1)} %copy-done.2, bf16[512,512]{1,0:T(8,128)(2,1)S(1)} %copy-done.4, bf16[512,512]{1,0:T(8,128)(2,1)S(1)} %copy-done.6, bf16[512,512]{1,0:T(8,128)(2,1)S(1)} %shard_map.89.refs_1_.refs_3_, ...), custom_call_target="tpu_custom_call" | custom-call | flops 1048576 | bytes 16384 | tf_op jit(solution)/shard_map/pallas_call | solution.py:29
  84.8 2.7 %collective-permute-done.23.e_ref = bf16[512,256]{1,0:T(8,128)(2,1)S(1)} collective-permute-done((bf16[512,256]{1,0:T(8,128)(2,1)S(1)}, bf16[512,256]{1,0:T(8,128)(2,1)S(1)}, u32[]{:S(2)}, u32[]{:S(2)}) %collective-permute-start.23) | collective-permute-done | bytes 262176 | tf_op jit(solution)/shard_map/ppermute | solution.py:287
  87.5 1.1 %shard_map.103 = f32[512,512]{1,0:T(8,128)} custom-call(f32[512,256]{1,0:T(8,128)S(1)} %shard_map.100.front_ref, f32[512,256]{1,0:T(8,128)S(1)} %copy-done.13, bf16[512,256]{1,0:T(8,128)(2,1)S(1)} %collective-permute-done.22.m_ref, bf16[512,256]{1,0:T(8,128)(2,1)S(1)} %collective-permute-done.23.e_ref), custom_call_target="tpu_custom_call" | custom-call | flops 1048576 | bytes 16384 | tf_op jit(solution)/shard_map/pallas_call | solution.py:253
  (67 shorter events, 0.8 us)
Async XLA Ops:
  0.6 27.1 %copy-start = (bf16[512,1024]{1,0:T(8,128)(2,1)S(1)}, bf16[512,1024]{1,0:T(8,128)(2,1)}, u32[]{:S(2)}) copy-start(bf16[512,1024]{1,0:T(8,128)(2,1)} %refs_2_.6) | copy-start | bytes 3145732
  0.6 26.5 %copy-start.2 = (bf16[512,512]{1,0:T(8,128)(2,1)S(1)}, bf16[512,512]{1,0:T(8,128)(2,1)}, u32[]{:S(2)}) copy-start(bf16[512,512]{1,0:T(8,128)(2,1)} %refs_0_.8) | copy-start | bytes 1572868
  0.7 26.4 %collective-permute-start.3 = (bf16[512,1024]{1,0:T(8,128)(2,1)}, bf16[512,1024]{1,0:T(8,128)(2,1)S(1)}, u32[]{:S(2)}, u32[]{:S(2)}) collective-permute-start(bf16[512,1024]{1,0:T(8,128)(2,1)} %refs_2_.6), channel_id=1, source_target_pairs={{0,2},{1,3},{2,0},{3,1},{4,6},{5,7},{6,4},{7,5},{8,10},{9,11},{10,... | collective-permute-start | bytes 3145736 | tf_op jit(solution)/shard_map/ppermute | solution.py:225
  6.1 5.2 %collective-permute-start = (bf16[512,128]{1,0:T(8,128)(2,1)}, bf16[512,128]{1,0:T(8,128)(2,1)S(1)}, u32[]{:S(2)}, u32[]{:S(2)}) collective-permute-start(bf16[512,128]{1,0:T(8,128)(2,1)} %get-tuple-element.49.refs_0_), channel_id=1, source_target_pairs={{0,4},{4,0},{8,12},{12,8},{16,20},{20,16},{24,28},{28,24},{1,5},{5... | collective-permute-start | bytes 393224 | tf_op jit(solution)/shard_map/ppermute | solution.py:225
  11.3 15.0 %collective-permute-start.4 = (bf16[512,512]{1,0:T(8,128)(2,1)}, bf16[512,512]{1,0:T(8,128)(2,1)}, u32[]{:S(2)}, u32[]{:S(2)}) collective-permute-start(bf16[512,512]{1,0:T(8,128)(2,1)} %get-tuple-element.54), channel_id=1, source_target_pairs={{0,4},{4,0},{8,12},{12,8},{16,20},{20,16},{24,28},{28,24},{1,5},{5... | collective-permute-start | bytes 1572872 | tf_op jit(solution)/shard_map/ppermute | solution.py:225
  12.9 0.9 %copy-start.19 = (bf16[512,128]{1,0:T(8,128)(2,1)S(1)}, bf16[512,128]{1,0:T(8,128)(2,1)}, u32[]{:S(2)}) copy-start(bf16[512,128]{1,0:T(8,128)(2,1)} %get-tuple-element.49.refs_0_) | copy-start | bytes 393220
  13.8 5.0 %collective-permute-start.1 = (bf16[512,128]{1,0:T(8,128)(2,1)S(1)}, bf16[512,128]{1,0:T(8,128)(2,1)S(1)}, u32[]{:S(2)}, u32[]{:S(2)}) collective-permute-start(bf16[512,128]{1,0:T(8,128)(2,1)S(1)} %shard_map.85.refs_0_), channel_id=1, source_target_pairs={{0,8},{4,12},{8,0},{12,4},{16,24},{20,28},{24,16},{28,20},{1,9},{5... | collective-permute-start | bytes 393224 | tf_op jit(solution)/shard_map/ppermute | solution.py:225
  18.9 7.4 %collective-permute-start.2 = (bf16[512,128]{1,0:T(8,128)(2,1)S(1)}, bf16[512,128]{1,0:T(8,128)(2,1)S(1)}, u32[]{:S(2)}, u32[]{:S(2)}) collective-permute-start(bf16[512,128]{1,0:T(8,128)(2,1)S(1)} %shard_map.86), channel_id=1, source_target_pairs={{0,16},{4,20},{8,24},{12,28},{16,0},{20,4},{24,8},{28,12},{1,17},{... | collective-permute-start | bytes 393224 | tf_op jit(solution)/shard_map/ppermute | solution.py:225
  21.5 1.0 %copy-start.1 = (bf16[512,512]{1,0:T(8,128)(2,1)S(1)}, bf16[512,512]{1,0:T(8,128)(2,1)}, u32[]{:S(2)}) copy-start(bf16[512,512]{1,0:T(8,128)(2,1)} %refs_0_.8) | copy-start | bytes 1572868
  22.6 1.0 %copy-start.3 = (bf16[512,512]{1,0:T(8,128)(2,1)S(1)}, bf16[512,512]{1,0:T(8,128)(2,1)}, u32[]{:S(2)}) copy-start(bf16[512,512]{1,0:T(8,128)(2,1)} %refs_1_.11) | copy-start | bytes 1572868
  23.6 1.0 %copy-start.5 = (bf16[512,512]{1,0:T(8,128)(2,1)S(1)}, bf16[512,512]{1,0:T(8,128)(2,1)}, u32[]{:S(2)}) copy-start(bf16[512,512]{1,0:T(8,128)(2,1)} %refs_2_.7) | copy-start | bytes 1572868
  24.7 7.4 %copy-start.7 = (bf16[4096,512]{1,0:T(8,128)(2,1)S(1)}, bf16[4096,512]{1,0:T(8,128)(2,1)}, u32[]{:S(2)}) copy-start(bf16[4096,512]{1,0:T(8,128)(2,1)} %refs_0_.6) | copy-start | bytes 12582916
  27.0 8.2 %copy-start.8 = (bf16[512,1024]{1,0:T(8,128)(2,1)}, bf16[512,1024]{1,0:T(8,128)(2,1)S(1)}, u32[]{:S(2)}) copy-start(bf16[512,1024]{1,0:T(8,128)(2,1)S(1)} %collective-permute-done.3.refs_3_.refs_4_) | copy-start | bytes 3145732
  27.8 7.5 %copy-start.12 = (bf16[512,512]{1,0:T(8,128)(2,1)}, bf16[512,512]{1,0:T(8,128)(2,1)S(1)}, u32[]{:S(2)}) copy-start(bf16[512,512]{1,0:T(8,128)(2,1)S(1)} %shard_map.88.refs_0_) | copy-start | bytes 1572868
  27.8 3.8 %collective-permute-start.5 = (bf16[512,1024]{1,0:T(8,128)(2,1)S(1)}, bf16[512,1024]{1,0:T(8,128)(2,1)S(1)}, u32[]{:S(2)}, u32[]{:S(2)}) collective-permute-start(bf16[512,1024]{1,0:T(8,128)(2,1)S(1)} %copy-done), channel_id=1, source_target_pairs={{0,1},{1,0},{2,3},{3,2},{4,5},{5,4},{6,7},{7,6},{8,9},{9,8},{10,11... | collective-permute-start | bytes 3145736 | tf_op jit(solution)/shard_map/ppermute | solution.py:225
  27.9 4.1 %collective-permute-start.6 = (bf16[512,1024]{1,0:T(8,128)(2,1)S(1)}, bf16[512,1024]{1,0:T(8,128)(2,1)S(1)}, u32[]{:S(2)}, u32[]{:S(2)}) collective-permute-start(bf16[512,1024]{1,0:T(8,128)(2,1)S(1)} %collective-permute-done.3.refs_3_.refs_4_), channel_id=1, source_target_pairs={{0,1},{1,0},{2,3},{3,2},{4,5},{5,4},{6,7},{7,6},{8,9},{9,8},{10,11... | collective-permute-start | bytes 3145736 | tf_op jit(solution)/shard_map/ppermute | solution.py:225
  28.4 14.0 %collective-permute-start.8 = (bf16[512,512]{1,0:T(8,128)(2,1)S(1)}, bf16[512,512]{1,0:T(8,128)(2,1)}, u32[]{:S(2)}, u32[]{:S(2)}) collective-permute-start(bf16[512,512]{1,0:T(8,128)(2,1)S(1)} %shard_map.88.refs_0_), channel_id=1, source_target_pairs={{0,4},{4,0},{8,12},{12,8},{16,20},{20,16},{24,28},{28,24},{1,5},{5... | collective-permute-start | bytes 1572872 | tf_op jit(solution)/shard_map/ppermute | solution.py:225
  30.1 13.9 %collective-permute-start.9 = (bf16[512,512]{1,0:T(8,128)(2,1)}, bf16[512,512]{1,0:T(8,128)(2,1)}, u32[]{:S(2)}, u32[]{:S(2)}) collective-permute-start(bf16[512,512]{1,0:T(8,128)(2,1)} %collective-permute-done.4.refs_1_.refs_6_), channel_id=1, source_target_pairs={{0,2},{1,3},{2,0},{3,1},{4,6},{5,7},{6,4},{7,5},{8,10},{9,11},{10,... | collective-permute-start | bytes 1572872 | tf_op jit(solution)/shard_map/ppermute | solution.py:225
  31.6 3.6 %copy-start.9 = (bf16[512,1024]{1,0:T(8,128)(2,1)}, bf16[512,1024]{1,0:T(8,128)(2,1)S(1)}, u32[]{:S(2)}) copy-start(bf16[512,1024]{1,0:T(8,128)(2,1)S(1)} %collective-permute-done.5.refs_2_.refs_3_) | copy-start | bytes 3145732
  32.0 3.3 %copy-start.10 = (bf16[512,1024]{1,0:T(8,128)(2,1)}, bf16[512,1024]{1,0:T(8,128)(2,1)S(1)}, u32[]{:S(2)}) copy-start(bf16[512,1024]{1,0:T(8,128)(2,1)S(1)} %collective-permute-done.6.refs_4_.refs_5_) | copy-start | bytes 3145732
  35.7 8.3 %collective-permute-start.7 = (bf16[512,128]{1,0:T(8,128)(2,1)S(1)}, bf16[512,128]{1,0:T(8,128)(2,1)S(1)}, u32[]{:S(2)}, u32[]{:S(2)}) collective-permute-start(bf16[512,128]{1,0:T(8,128)(2,1)S(1)} %shard_map.90.refs_0_), channel_id=1, source_target_pairs={{0,8},{4,12},{8,0},{12,4},{16,24},{20,28},{24,16},{28,20},{1,9},{5... | collective-permute-start | bytes 393224 | tf_op jit(solution)/shard_map/ppermute | solution.py:225
  37.6 9.1 %collective-permute-start.11 = (bf16[512,512]{1,0:T(8,128)(2,1)}, bf16[512,512]{1,0:T(8,128)(2,1)S(1)}, u32[]{:S(2)}, u32[]{:S(2)}) collective-permute-start(bf16[512,512]{1,0:T(8,128)(2,1)} %collective-permute-done.4.refs_1_.refs_6_), channel_id=1, source_target_pairs={{0,1},{1,0},{2,3},{3,2},{4,5},{5,4},{6,7},{7,6},{8,9},{9,8},{10,11... | collective-permute-start | bytes 1572872 | tf_op jit(solution)/shard_map/ppermute | solution.py:225
  44.1 2.7 %collective-permute-start.12 = (bf16[512,512]{1,0:T(8,128)(2,1)}, bf16[512,512]{1,0:T(8,128)(2,1)S(1)}, u32[]{:S(2)}, u32[]{:S(2)}) collective-permute-start(bf16[512,512]{1,0:T(8,128)(2,1)} %collective-permute-done.9.refs_3_.refs_8_), channel_id=1, source_target_pairs={{0,1},{1,0},{2,3},{3,2},{4,5},{5,4},{6,7},{7,6},{8,9},{9,8},{10,11... | collective-permute-start | bytes 1572872 | tf_op jit(solution)/shard_map/ppermute | solution.py:225
  44.1 9.7 %collective-permute-start.10 = (bf16[512,128]{1,0:T(8,128)(2,1)S(1)}, bf16[512,128]{1,0:T(8,128)(2,1)S(1)}, u32[]{:S(2)}, u32[]{:S(2)}) collective-permute-start(bf16[512,128]{1,0:T(8,128)(2,1)S(1)} %shard_map.92), channel_id=1, source_target_pairs={{0,16},{4,20},{8,24},{12,28},{16,0},{20,4},{24,8},{28,12},{1,17},{... | collective-permute-start | bytes 393224 | tf_op jit(solution)/shard_map/ppermute | solution.py:225
  46.8 7.6 %copy-start.14 = (bf16[512,512]{1,0:T(8,128)(2,1)}, bf16[512,512]{1,0:T(8,128)(2,1)S(1)}, u32[]{:S(2)}) copy-start(bf16[512,512]{1,0:T(8,128)(2,1)S(1)} %collective-permute-done.11.refs_2_.refs_7_) | copy-start | bytes 1572868
  46.8 1.4 %copy-start.11 = (f32[512,512]{1,0:T(8,128)S(1)}, f32[512,512]{1,0:T(8,128)}, u32[]{:S(2)}) copy-start(f32[512,512]{1,0:T(8,128)} %shard_map.91.refs_5_) | copy-start | bytes 3145732
  48.2 6.2 %copy-start.15 = (bf16[512,512]{1,0:T(8,128)(2,1)}, bf16[512,512]{1,0:T(8,128)(2,1)S(1)}, u32[]{:S(2)}) copy-start(bf16[512,512]{1,0:T(8,128)(2,1)S(1)} %collective-permute-done.12.refs_4_.refs_9_) | copy-start | bytes 1572868
  50.0 10.2 %collective-permute-start.15 = (bf16[512,256]{1,0:T(8,128)(2,1)S(1)}, bf16[512,256]{1,0:T(8,128)(2,1)S(1)}, u32[]{:S(2)}, u32[]{:S(2)}) collective-permute-start(bf16[512,256]{1,0:T(8,128)(2,1)S(1)} %get-tuple-element.79.refs_0_), channel_id=1, source_target_pairs={{0,8},{4,12},{8,0},{12,4},{16,24},{20,28},{24,16},{28,20},{1,9},{5... | collective-permute-start | bytes 786440 | tf_op jit(solution)/shard_map/ppermute | solution.py:287
  51.6 13.3 %collective-permute-start.13 = (bf16[512,256]{1,0:T(8,128)(2,1)S(1)}, bf16[512,256]{1,0:T(8,128)(2,1)S(1)}, u32[]{:S(2)}, u32[]{:S(2)}) collective-permute-start(bf16[512,256]{1,0:T(8,128)(2,1)S(1)} %get-tuple-element.72.refs_0_), channel_id=1, source_target_pairs={{0,8},{4,12},{8,0},{12,4},{16,24},{20,28},{24,16},{28,20},{1,9},{5... | collective-permute-start | bytes 786440 | tf_op jit(solution)/shard_map/ppermute | solution.py:287
  53.9 6.3 %collective-permute-start.16 = (bf16[512,128]{1,0:T(8,128)(2,1)S(1)}, bf16[512,128]{1,0:T(8,128)(2,1)S(1)}, u32[]{:S(2)}, u32[]{:S(2)}) collective-permute-start(bf16[512,128]{1,0:T(8,128)(2,1)S(1)} %add_convert_fusion.1), channel_id=1, source_target_pairs={{0,4},{4,0},{8,12},{12,8},{16,20},{20,16},{24,28},{28,24},{1,5},{5... | collective-permute-start | bytes 393224 | tf_op jit(solution)/shard_map/ppermute | solution.py:225
  59.3 6.5 %copy-start.18 = (bf16[512,256]{1,0:T(8,128)(2,1)S(1)}, bf16[512,256]{1,0:T(8,128)(2,1)}, u32[]{:S(2)}) copy-start(bf16[512,256]{1,0:T(8,128)(2,1)} %get-tuple-element.90.refs_0_) | copy-start | bytes 786436
  59.3 11.2 %copy-start.20 = (bf16[512,256]{1,0:T(8,128)(2,1)S(1)}, bf16[512,256]{1,0:T(8,128)(2,1)}, u32[]{:S(2)}) copy-start(bf16[512,256]{1,0:T(8,128)(2,1)} %get-tuple-element.78.refs_0_) | copy-start | bytes 786436
  59.3 11.2 %collective-permute-start.17 = (bf16[512,256]{1,0:T(8,128)(2,1)}, bf16[512,256]{1,0:T(8,128)(2,1)S(1)}, u32[]{:S(2)}, u32[]{:S(2)}) collective-permute-start(bf16[512,256]{1,0:T(8,128)(2,1)} %get-tuple-element.78.refs_0_), channel_id=1, source_target_pairs={{0,8},{4,12},{8,0},{12,4},{16,24},{20,28},{24,16},{28,20},{1,9},{5... | collective-permute-start | bytes 786440 | tf_op jit(solution)/shard_map/ppermute | solution.py:287
  60.2 10.3 %collective-permute-start.18 = (bf16[512,256]{1,0:T(8,128)(2,1)S(1)}, bf16[512,256]{1,0:T(8,128)(2,1)S(1)}, u32[]{:S(2)}, u32[]{:S(2)}) collective-permute-start(bf16[512,256]{1,0:T(8,128)(2,1)S(1)} %shard_map.96), channel_id=1, source_target_pairs={{8,16},{12,20},{16,8},{20,12},{9,17},{13,21},{17,9},{21,13},{10,18... | collective-permute-start | bytes 786440 | tf_op jit(solution)/shard_map/ppermute | solution.py:287
  65.0 6.5 %copy-start.17 = (f32[512,256]{1,0:T(8,128)S(1)}, f32[512,256]{1,0:T(8,128)}, u32[]{:S(2)}) copy-start(f32[512,256]{1,0:T(8,128)} %get-tuple-element.87.refs_0_) | copy-start | bytes 1572868
  65.0 12.6 %copy-start.16 = (f32[512,256]{1,0:T(8,128)S(1)}, f32[512,256]{1,0:T(8,128)}, u32[]{:S(2)}) copy-start(f32[512,256]{1,0:T(8,128)} %get-tuple-element.91.refs_0_) | copy-start | bytes 1572868
  65.0 14.6 %copy-start.4 = (bf16[512,512]{1,0:T(8,128)(2,1)S(1)}, bf16[512,512]{1,0:T(8,128)(2,1)}, u32[]{:S(2)}) copy-start(bf16[512,512]{1,0:T(8,128)(2,1)} %refs_1_.11) | copy-start | bytes 1572868
  65.0 14.6 %copy-start.6 = (bf16[512,512]{1,0:T(8,128)(2,1)S(1)}, bf16[512,512]{1,0:T(8,128)(2,1)}, u32[]{:S(2)}) copy-start(bf16[512,512]{1,0:T(8,128)(2,1)} %refs_2_.7) | copy-start | bytes 1572868
  65.0 12.6 %collective-permute-start.14 = (bf16[512,256]{1,0:T(8,128)(2,1)S(1)}, bf16[512,256]{1,0:T(8,128)(2,1)S(1)}, u32[]{:S(2)}, u32[]{:S(2)}) collective-permute-start(bf16[512,256]{1,0:T(8,128)(2,1)S(1)} %shard_map.94), channel_id=1, source_target_pairs={{8,16},{12,20},{16,8},{20,12},{9,17},{13,21},{17,9},{21,13},{10,18... | collective-permute-start | bytes 786440 | tf_op jit(solution)/shard_map/ppermute | solution.py:287
  65.9 12.8 %collective-permute-start.21 = (bf16[512,256]{1,0:T(8,128)(2,1)S(1)}, bf16[512,256]{1,0:T(8,128)(2,1)S(1)}, u32[]{:S(2)}, u32[]{:S(2)}) collective-permute-start(bf16[512,256]{1,0:T(8,128)(2,1)S(1)} %copy-done.18), channel_id=1, source_target_pairs={{0,8},{4,12},{8,0},{12,4},{16,24},{20,28},{24,16},{28,20},{1,9},{5... | collective-permute-start | bytes 786440 | tf_op jit(solution)/shard_map/ppermute | solution.py:287
  70.6 14.1 %copy-start.21 = (f32[512,256]{1,0:T(8,128)S(1)}, f32[512,256]{1,0:T(8,128)}, u32[]{:S(2)}) copy-start(f32[512,256]{1,0:T(8,128)} %get-tuple-element.86.refs_0_) | copy-start | bytes 1572868
  70.6 14.1 %collective-permute-start.19 = (bf16[512,256]{1,0:T(8,128)(2,1)S(1)}, bf16[512,256]{1,0:T(8,128)(2,1)S(1)}, u32[]{:S(2)}, u32[]{:S(2)}) collective-permute-start(bf16[512,256]{1,0:T(8,128)(2,1)S(1)} %shard_map.97), channel_id=1, source_target_pairs={{8,16},{12,20},{16,8},{20,12},{9,17},{13,21},{17,9},{21,13},{10,18... | collective-permute-start | bytes 786440 | tf_op jit(solution)/shard_map/ppermute | solution.py:287
  71.5 13.2 %collective-permute-start.20 = (bf16[512,256]{1,0:T(8,128)(2,1)S(1)}, bf16[512,256]{1,0:T(8,128)(2,1)S(1)}, u32[]{:S(2)}, u32[]{:S(2)}) collective-permute-start(bf16[512,256]{1,0:T(8,128)(2,1)S(1)} %shard_map.99), channel_id=1, source_target_pairs={{0,8},{4,12},{8,0},{12,4},{16,24},{20,28},{24,16},{28,20},{1,9},{5... | collective-permute-start | bytes 786440 | tf_op jit(solution)/shard_map/ppermute | solution.py:287
  77.7 9.8 %collective-permute-start.23 = (bf16[512,256]{1,0:T(8,128)(2,1)S(1)}, bf16[512,256]{1,0:T(8,128)(2,1)S(1)}, u32[]{:S(2)}, u32[]{:S(2)}) collective-permute-start(bf16[512,256]{1,0:T(8,128)(2,1)S(1)} %shard_map.101), channel_id=1, source_target_pairs={{0,8},{4,12},{8,0},{12,4},{16,24},{20,28},{24,16},{28,20},{1,9},{5... | collective-permute-start | bytes 786440 | tf_op jit(solution)/shard_map/ppermute | solution.py:287
  78.7 6.1 %collective-permute-start.22 = (bf16[512,256]{1,0:T(8,128)(2,1)S(1)}, bf16[512,256]{1,0:T(8,128)(2,1)S(1)}, u32[]{:S(2)}, u32[]{:S(2)}) collective-permute-start(bf16[512,256]{1,0:T(8,128)(2,1)S(1)} %shard_map.102), channel_id=1, source_target_pairs={{8,16},{12,20},{16,8},{20,12},{9,17},{13,21},{17,9},{21,13},{10,18... | collective-permute-start | bytes 786440 | tf_op jit(solution)/shard_map/ppermute | solution.py:287
  84.7 2.8 %copy-start.13 = (f32[512,256]{1,0:T(8,128)S(1)}, f32[512,256]{1,0:T(8,128)}, u32[]{:S(2)}) copy-start(f32[512,256]{1,0:T(8,128)} %get-tuple-element.89.back_ref) | copy-start | bytes 1572868

commit v6 on v5

--- a/solution.py
+++ b/solution.py
@@ -242,10 +242,31 @@
     )(*terms)
 
 
-def total_body(front_ref, back_ref, m_ref, e_ref, out_ref):
-    width = front_ref.shape[1]
-    out_ref[:, :width] = front_ref[...]
-    out_ref[:, width:] = back_ref[...] + m_ref[...].astype(F32) + e_ref[...].astype(F32)
+def half_body(first, *refs):
+    *sources, out_ref, sum_ref, sem = refs
+    sources = sources[-3:]
+    sum_ref[...] = sum(ref[...].astype(F32) for ref in sources)
+    columns = out_ref.at[:, pl.ds(first, sum_ref.shape[1])]
+    copy = pltpu.make_async_copy(sum_ref, columns, sem)
+    copy.start()
+    copy.wait()
+
+
+def half_sum(first, width, out, *terms, cost=1):
+    rows, part = terms[0].shape
+    spec = pl.BlockSpec(memory_space=pltpu.VMEM)
+    whole = pl.BlockSpec(memory_space=pl.ANY)
+    operands = terms if out is None else (out, *terms)
+    return pl.pallas_call(
+        functools.partial(half_body, first),
+        out_shape=jax.ShapeDtypeStruct((rows, width), F32),
+        in_specs=([] if out is None else [whole]) + [spec] * len(terms),
+        out_specs=whole,
+        scratch_shapes=[pltpu.VMEM((rows, part), F32), pltpu.SemaphoreType.DMA],
+        input_output_aliases={} if out is None else {0: 0},
+        compiler_params=pltpu.CompilerParams(vmem_limit_bytes=8 << 20),
+        cost_estimate=pl.CostEstimate(flops=cost << 20, bytes_accessed=1 << 14, transcendentals=0),
+    )(*operands)
 
 
 def small(body, kind, *terms, wide=1):
@@ -336,6 +357,7 @@
     got = prior.start(1)
     got, other, q, grad = phase(got, other, queries, out_grad)
     near = flip(other, "seq", 1)
+    by_core = flip(grad, "head", 1)
     prior.take(1, got)
     for bit in prior.bits[1:]:
         got = prior.start(bit)
@@ -346,10 +368,10 @@
     prior = prior.result()
 
     (o,) = call(outputs, [matrix], prior, queries, pv)
-    o, by_x, near, grad = phase(o, by_x, near, grad)
+    o, by_x, near = phase(o, by_x, near)
     n = flip(o, "seq", 1)
     far = flip(near, "head", 2)
-    by_core, by_xc, near_c = (flip(a, "head", 1) for a in (grad, by_x, near))
+    by_xc = flip(by_x, "head", 1)
 
     pieces = [out_grad, by_core, by_x, by_xc]
     mine = pieces if short else [half(p, y) for p in pieces]
@@ -361,10 +383,12 @@
         first = functools.partial(first_body, factor, n_head)
         scratch = [((rows, cols // 2), BF16), ((rows, width), BF16)]
         outs = [shaped((cols // 2, width), F32)]
-        o, _ = phase(o, back_term)
+        o, near, back_term = phase(o, near, back_term)
+        near_c = flip(near, "head", 1)
         (begun,) = call(functools.partial(first, True), outs, o, *mine, scratch=scratch, vmem=60)
         got, n, far, begun = phase(got, n, far, begun)
     else:
+        near_c = flip(near, "head", 1)
         got, n, far = phase(got, n, far)
     far_c = flip(far, "head", 1)
     later.take(2, got)
@@ -401,8 +425,8 @@
         e2[1], _, _ = phase(e2[1], *parts)
         m3 += [send(add(b1[1], e2[1]), MIDDLE)]
         grads = gradients(later.result(got))
-        front = add(b3, m3[0], e3[0], kind=F32, cost=2048)
-        weight_grad = small(total_body, F32, front, b3_back, m3[1], e3[1], wide=2)
+        weight_grad = half_sum(0, width, None, b3, m3[0], e3[0], cost=2048)
+        weight_grad = half_sum(width // 2, width, weight_grad, b3_back, m3[1], e3[1])
     else:
         for bit in later.bits[1:]:
             later.take(bit, later.start(bit))

time: 89.1 us -> 89 us (level)
  transfers between devices with their start and end apart: 24 -> 24, of which waited for: 10 -> 9; matrix products, arithmetic and copies ran while one was open for 0% -> 0% of each run, Pallas kernels for 26% -> 27%
where the time goes in v6:
time: 89 us; the launch traced here: 88.5 us
  starting transfers between devices  35.9 us (40%)
  Pallas kernels  25 us (28%)
  waiting for transfers between devices  20.6 us (23%)
  local copies, waits for them, and re-layouts  5.51 us (6%)
  between operations  1.23 us (1%)
    pallas_call x9, Pallas kernels, call(): pl.pallas_call(kernel, out_shape=outs, in_specs=[pl.BlockSpec(memory_spac...  22.8 us
    ppermute x14, starting transfers between devices, flip(): lax.ppermute(a, axis, [(i, i ^ bit) for i in range(lax.axis_size(axis))])  18.6 us
    ppermute x10, starting transfers between devices, send(): lax.ppermute(a, 'seq', [(2 * s + i, 2 * t + i) for s, t in pairs for i in...  17.3 us
    ppermute x14, waiting for transfers between devices, flip(): lax.ppermute(a, axis, [(i, i ^ bit) for i in range(lax.axis_size(axis))])  14.2 us
    ppermute x10, waiting for transfers between devices, send(): lax.ppermute(a, 'seq', [(2 * s + i, 2 * t + i) for s, t in pairs for i in...  6.37 us
    unnamed x44, local copies, waits for them, and re-layouts  5.51 us
  transfers between devices with their start and end apart: 24, of which 9 were waited for; matrix products, arithmetic and copies ran while one was open for 0% of the time, Pallas kernels for 27%

profile of v6, /device:TPU:0, one launch (start us, length us, event | category | flops | bytes accessed | tf_op | source)
XLA Modules:
  0.0 88.5 jit_solution(14108176311046227771)
XLA Ops:
  0.7 3.0 %collective-permute-start.4 = (bf16[512,1024]{1,0:T(8,128)(2,1)}, bf16[512,1024]{1,0:T(8,128)(2,1)S(1)}, u32[]{:S(2)}, u32[]{:S(2)}) collective-permute-start(bf16[512,1024]{1,0:T(8,128)(2,1)} %refs_2_.6), channel_id=1, source_target_pairs={{0,2},{1,3},{2,0},{3,1},{4,6},{5,7},{6,4},{7,5},{8,10},{9,11},{10,... | collective-permute-start | bytes 3145736 | tf_op jit(solution)/shard_map/ppermute | solution.py:225
  3.7 2.4 %shard_map.84 = (bf16[512,128]{1,0:T(8,128)(2,1)}, bf16[512,512]{1,0:T(8,128)(2,1)}) custom-call(bf16[512,512]{1,0:T(8,128)(2,1)} %refs_1_.11, bf16[512,512]{1,0:T(8,128)(2,1)} %refs_2_.7, bf16[512,1024]{1,0:T(8,128)(2,1)} %refs_2_.6), custom_call_target="tpu_custom_call" | custom-call | flops 1048576 | bytes 16384 | tf_op jit(solution)/shard_map/pallas_call | solution.py:29
  6.1 1.6 %collective-permute-start = (bf16[512,128]{1,0:T(8,128)(2,1)}, bf16[512,128]{1,0:T(8,128)(2,1)S(1)}, u32[]{:S(2)}, u32[]{:S(2)}) collective-permute-start(bf16[512,128]{1,0:T(8,128)(2,1)} %get-tuple-element.48.refs_0_), channel_id=1, source_target_pairs={{0,4},{4,0},{8,12},{12,8},{16,20},{20,16},{24,28},{28,24},{1,5},{5... | collective-permute-start | bytes 393224 | tf_op jit(solution)/shard_map/ppermute | solution.py:225
  7.7 3.7 %collective-permute-done.refs_1_ = bf16[512,128]{1,0:T(8,128)(2,1)S(1)} collective-permute-done((bf16[512,128]{1,0:T(8,128)(2,1)}, bf16[512,128]{1,0:T(8,128)(2,1)S(1)}, u32[]{:S(2)}, u32[]{:S(2)}) %collective-permute-start) | collective-permute-done | bytes 131104 | tf_op jit(solution)/shard_map/ppermute | solution.py:225
  11.3 1.5 %collective-permute-start.5 = (bf16[512,512]{1,0:T(8,128)(2,1)}, bf16[512,512]{1,0:T(8,128)(2,1)}, u32[]{:S(2)}, u32[]{:S(2)}) collective-permute-start(bf16[512,512]{1,0:T(8,128)(2,1)} %get-tuple-element.53), channel_id=1, source_target_pairs={{0,4},{4,0},{8,12},{12,8},{16,20},{20,16},{24,28},{28,24},{1,5},{5... | collective-permute-start | bytes 1572872 | tf_op jit(solution)/shard_map/ppermute | solution.py:225
  12.9 0.9 %copy-done.19 = bf16[512,128]{1,0:T(8,128)(2,1)S(1)} copy-done((bf16[512,128]{1,0:T(8,128)(2,1)S(1)}, bf16[512,128]{1,0:T(8,128)(2,1)}, u32[]{:S(2)}) %copy-start.19) | copy-done | bytes 131096
  13.8 1.6 %collective-permute-start.2 = (bf16[512,128]{1,0:T(8,128)(2,1)S(1)}, bf16[512,128]{1,0:T(8,128)(2,1)S(1)}, u32[]{:S(2)}, u32[]{:S(2)}) collective-permute-start(bf16[512,128]{1,0:T(8,128)(2,1)S(1)} %shard_map.85.refs_0_), channel_id=1, source_target_pairs={{0,8},{4,12},{8,0},{12,4},{16,24},{20,28},{24,16},{28,20},{1,9},{5... | collective-permute-start | bytes 393224 | tf_op jit(solution)/shard_map/ppermute | solution.py:225
  15.4 3.4 %collective-permute-done.2.refs_1_ = bf16[512,128]{1,0:T(8,128)(2,1)S(1)} collective-permute-done((bf16[512,128]{1,0:T(8,128)(2,1)S(1)}, bf16[512,128]{1,0:T(8,128)(2,1)S(1)}, u32[]{:S(2)}, u32[]{:S(2)}) %collective-permute-start.2) | collective-permute-done | bytes 131104 | tf_op jit(solution)/shard_map/ppermute | solution.py:225
  18.9 2.7 %collective-permute-start.3 = (bf16[512,128]{1,0:T(8,128)(2,1)S(1)}, bf16[512,128]{1,0:T(8,128)(2,1)S(1)}, u32[]{:S(2)}, u32[]{:S(2)}) collective-permute-start(bf16[512,128]{1,0:T(8,128)(2,1)S(1)} %shard_map.86), channel_id=1, source_target_pairs={{0,16},{4,20},{8,24},{12,28},{16,0},{20,4},{24,8},{28,12},{1,17},{... | collective-permute-start | bytes 393224 | tf_op jit(solution)/shard_map/ppermute | solution.py:225
  21.5 1.0 %copy-done.1 = bf16[512,512]{1,0:T(8,128)(2,1)S(1)} copy-done((bf16[512,512]{1,0:T(8,128)(2,1)S(1)}, bf16[512,512]{1,0:T(8,128)(2,1)}, u32[]{:S(2)}) %copy-start.1) | copy-done | bytes 524312
  22.6 1.0 %copy-done.3 = bf16[512,512]{1,0:T(8,128)(2,1)S(1)} copy-done((bf16[512,512]{1,0:T(8,128)(2,1)S(1)}, bf16[512,512]{1,0:T(8,128)(2,1)}, u32[]{:S(2)}) %copy-start.3) | copy-done | bytes 524312
  23.6 1.0 %copy-done.5 = bf16[512,512]{1,0:T(8,128)(2,1)S(1)} copy-done((bf16[512,512]{1,0:T(8,128)(2,1)S(1)}, bf16[512,512]{1,0:T(8,128)(2,1)}, u32[]{:S(2)}) %copy-start.5) | copy-done | bytes 524312
  24.7 1.6 %shard_map.87.refs_2_ = f32[512,512]{1,0:T(8,128)S(1)} custom-call(bf16[512,512]{1,0:T(8,128)(2,1)S(1)} %copy-done.1, bf16[512,512]{1,0:T(8,128)(2,1)S(1)} %copy-done.3, bf16[512,512]{1,0:T(8,128)(2,1)S(1)} %copy-done.5), custom_call_target="tpu_custom_call" | custom-call | flops 1048576 | bytes 16384 | tf_op jit(solution)/shard_map/pallas_call | solution.py:29
  26.3 0.7 collective-permute-done.4.refs_3_.refs_4_
  27.0 0.1 add_convert_fusion.2.refs_0_.refs_4_
  27.1 0.6 shard_map.88.refs_0_
  27.8 1.8 %collective-permute-start.8 = (bf16[512,512]{1,0:T(8,128)(2,1)S(1)}, bf16[512,512]{1,0:T(8,128)(2,1)}, u32[]{:S(2)}, u32[]{:S(2)}) collective-permute-start(bf16[512,512]{1,0:T(8,128)(2,1)S(1)} %shard_map.88.refs_0_), channel_id=1, source_target_pairs={{0,4},{4,0},{8,12},{12,8},{16,20},{20,16},{24,28},{28,24},{1,5},{5... | collective-permute-start | bytes 1572872 | tf_op jit(solution)/shard_map/ppermute | solution.py:225
  29.7 1.5 %collective-permute-start.9 = (bf16[512,512]{1,0:T(8,128)(2,1)}, bf16[512,512]{1,0:T(8,128)(2,1)}, u32[]{:S(2)}, u32[]{:S(2)}) collective-permute-start(bf16[512,512]{1,0:T(8,128)(2,1)} %collective-permute-done.5.refs_1_.refs_6_), channel_id=1, source_target_pairs={{0,2},{1,3},{2,0},{3,1},{4,6},{5,7},{6,4},{7,5},{8,10},{9,11},{10,... | collective-permute-start | bytes 1572872 | tf_op jit(solution)/shard_map/ppermute | solution.py:225
  31.2 3.2 %shard_map.89.refs_1_.refs_3_ = bf16[512,512]{1,0:T(8,128)(2,1)S(1)} custom-call(bf16[4096,512]{1,0:T(8,128)(2,1)S(1)} %copy-done.7, bf16[512,1024]{1,0:T(8,128)(2,1)S(1)} %copy-done, bf16[512,1024]{1,0:T(8,128)(2,1)S(1)} %collective-permute-done.1.refs_2_.refs_3_, bf16[512,1024]{1,0:T(8,128)(2,1)S(1)} %collective-permute-done.4.refs_3_.refs_4_, ...), custom_call_target="tpu_custom_call" | custom-call | flops 1048576 | bytes 16384 | tf_op jit(solution)/shard_map/pallas_call | solution.py:29
  34.5 0.5 shard_map.90.refs_0_
  35.0 1.6 %collective-permute-start.7 = (bf16[512,128]{1,0:T(8,128)(2,1)S(1)}, bf16[512,128]{1,0:T(8,128)(2,1)S(1)}, u32[]{:S(2)}, u32[]{:S(2)}) collective-permute-start(bf16[512,128]{1,0:T(8,128)(2,1)S(1)} %shard_map.90.refs_0_), channel_id=1, source_target_pairs={{0,8},{4,12},{8,0},{12,4},{16,24},{20,28},{24,16},{28,20},{1,9},{5... | collective-permute-start | bytes 393224 | tf_op jit(solution)/shard_map/ppermute | solution.py:225
  36.6 2.7 %shard_map.91.refs_5_ = f32[512,512]{1,0:T(8,128)} custom-call(bf16[512,512]{1,0:T(8,128)(2,1)} %copy-done.12, bf16[512,1024]{1,0:T(8,128)(2,1)} %refs_2_.6, bf16[512,1024]{1,0:T(8,128)(2,1)} %copy-done.9, bf16[512,1024]{1,0:T(8,128)(2,1)} %copy-done.8, bf16[512,1024]{1,0:T(8,128)(2,1)} %copy-done.10), custom_call_target="tpu_custom_call" | custom-call | flops 1048576 | bytes 16384 | tf_op jit(solution)/shard_map/pallas_call | solution.py:29
  39.3 3.0 %collective-permute-done.8.refs_0_.refs_1_ = bf16[512,512]{1,0:T(8,128)(2,1)} collective-permute-done((bf16[512,512]{1,0:T(8,128)(2,1)S(1)}, bf16[512,512]{1,0:T(8,128)(2,1)}, u32[]{:S(2)}, u32[]{:S(2)}) %collective-permute-start.8) | collective-permute-done | bytes 524320 | tf_op jit(solution)/shard_map/ppermute | solution.py:225
  42.3 1.7 %collective-permute-done.9.refs_3_.refs_8_ = bf16[512,512]{1,0:T(8,128)(2,1)} collective-permute-done((bf16[512,512]{1,0:T(8,128)(2,1)}, bf16[512,512]{1,0:T(8,128)(2,1)}, u32[]{:S(2)}, u32[]{:S(2)}) %collective-permute-start.9) | collective-permute-done | bytes 524320 | tf_op jit(solution)/shard_map/ppermute | solution.py:225
  44.0 2.7 %collective-permute-start.10 = (bf16[512,128]{1,0:T(8,128)(2,1)S(1)}, bf16[512,128]{1,0:T(8,128)(2,1)S(1)}, u32[]{:S(2)}, u32[]{:S(2)}) collective-permute-start(bf16[512,128]{1,0:T(8,128)(2,1)S(1)} %shard_map.92), channel_id=1, source_target_pairs={{0,16},{4,20},{8,24},{12,28},{16,0},{20,4},{24,8},{28,12},{1,17},{... | collective-permute-start | bytes 393224 | tf_op jit(solution)/shard_map/ppermute | solution.py:225
  46.7 1.4 %copy-done.11 = f32[512,512]{1,0:T(8,128)S(1)} copy-done((f32[512,512]{1,0:T(8,128)S(1)}, f32[512,512]{1,0:T(8,128)}, u32[]{:S(2)}) %copy-start.11) | copy-done | bytes 1048600
  48.1 1.8 %shard_map.93 = (bf16[512,256]{1,0:T(8,128)(2,1)S(1)}, bf16[512,256]{1,0:T(8,128)(2,1)S(1)}) custom-call(bf16[512,512]{1,0:T(8,128)(2,1)} %collective-permute-done.8.refs_0_.refs_1_, bf16[512,512]{1,0:T(8,128)(2,1)} %collective-permute-done.5.refs_1_.refs_6_, bf16[512,512]{1,0:T(8,128)(2,1)S(1)} %collective-permute-done.11.refs_2_.refs_7_, ...), custom_call_target="tpu_custom_call" | custom-call | flops 1048576 | bytes 16384 | tf_op jit(solution)/shard_map/pallas_call | solution.py:29
  49.9 1.6 %collective-permute-start.15 = (bf16[512,256]{1,0:T(8,128)(2,1)S(1)}, bf16[512,256]{1,0:T(8,128)(2,1)S(1)}, u32[]{:S(2)}, u32[]{:S(2)}) collective-permute-start(bf16[512,256]{1,0:T(8,128)(2,1)S(1)} %get-tuple-element.77.refs_0_), channel_id=1, source_target_pairs={{0,8},{4,12},{8,0},{12,4},{16,24},{20,28},{24,16},{28,20},{1,9},{5... | collective-permute-start | bytes 786440 | tf_op jit(solution)/shard_map/ppermute | solution.py:308
  51.6 0.4 collective-permute-start.13
  52.0 1.7 %collective-permute-done.10 = bf16[512,128]{1,0:T(8,128)(2,1)S(1)} collective-permute-done((bf16[512,128]{1,0:T(8,128)(2,1)S(1)}, bf16[512,128]{1,0:T(8,128)(2,1)S(1)}, u32[]{:S(2)}, u32[]{:S(2)}) %collective-permute-start.10) | collective-permute-done | bytes 131104 | tf_op jit(solution)/shard_map/ppermute | solution.py:225
  53.7 0.1 add_convert_fusion.1
  53.8 0.5 collective-permute-start.16
  54.3 4.9 %shard_map.95 = (bf16[512,256]{1,0:T(8,128)(2,1)}, bf16[512,256]{1,0:T(8,128)(2,1)}, f32[512,256]{1,0:T(8,128)}, f32[512,256]{1,0:T(8,128)}, f32[512,256]{1,0:T(8,128)}, /*index=5*/f32[512,256]{1,0:T(8,128)}) custom-call(bf16[512,512]{1,0:T(8,128)(2,1)} %copy-done.12, bf16[512,512]{1,0:T(8,128)(2,1)} %collective-permute-done.8.refs_0_.refs_1_, ...), custom_call_target="tpu_custom_call" | custom-call | flops 17179869184 | bytes 16384 | tf_op jit(solution)/shard_map/pallas_call | solution.py:29
  59.3 0.8 collective-permute-start.17
  60.2 0.7 collective-permute-start.18
  60.9 4.0 %collective-permute-done.13.refs_1_ = bf16[512,256]{1,0:T(8,128)(2,1)S(1)} collective-permute-done((bf16[512,256]{1,0:T(8,128)(2,1)S(1)}, bf16[512,256]{1,0:T(8,128)(2,1)S(1)}, u32[]{:S(2)}, u32[]{:S(2)}) %collective-permute-start.13) | collective-permute-done | bytes 262176 | tf_op jit(solution)/shard_map/ppermute | solution.py:308
  65.0 0.8 collective-permute-start.14
  65.8 4.2 %collective-permute-start.21 = (bf16[512,256]{1,0:T(8,128)(2,1)S(1)}, bf16[512,256]{1,0:T(8,128)(2,1)S(1)}, u32[]{:S(2)}, u32[]{:S(2)}) collective-permute-start(bf16[512,256]{1,0:T(8,128)(2,1)S(1)} %copy-done.18), channel_id=1, source_target_pairs={{0,8},{4,12},{8,0},{12,4},{16,24},{20,28},{24,16},{28,20},{1,9},{5... | collective-permute-start | bytes 786440 | tf_op jit(solution)/shard_map/ppermute | solution.py:308
  70.0 0.5 collective-permute-done.17.refs_1_
  70.5 0.8 collective-permute-start.19
  71.4 6.1 %collective-permute-start.20 = (bf16[512,256]{1,0:T(8,128)(2,1)S(1)}, bf16[512,256]{1,0:T(8,128)(2,1)S(1)}, u32[]{:S(2)}, u32[]{:S(2)}) collective-permute-start(bf16[512,256]{1,0:T(8,128)(2,1)S(1)} %shard_map.99), channel_id=1, source_target_pairs={{0,8},{4,12},{8,0},{12,4},{16,24},{20,28},{24,16},{28,20},{1,9},{5... | collective-permute-start | bytes 786440 | tf_op jit(solution)/shard_map/ppermute | solution.py:308
  77.6 0.9 %collective-permute-start.23 = (bf16[512,256]{1,0:T(8,128)(2,1)S(1)}, bf16[512,256]{1,0:T(8,128)(2,1)S(1)}, u32[]{:S(2)}, u32[]{:S(2)}) collective-permute-start(bf16[512,256]{1,0:T(8,128)(2,1)S(1)} %shard_map.101), channel_id=1, source_target_pairs={{0,8},{4,12},{8,0},{12,4},{16,24},{20,28},{24,16},{28,20},{1,9},{5... | collective-permute-start | bytes 786440 | tf_op jit(solution)/shard_map/ppermute | solution.py:308
  78.6 0.9 collective-permute-start.22
  79.5 0.1 add_convert_fusion.refs_5_
  79.6 5.0 %shard_map.98 = (bf16[512,512]{1,0:T(8,128)(2,1)}, bf16[512,512]{1,0:T(8,128)(2,1)}, bf16[512,512]{1,0:T(8,128)(2,1)}) custom-call(bf16[512,512]{1,0:T(8,128)(2,1)S(1)} %copy-done.2, bf16[512,512]{1,0:T(8,128)(2,1)S(1)} %copy-done.4, bf16[512,512]{1,0:T(8,128)(2,1)S(1)} %copy-done.6, bf16[512,512]{1,0:T(8,128)(2,1)S(1)} %shard_map.89.refs_1_.refs_3_, ...), custom_call_target="tpu_custom_call" | custom-call | flops 1048576 | bytes 16384 | tf_op jit(solution)/shard_map/pallas_call | solution.py:29
  84.7 0.9 shard_map.100.refs_0_
  85.6 1.9 %collective-permute-done.23.refs_3_ = bf16[512,256]{1,0:T(8,128)(2,1)S(1)} collective-permute-done((bf16[512,256]{1,0:T(8,128)(2,1)S(1)}, bf16[512,256]{1,0:T(8,128)(2,1)S(1)}, u32[]{:S(2)}, u32[]{:S(2)}) %collective-permute-start.23) | collective-permute-done | bytes 262176 | tf_op jit(solution)/shard_map/ppermute | solution.py:308
  87.4 0.9 shard_map.103
  (67 shorter events, 0.7 us)
Async XLA Ops:
  0.6 30.6 %copy-start = (bf16[512,1024]{1,0:T(8,128)(2,1)S(1)}, bf16[512,1024]{1,0:T(8,128)(2,1)}, u32[]{:S(2)}) copy-start(bf16[512,1024]{1,0:T(8,128)(2,1)} %refs_2_.6) | copy-start | bytes 3145732
  0.6 26.5 %copy-start.2 = (bf16[512,512]{1,0:T(8,128)(2,1)S(1)}, bf16[512,512]{1,0:T(8,128)(2,1)}, u32[]{:S(2)}) copy-start(bf16[512,512]{1,0:T(8,128)(2,1)} %refs_0_.8) | copy-start | bytes 1572868
  0.7 26.4 %collective-permute-start.4 = (bf16[512,1024]{1,0:T(8,128)(2,1)}, bf16[512,1024]{1,0:T(8,128)(2,1)S(1)}, u32[]{:S(2)}, u32[]{:S(2)}) collective-permute-start(bf16[512,1024]{1,0:T(8,128)(2,1)} %refs_2_.6), channel_id=1, source_target_pairs={{0,2},{1,3},{2,0},{3,1},{4,6},{5,7},{6,4},{7,5},{8,10},{9,11},{10,... | collective-permute-start | bytes 3145736 | tf_op jit(solution)/shard_map/ppermute | solution.py:225
  6.1 5.2 %collective-permute-start = (bf16[512,128]{1,0:T(8,128)(2,1)}, bf16[512,128]{1,0:T(8,128)(2,1)S(1)}, u32[]{:S(2)}, u32[]{:S(2)}) collective-permute-start(bf16[512,128]{1,0:T(8,128)(2,1)} %get-tuple-element.48.refs_0_), channel_id=1, source_target_pairs={{0,4},{4,0},{8,12},{12,8},{16,20},{20,16},{24,28},{28,24},{1,5},{5... | collective-permute-start | bytes 393224 | tf_op jit(solution)/shard_map/ppermute | solution.py:225
  11.3 15.0 %collective-permute-start.5 = (bf16[512,512]{1,0:T(8,128)(2,1)}, bf16[512,512]{1,0:T(8,128)(2,1)}, u32[]{:S(2)}, u32[]{:S(2)}) collective-permute-start(bf16[512,512]{1,0:T(8,128)(2,1)} %get-tuple-element.53), channel_id=1, source_target_pairs={{0,4},{4,0},{8,12},{12,8},{16,20},{20,16},{24,28},{28,24},{1,5},{5... | collective-permute-start | bytes 1572872 | tf_op jit(solution)/shard_map/ppermute | solution.py:225
  12.9 0.9 %copy-start.19 = (bf16[512,128]{1,0:T(8,128)(2,1)S(1)}, bf16[512,128]{1,0:T(8,128)(2,1)}, u32[]{:S(2)}) copy-start(bf16[512,128]{1,0:T(8,128)(2,1)} %get-tuple-element.48.refs_0_) | copy-start | bytes 393220
  13.8 5.0 %collective-permute-start.2 = (bf16[512,128]{1,0:T(8,128)(2,1)S(1)}, bf16[512,128]{1,0:T(8,128)(2,1)S(1)}, u32[]{:S(2)}, u32[]{:S(2)}) collective-permute-start(bf16[512,128]{1,0:T(8,128)(2,1)S(1)} %shard_map.85.refs_0_), channel_id=1, source_target_pairs={{0,8},{4,12},{8,0},{12,4},{16,24},{20,28},{24,16},{28,20},{1,9},{5... | collective-permute-start | bytes 393224 | tf_op jit(solution)/shard_map/ppermute | solution.py:225
  18.9 7.4 %collective-permute-start.3 = (bf16[512,128]{1,0:T(8,128)(2,1)S(1)}, bf16[512,128]{1,0:T(8,128)(2,1)S(1)}, u32[]{:S(2)}, u32[]{:S(2)}) collective-permute-start(bf16[512,128]{1,0:T(8,128)(2,1)S(1)} %shard_map.86), channel_id=1, source_target_pairs={{0,16},{4,20},{8,24},{12,28},{16,0},{20,4},{24,8},{28,12},{1,17},{... | collective-permute-start | bytes 393224 | tf_op jit(solution)/shard_map/ppermute | solution.py:225
  21.5 9.6 %collective-permute-start.1 = (bf16[512,1024]{1,0:T(8,128)(2,1)}, bf16[512,1024]{1,0:T(8,128)(2,1)S(1)}, u32[]{:S(2)}, u32[]{:S(2)}) collective-permute-start(bf16[512,1024]{1,0:T(8,128)(2,1)} %refs_2_.6), channel_id=1, source_target_pairs={{0,1},{1,0},{2,3},{3,2},{4,5},{5,4},{6,7},{7,6},{8,9},{9,8},{10,11... | collective-permute-start | bytes 3145736 | tf_op jit(solution)/shard_map/ppermute | solution.py:225
  21.5 1.0 %copy-start.1 = (bf16[512,512]{1,0:T(8,128)(2,1)S(1)}, bf16[512,512]{1,0:T(8,128)(2,1)}, u32[]{:S(2)}) copy-start(bf16[512,512]{1,0:T(8,128)(2,1)} %refs_0_.8) | copy-start | bytes 1572868
  22.6 1.0 %copy-start.3 = (bf16[512,512]{1,0:T(8,128)(2,1)S(1)}, bf16[512,512]{1,0:T(8,128)(2,1)}, u32[]{:S(2)}) copy-start(bf16[512,512]{1,0:T(8,128)(2,1)} %refs_1_.11) | copy-start | bytes 1572868
  23.6 1.0 %copy-start.5 = (bf16[512,512]{1,0:T(8,128)(2,1)S(1)}, bf16[512,512]{1,0:T(8,128)(2,1)}, u32[]{:S(2)}) copy-start(bf16[512,512]{1,0:T(8,128)(2,1)} %refs_2_.7) | copy-start | bytes 1572868
  24.7 6.5 %copy-start.7 = (bf16[4096,512]{1,0:T(8,128)(2,1)S(1)}, bf16[4096,512]{1,0:T(8,128)(2,1)}, u32[]{:S(2)}) copy-start(bf16[4096,512]{1,0:T(8,128)(2,1)} %refs_0_.6) | copy-start | bytes 12582916
  27.0 7.4 %copy-start.8 = (bf16[512,1024]{1,0:T(8,128)(2,1)}, bf16[512,1024]{1,0:T(8,128)(2,1)S(1)}, u32[]{:S(2)}) copy-start(bf16[512,1024]{1,0:T(8,128)(2,1)S(1)} %collective-permute-done.4.refs_3_.refs_4_) | copy-start | bytes 3145732
  27.8 6.7 %copy-start.12 = (bf16[512,512]{1,0:T(8,128)(2,1)}, bf16[512,512]{1,0:T(8,128)(2,1)S(1)}, u32[]{:S(2)}) copy-start(bf16[512,512]{1,0:T(8,128)(2,1)S(1)} %shard_map.88.refs_0_) | copy-start | bytes 1572868
  27.8 3.4 %collective-permute-start.6 = (bf16[512,1024]{1,0:T(8,128)(2,1)S(1)}, bf16[512,1024]{1,0:T(8,128)(2,1)S(1)}, u32[]{:S(2)}, u32[]{:S(2)}) collective-permute-start(bf16[512,1024]{1,0:T(8,128)(2,1)S(1)} %collective-permute-done.4.refs_3_.refs_4_), channel_id=1, source_target_pairs={{0,1},{1,0},{2,3},{3,2},{4,5},{5,4},{6,7},{7,6},{8,9},{9,8},{10,11... | collective-permute-start | bytes 3145736 | tf_op jit(solution)/shard_map/ppermute | solution.py:225
  27.8 14.5 %collective-permute-start.8 = (bf16[512,512]{1,0:T(8,128)(2,1)S(1)}, bf16[512,512]{1,0:T(8,128)(2,1)}, u32[]{:S(2)}, u32[]{:S(2)}) collective-permute-start(bf16[512,512]{1,0:T(8,128)(2,1)S(1)} %shard_map.88.refs_0_), channel_id=1, source_target_pairs={{0,4},{4,0},{8,12},{12,8},{16,20},{20,16},{24,28},{28,24},{1,5},{5... | collective-permute-start | bytes 1572872 | tf_op jit(solution)/shard_map/ppermute | solution.py:225
  29.7 14.3 %collective-permute-start.9 = (bf16[512,512]{1,0:T(8,128)(2,1)}, bf16[512,512]{1,0:T(8,128)(2,1)}, u32[]{:S(2)}, u32[]{:S(2)}) collective-permute-start(bf16[512,512]{1,0:T(8,128)(2,1)} %collective-permute-done.5.refs_1_.refs_6_), channel_id=1, source_target_pairs={{0,2},{1,3},{2,0},{3,1},{4,6},{5,7},{6,4},{7,5},{8,10},{9,11},{10,... | collective-permute-start | bytes 1572872 | tf_op jit(solution)/shard_map/ppermute | solution.py:225
  31.2 3.3 %copy-start.9 = (bf16[512,1024]{1,0:T(8,128)(2,1)}, bf16[512,1024]{1,0:T(8,128)(2,1)S(1)}, u32[]{:S(2)}) copy-start(bf16[512,1024]{1,0:T(8,128)(2,1)S(1)} %collective-permute-done.1.refs_2_.refs_3_) | copy-start | bytes 3145732
  31.2 3.3 %copy-start.10 = (bf16[512,1024]{1,0:T(8,128)(2,1)}, bf16[512,1024]{1,0:T(8,128)(2,1)S(1)}, u32[]{:S(2)}) copy-start(bf16[512,1024]{1,0:T(8,128)(2,1)S(1)} %collective-permute-done.6.refs_4_.refs_5_) | copy-start | bytes 3145732
  35.0 9.0 %collective-permute-start.7 = (bf16[512,128]{1,0:T(8,128)(2,1)S(1)}, bf16[512,128]{1,0:T(8,128)(2,1)S(1)}, u32[]{:S(2)}, u32[]{:S(2)}) collective-permute-start(bf16[512,128]{1,0:T(8,128)(2,1)S(1)} %shard_map.90.refs_0_), channel_id=1, source_target_pairs={{0,8},{4,12},{8,0},{12,4},{16,24},{20,28},{24,16},{28,20},{1,9},{5... | collective-permute-start | bytes 393224 | tf_op jit(solution)/shard_map/ppermute | solution.py:225
  36.6 10.1 %collective-permute-start.11 = (bf16[512,512]{1,0:T(8,128)(2,1)}, bf16[512,512]{1,0:T(8,128)(2,1)S(1)}, u32[]{:S(2)}, u32[]{:S(2)}) collective-permute-start(bf16[512,512]{1,0:T(8,128)(2,1)} %collective-permute-done.5.refs_1_.refs_6_), channel_id=1, source_target_pairs={{0,1},{1,0},{2,3},{3,2},{4,5},{5,4},{6,7},{7,6},{8,9},{9,8},{10,11... | collective-permute-start | bytes 1572872 | tf_op jit(solution)/shard_map/ppermute | solution.py:225
  44.0 2.7 %collective-permute-start.12 = (bf16[512,512]{1,0:T(8,128)(2,1)}, bf16[512,512]{1,0:T(8,128)(2,1)S(1)}, u32[]{:S(2)}, u32[]{:S(2)}) collective-permute-start(bf16[512,512]{1,0:T(8,128)(2,1)} %collective-permute-done.9.refs_3_.refs_8_), channel_id=1, source_target_pairs={{0,1},{1,0},{2,3},{3,2},{4,5},{5,4},{6,7},{7,6},{8,9},{9,8},{10,11... | collective-permute-start | bytes 1572872 | tf_op jit(solution)/shard_map/ppermute | solution.py:225
  44.0 9.7 %collective-permute-start.10 = (bf16[512,128]{1,0:T(8,128)(2,1)S(1)}, bf16[512,128]{1,0:T(8,128)(2,1)S(1)}, u32[]{:S(2)}, u32[]{:S(2)}) collective-permute-start(bf16[512,128]{1,0:T(8,128)(2,1)S(1)} %shard_map.92), channel_id=1, source_target_pairs={{0,16},{4,20},{8,24},{12,28},{16,0},{20,4},{24,8},{28,12},{1,17},{... | collective-permute-start | bytes 393224 | tf_op jit(solution)/shard_map/ppermute | solution.py:225
  46.7 7.6 %copy-start.13 = (bf16[512,512]{1,0:T(8,128)(2,1)}, bf16[512,512]{1,0:T(8,128)(2,1)S(1)}, u32[]{:S(2)}) copy-start(bf16[512,512]{1,0:T(8,128)(2,1)S(1)} %collective-permute-done.11.refs_2_.refs_7_) | copy-start | bytes 1572868
  46.7 1.4 %copy-start.11 = (f32[512,512]{1,0:T(8,128)S(1)}, f32[512,512]{1,0:T(8,128)}, u32[]{:S(2)}) copy-start(f32[512,512]{1,0:T(8,128)} %shard_map.91.refs_5_) | copy-start | bytes 3145732
  48.1 6.2 %copy-start.14 = (bf16[512,512]{1,0:T(8,128)(2,1)}, bf16[512,512]{1,0:T(8,128)(2,1)S(1)}, u32[]{:S(2)}) copy-start(bf16[512,512]{1,0:T(8,128)(2,1)S(1)} %collective-permute-done.12.refs_4_.refs_9_) | copy-start | bytes 1572868
  49.9 10.2 %collective-permute-start.15 = (bf16[512,256]{1,0:T(8,128)(2,1)S(1)}, bf16[512,256]{1,0:T(8,128)(2,1)S(1)}, u32[]{:S(2)}, u32[]{:S(2)}) collective-permute-start(bf16[512,256]{1,0:T(8,128)(2,1)S(1)} %get-tuple-element.77.refs_0_), channel_id=1, source_target_pairs={{0,8},{4,12},{8,0},{12,4},{16,24},{20,28},{24,16},{28,20},{1,9},{5... | collective-permute-start | bytes 786440 | tf_op jit(solution)/shard_map/ppermute | solution.py:308
  51.6 13.3 %collective-permute-start.13 = (bf16[512,256]{1,0:T(8,128)(2,1)S(1)}, bf16[512,256]{1,0:T(8,128)(2,1)S(1)}, u32[]{:S(2)}, u32[]{:S(2)}) collective-permute-start(bf16[512,256]{1,0:T(8,128)(2,1)S(1)} %get-tuple-element.70.refs_0_), channel_id=1, source_target_pairs={{0,8},{4,12},{8,0},{12,4},{16,24},{20,28},{24,16},{28,20},{1,9},{5... | collective-permute-start | bytes 786440 | tf_op jit(solution)/shard_map/ppermute | solution.py:308
  53.8 6.3 %collective-permute-start.16 = (bf16[512,128]{1,0:T(8,128)(2,1)S(1)}, bf16[512,128]{1,0:T(8,128)(2,1)S(1)}, u32[]{:S(2)}, u32[]{:S(2)}) collective-permute-start(bf16[512,128]{1,0:T(8,128)(2,1)S(1)} %add_convert_fusion.1), channel_id=1, source_target_pairs={{0,4},{4,0},{8,12},{12,8},{16,20},{20,16},{24,28},{28,24},{1,5},{5... | collective-permute-start | bytes 393224 | tf_op jit(solution)/shard_map/ppermute | solution.py:225
  59.2 6.5 %copy-start.18 = (bf16[512,256]{1,0:T(8,128)(2,1)S(1)}, bf16[512,256]{1,0:T(8,128)(2,1)}, u32[]{:S(2)}) copy-start(bf16[512,256]{1,0:T(8,128)(2,1)} %get-tuple-element.88.refs_0_) | copy-start | bytes 786436
  59.3 11.2 %copy-start.20 = (bf16[512,256]{1,0:T(8,128)(2,1)S(1)}, bf16[512,256]{1,0:T(8,128)(2,1)}, u32[]{:S(2)}) copy-start(bf16[512,256]{1,0:T(8,128)(2,1)} %get-tuple-element.76.refs_0_) | copy-start | bytes 786436
  59.3 11.2 %collective-permute-start.17 = (bf16[512,256]{1,0:T(8,128)(2,1)}, bf16[512,256]{1,0:T(8,128)(2,1)S(1)}, u32[]{:S(2)}, u32[]{:S(2)}) collective-permute-start(bf16[512,256]{1,0:T(8,128)(2,1)} %get-tuple-element.76.refs_0_), channel_id=1, source_target_pairs={{0,8},{4,12},{8,0},{12,4},{16,24},{20,28},{24,16},{28,20},{1,9},{5... | collective-permute-start | bytes 786440 | tf_op jit(solution)/shard_map/ppermute | solution.py:308
  60.2 10.3 %collective-permute-start.18 = (bf16[512,256]{1,0:T(8,128)(2,1)S(1)}, bf16[512,256]{1,0:T(8,128)(2,1)S(1)}, u32[]{:S(2)}, u32[]{:S(2)}) collective-permute-start(bf16[512,256]{1,0:T(8,128)(2,1)S(1)} %shard_map.96), channel_id=1, source_target_pairs={{8,16},{12,20},{16,8},{20,12},{9,17},{13,21},{17,9},{21,13},{10,18... | collective-permute-start | bytes 786440 | tf_op jit(solution)/shard_map/ppermute | solution.py:308
  64.9 6.5 %copy-start.16 = (f32[512,256]{1,0:T(8,128)S(1)}, f32[512,256]{1,0:T(8,128)}, u32[]{:S(2)}) copy-start(f32[512,256]{1,0:T(8,128)} %get-tuple-element.85.refs_0_) | copy-start | bytes 1572868
  64.9 12.6 %copy-start.15 = (f32[512,256]{1,0:T(8,128)S(1)}, f32[512,256]{1,0:T(8,128)}, u32[]{:S(2)}) copy-start(f32[512,256]{1,0:T(8,128)} %get-tuple-element.89.refs_0_) | copy-start | bytes 1572868
  64.9 14.6 %copy-start.4 = (bf16[512,512]{1,0:T(8,128)(2,1)S(1)}, bf16[512,512]{1,0:T(8,128)(2,1)}, u32[]{:S(2)}) copy-start(bf16[512,512]{1,0:T(8,128)(2,1)} %refs_1_.11) | copy-start | bytes 1572868
  64.9 14.6 %copy-start.6 = (bf16[512,512]{1,0:T(8,128)(2,1)S(1)}, bf16[512,512]{1,0:T(8,128)(2,1)}, u32[]{:S(2)}) copy-start(bf16[512,512]{1,0:T(8,128)(2,1)} %refs_2_.7) | copy-start | bytes 1572868
  65.0 12.6 %collective-permute-start.14 = (bf16[512,256]{1,0:T(8,128)(2,1)S(1)}, bf16[512,256]{1,0:T(8,128)(2,1)S(1)}, u32[]{:S(2)}, u32[]{:S(2)}) collective-permute-start(bf16[512,256]{1,0:T(8,128)(2,1)S(1)} %shard_map.94), channel_id=1, source_target_pairs={{8,16},{12,20},{16,8},{20,12},{9,17},{13,21},{17,9},{21,13},{10,18... | collective-permute-start | bytes 786440 | tf_op jit(solution)/shard_map/ppermute | solution.py:308
  65.8 12.8 %collective-permute-start.21 = (bf16[512,256]{1,0:T(8,128)(2,1)S(1)}, bf16[512,256]{1,0:T(8,128)(2,1)S(1)}, u32[]{:S(2)}, u32[]{:S(2)}) collective-permute-start(bf16[512,256]{1,0:T(8,128)(2,1)S(1)} %copy-done.18), channel_id=1, source_target_pairs={{0,8},{4,12},{8,0},{12,4},{16,24},{20,28},{24,16},{28,20},{1,9},{5... | collective-permute-start | bytes 786440 | tf_op jit(solution)/shard_map/ppermute | solution.py:308
  70.5 14.1 %copy-start.21 = (f32[512,256]{1,0:T(8,128)S(1)}, f32[512,256]{1,0:T(8,128)}, u32[]{:S(2)}) copy-start(f32[512,256]{1,0:T(8,128)} %get-tuple-element.84.refs_0_) | copy-start | bytes 1572868
  70.5 14.1 %collective-permute-start.19 = (bf16[512,256]{1,0:T(8,128)(2,1)S(1)}, bf16[512,256]{1,0:T(8,128)(2,1)S(1)}, u32[]{:S(2)}, u32[]{:S(2)}) collective-permute-start(bf16[512,256]{1,0:T(8,128)(2,1)S(1)} %shard_map.97), channel_id=1, source_target_pairs={{8,16},{12,20},{16,8},{20,12},{9,17},{13,21},{17,9},{21,13},{10,18... | collective-permute-start | bytes 786440 | tf_op jit(solution)/shard_map/ppermute | solution.py:308
  71.4 13.2 %collective-permute-start.20 = (bf16[512,256]{1,0:T(8,128)(2,1)S(1)}, bf16[512,256]{1,0:T(8,128)(2,1)S(1)}, u32[]{:S(2)}, u32[]{:S(2)}) collective-permute-start(bf16[512,256]{1,0:T(8,128)(2,1)S(1)} %shard_map.99), channel_id=1, source_target_pairs={{0,8},{4,12},{8,0},{12,4},{16,24},{20,28},{24,16},{28,20},{1,9},{5... | collective-permute-start | bytes 786440 | tf_op jit(solution)/shard_map/ppermute | solution.py:308
  77.6 9.8 %collective-permute-start.23 = (bf16[512,256]{1,0:T(8,128)(2,1)S(1)}, bf16[512,256]{1,0:T(8,128)(2,1)S(1)}, u32[]{:S(2)}, u32[]{:S(2)}) collective-permute-start(bf16[512,256]{1,0:T(8,128)(2,1)S(1)} %shard_map.101), channel_id=1, source_target_pairs={{0,8},{4,12},{8,0},{12,4},{16,24},{20,28},{24,16},{28,20},{1,9},{5... | collective-permute-start | bytes 786440 | tf_op jit(solution)/shard_map/ppermute | solution.py:308
  78.6 6.9 %collective-permute-start.22 = (bf16[512,256]{1,0:T(8,128)(2,1)S(1)}, bf16[512,256]{1,0:T(8,128)(2,1)S(1)}, u32[]{:S(2)}, u32[]{:S(2)}) collective-permute-start(bf16[512,256]{1,0:T(8,128)(2,1)S(1)} %shard_map.102), channel_id=1, source_target_pairs={{8,16},{12,20},{16,8},{20,12},{9,17},{13,21},{17,9},{21,13},{10,18... | collective-permute-start | bytes 786440 | tf_op jit(solution)/shard_map/ppermute | solution.py:308
  84.6 2.8 %copy-start.17 = (f32[512,256]{1,0:T(8,128)S(1)}, f32[512,256]{1,0:T(8,128)}, u32[]{:S(2)}) copy-start(f32[512,256]{1,0:T(8,128)} %get-tuple-element.87.refs_1_) | copy-start | bytes 1572868

commit v7 on v6

--- a/solution.py
+++ b/solution.py
@@ -385,7 +385,7 @@
         outs = [shaped((cols // 2, width), F32)]
         o, near, back_term = phase(o, near, back_term)
         near_c = flip(near, "head", 1)
-        (begun,) = call(functools.partial(first, True), outs, o, *mine, scratch=scratch, vmem=60)
+        (begun,) = call(functools.partial(first, True), outs, o, *mine, scratch=scratch, vmem=12)
         got, n, far, begun = phase(got, n, far, begun)
     else:
         near_c = flip(near, "head", 1)

time: 89 us -> 89 us (level)
  Pallas kernels: 25 us -> 21.7 us
  local copies, waits for them, and re-layouts: 5.51 us -> 8.13 us
    pallas_call x9, Pallas kernels: 22.8 us -> 19.5 us  [call(): pl.pallas_call(kernel, out_shape=outs, in_specs=[pl.BlockSpec(memory_spac...]
    unnamed x44 -> x52, local copies, waits for them, and re-layouts: 5.51 us -> 8.13 us
  transfers between devices with their start and end apart: 24 -> 24, of which waited for: 9 -> 9; matrix products, arithmetic and copies ran while one was open for 0% -> 0% of each run, Pallas kernels for 27% -> 24%
where the time goes in v7:
time: 89 us; the launch traced here: 88.5 us
  starting transfers between devices  36.7 us (41%)
  Pallas kernels  21.7 us (24%)
  waiting for transfers between devices  20.5 us (23%)
  local copies, waits for them, and re-layouts  8.13 us (9%)
  between operations  1.24 us (1%)
    pallas_call x9, Pallas kernels, call(): pl.pallas_call(kernel, out_shape=outs, in_specs=[pl.BlockSpec(memory_spac...  19.5 us
    ppermute x14, starting transfers between devices, flip(): lax.ppermute(a, axis, [(i, i ^ bit) for i in range(lax.axis_size(axis))])  18.9 us
    ppermute x10, starting transfers between devices, send(): lax.ppermute(a, 'seq', [(2 * s + i, 2 * t + i) for s, t in pairs for i in...  17.7 us
    ppermute x14, waiting for transfers between devices, flip(): lax.ppermute(a, axis, [(i, i ^ bit) for i in range(lax.axis_size(axis))])  14.9 us
    unnamed x52, local copies, waits for them, and re-layouts  8.13 us
    ppermute x10, waiting for transfers between devices, send(): lax.ppermute(a, 'seq', [(2 * s + i, 2 * t + i) for s, t in pairs for i in...  5.64 us
  transfers between devices with their start and end apart: 24, of which 9 were waited for; matrix products, arithmetic and copies ran while one was open for 0% of the time, Pallas kernels for 24%

profile of v7, /device:TPU:0, one launch (start us, length us, event | category | flops | bytes accessed | tf_op | source)
XLA Modules:
  0.0 88.5 jit_solution(14210336402205643343)
XLA Ops:
  0.7 3.0 %collective-permute-start.4 = (bf16[512,1024]{1,0:T(8,128)(2,1)}, bf16[512,1024]{1,0:T(8,128)(2,1)S(1)}, u32[]{:S(2)}, u32[]{:S(2)}) collective-permute-start(bf16[512,1024]{1,0:T(8,128)(2,1)} %refs_2_.6), channel_id=1, source_target_pairs={{0,2},{1,3},{2,0},{3,1},{4,6},{5,7},{6,4},{7,5},{8,10},{9,11},{10,... | collective-permute-start | bytes 3145736 | tf_op jit(solution)/shard_map/ppermute | solution.py:225
  3.7 2.4 %shard_map.84 = (bf16[512,128]{1,0:T(8,128)(2,1)}, bf16[512,512]{1,0:T(8,128)(2,1)}) custom-call(bf16[512,512]{1,0:T(8,128)(2,1)} %refs_1_.11, bf16[512,512]{1,0:T(8,128)(2,1)} %refs_2_.7, bf16[512,1024]{1,0:T(8,128)(2,1)} %refs_2_.6), custom_call_target="tpu_custom_call" | custom-call | flops 1048576 | bytes 16384 | tf_op jit(solution)/shard_map/pallas_call | solution.py:29
  6.1 1.6 %collective-permute-start = (bf16[512,128]{1,0:T(8,128)(2,1)}, bf16[512,128]{1,0:T(8,128)(2,1)S(1)}, u32[]{:S(2)}, u32[]{:S(2)}) collective-permute-start(bf16[512,128]{1,0:T(8,128)(2,1)} %get-tuple-element.48.refs_0_), channel_id=1, source_target_pairs={{0,4},{4,0},{8,12},{12,8},{16,20},{20,16},{24,28},{28,24},{1,5},{5... | collective-permute-start | bytes 393224 | tf_op jit(solution)/shard_map/ppermute | solution.py:225
  7.7 3.7 %collective-permute-done.refs_1_ = bf16[512,128]{1,0:T(8,128)(2,1)S(1)} collective-permute-done((bf16[512,128]{1,0:T(8,128)(2,1)}, bf16[512,128]{1,0:T(8,128)(2,1)S(1)}, u32[]{:S(2)}, u32[]{:S(2)}) %collective-permute-start) | collective-permute-done | bytes 131104 | tf_op jit(solution)/shard_map/ppermute | solution.py:225
  11.3 1.5 %collective-permute-start.5 = (bf16[512,512]{1,0:T(8,128)(2,1)}, bf16[512,512]{1,0:T(8,128)(2,1)}, u32[]{:S(2)}, u32[]{:S(2)}) collective-permute-start(bf16[512,512]{1,0:T(8,128)(2,1)} %get-tuple-element.53), channel_id=1, source_target_pairs={{0,4},{4,0},{8,12},{12,8},{16,20},{20,16},{24,28},{28,24},{1,5},{5... | collective-permute-start | bytes 1572872 | tf_op jit(solution)/shard_map/ppermute | solution.py:225
  12.9 0.9 %copy-done.21 = bf16[512,128]{1,0:T(8,128)(2,1)S(1)} copy-done((bf16[512,128]{1,0:T(8,128)(2,1)S(1)}, bf16[512,128]{1,0:T(8,128)(2,1)}, u32[]{:S(2)}) %copy-start.21) | copy-done | bytes 131096
  13.8 1.6 %collective-permute-start.2 = (bf16[512,128]{1,0:T(8,128)(2,1)S(1)}, bf16[512,128]{1,0:T(8,128)(2,1)S(1)}, u32[]{:S(2)}, u32[]{:S(2)}) collective-permute-start(bf16[512,128]{1,0:T(8,128)(2,1)S(1)} %shard_map.85.refs_0_), channel_id=1, source_target_pairs={{0,8},{4,12},{8,0},{12,4},{16,24},{20,28},{24,16},{28,20},{1,9},{5... | collective-permute-start | bytes 393224 | tf_op jit(solution)/shard_map/ppermute | solution.py:225
  15.4 3.4 %collective-permute-done.2.refs_1_ = bf16[512,128]{1,0:T(8,128)(2,1)S(1)} collective-permute-done((bf16[512,128]{1,0:T(8,128)(2,1)S(1)}, bf16[512,128]{1,0:T(8,128)(2,1)S(1)}, u32[]{:S(2)}, u32[]{:S(2)}) %collective-permute-start.2) | collective-permute-done | bytes 131104 | tf_op jit(solution)/shard_map/ppermute | solution.py:225
  18.9 2.7 %collective-permute-start.3 = (bf16[512,128]{1,0:T(8,128)(2,1)S(1)}, bf16[512,128]{1,0:T(8,128)(2,1)S(1)}, u32[]{:S(2)}, u32[]{:S(2)}) collective-permute-start(bf16[512,128]{1,0:T(8,128)(2,1)S(1)} %shard_map.86), channel_id=1, source_target_pairs={{0,16},{4,20},{8,24},{12,28},{16,0},{20,4},{24,8},{28,12},{1,17},{... | collective-permute-start | bytes 393224 | tf_op jit(solution)/shard_map/ppermute | solution.py:225
  21.5 1.0 %copy-done.1 = bf16[512,512]{1,0:T(8,128)(2,1)S(1)} copy-done((bf16[512,512]{1,0:T(8,128)(2,1)S(1)}, bf16[512,512]{1,0:T(8,128)(2,1)}, u32[]{:S(2)}) %copy-start.1) | copy-done | bytes 524312
  22.6 1.0 %copy-done.3 = bf16[512,512]{1,0:T(8,128)(2,1)S(1)} copy-done((bf16[512,512]{1,0:T(8,128)(2,1)S(1)}, bf16[512,512]{1,0:T(8,128)(2,1)}, u32[]{:S(2)}) %copy-start.3) | copy-done | bytes 524312
  23.6 1.0 %copy-done.5 = bf16[512,512]{1,0:T(8,128)(2,1)S(1)} copy-done((bf16[512,512]{1,0:T(8,128)(2,1)S(1)}, bf16[512,512]{1,0:T(8,128)(2,1)}, u32[]{:S(2)}) %copy-start.5) | copy-done | bytes 524312
  24.7 1.6 %shard_map.87.refs_2_ = f32[512,512]{1,0:T(8,128)S(1)} custom-call(bf16[512,512]{1,0:T(8,128)(2,1)S(1)} %copy-done.1, bf16[512,512]{1,0:T(8,128)(2,1)S(1)} %copy-done.3, bf16[512,512]{1,0:T(8,128)(2,1)S(1)} %copy-done.5), custom_call_target="tpu_custom_call" | custom-call | flops 1048576 | bytes 16384 | tf_op jit(solution)/shard_map/pallas_call | solution.py:29
  26.3 0.7 collective-permute-done.4.refs_3_.refs_4_
  27.1 0.6 shard_map.88.refs_0_
  27.8 1.8 %collective-permute-start.8 = (bf16[512,512]{1,0:T(8,128)(2,1)S(1)}, bf16[512,512]{1,0:T(8,128)(2,1)S(1)}, u32[]{:S(2)}, u32[]{:S(2)}) collective-permute-start(bf16[512,512]{1,0:T(8,128)(2,1)S(1)} %shard_map.88.refs_0_), channel_id=1, source_target_pairs={{0,4},{4,0},{8,12},{12,8},{16,20},{20,16},{24,28},{28,24},{1,5},{5... | collective-permute-start | bytes 1572872 | tf_op jit(solution)/shard_map/ppermute | solution.py:225
  29.7 1.5 %collective-permute-start.9 = (bf16[512,512]{1,0:T(8,128)(2,1)}, bf16[512,512]{1,0:T(8,128)(2,1)}, u32[]{:S(2)}, u32[]{:S(2)}) collective-permute-start(bf16[512,512]{1,0:T(8,128)(2,1)} %collective-permute-done.5.refs_1_.refs_6_), channel_id=1, source_target_pairs={{0,2},{1,3},{2,0},{3,1},{4,6},{5,7},{6,4},{7,5},{8,10},{9,11},{10,... | collective-permute-start | bytes 1572872 | tf_op jit(solution)/shard_map/ppermute | solution.py:225
  31.2 3.2 %shard_map.89.refs_1_.refs_3_ = bf16[512,512]{1,0:T(8,128)(2,1)S(1)} custom-call(bf16[4096,512]{1,0:T(8,128)(2,1)S(1)} %copy-done.7, bf16[512,1024]{1,0:T(8,128)(2,1)S(1)} %copy-done, bf16[512,1024]{1,0:T(8,128)(2,1)S(1)} %collective-permute-done.1.refs_2_.refs_3_, bf16[512,1024]{1,0:T(8,128)(2,1)S(1)} %collective-permute-done.4.refs_3_.refs_4_, ...), custom_call_target="tpu_custom_call" | custom-call | flops 1048576 | bytes 16384 | tf_op jit(solution)/shard_map/pallas_call | solution.py:29
  34.4 0.5 shard_map.90.refs_0_
  34.9 1.6 %collective-permute-start.7 = (bf16[512,128]{1,0:T(8,128)(2,1)S(1)}, bf16[512,128]{1,0:T(8,128)(2,1)S(1)}, u32[]{:S(2)}, u32[]{:S(2)}) collective-permute-start(bf16[512,128]{1,0:T(8,128)(2,1)S(1)} %shard_map.90.refs_0_), channel_id=1, source_target_pairs={{0,8},{4,12},{8,0},{12,4},{16,24},{20,28},{24,16},{28,20},{1,9},{5... | collective-permute-start | bytes 393224 | tf_op jit(solution)/shard_map/ppermute | solution.py:225
  36.6 0.7 shard_map.91.refs_5_
  37.3 1.0 %copy-done.11 = f32[512,512]{1,0:T(8,128)} copy-done((f32[512,512]{1,0:T(8,128)}, f32[512,512]{1,0:T(8,128)S(1)}, u32[]{:S(2)}) %copy-start.11) | copy-done | bytes 1048600
  38.2 4.0 %collective-permute-done.8.refs_0_.refs_1_ = bf16[512,512]{1,0:T(8,128)(2,1)S(1)} collective-permute-done((bf16[512,512]{1,0:T(8,128)(2,1)S(1)}, bf16[512,512]{1,0:T(8,128)(2,1)S(1)}, u32[]{:S(2)}, u32[]{:S(2)}) %collective-permute-start.8) | collective-permute-done | bytes 524320 | tf_op jit(solution)/shard_map/ppermute | solution.py:225
  42.2 0.8 copy-done.14
  43.0 1.0 %collective-permute-done.9.refs_3_.refs_8_ = bf16[512,512]{1,0:T(8,128)(2,1)} collective-permute-done((bf16[512,512]{1,0:T(8,128)(2,1)}, bf16[512,512]{1,0:T(8,128)(2,1)}, u32[]{:S(2)}, u32[]{:S(2)}) %collective-permute-start.9) | collective-permute-done | bytes 524320 | tf_op jit(solution)/shard_map/ppermute | solution.py:225
  44.0 2.7 %collective-permute-start.10 = (bf16[512,128]{1,0:T(8,128)(2,1)S(1)}, bf16[512,128]{1,0:T(8,128)(2,1)S(1)}, u32[]{:S(2)}, u32[]{:S(2)}) collective-permute-start(bf16[512,128]{1,0:T(8,128)(2,1)S(1)} %shard_map.92), channel_id=1, source_target_pairs={{0,16},{4,20},{8,24},{12,28},{16,0},{20,4},{24,8},{28,12},{1,17},{... | collective-permute-start | bytes 393224 | tf_op jit(solution)/shard_map/ppermute | solution.py:225
  46.7 1.2 %copy-done.12 = f32[512,512]{1,0:T(8,128)S(1)} copy-done((f32[512,512]{1,0:T(8,128)S(1)}, f32[512,512]{1,0:T(8,128)}, u32[]{:S(2)}) %copy-start.12) | copy-done | bytes 1048600
  47.9 1.0 %copy-done.15 = bf16[512,512]{1,0:T(8,128)(2,1)S(1)} copy-done((bf16[512,512]{1,0:T(8,128)(2,1)S(1)}, bf16[512,512]{1,0:T(8,128)(2,1)}, u32[]{:S(2)}) %copy-start.15) | copy-done | bytes 524312
  49.0 0.6 shard_map.93
  49.5 1.6 %collective-permute-start.15 = (bf16[512,256]{1,0:T(8,128)(2,1)S(1)}, bf16[512,256]{1,0:T(8,128)(2,1)S(1)}, u32[]{:S(2)}, u32[]{:S(2)}) collective-permute-start(bf16[512,256]{1,0:T(8,128)(2,1)S(1)} %get-tuple-element.77.refs_0_), channel_id=1, source_target_pairs={{0,8},{4,12},{8,0},{12,4},{16,24},{20,28},{24,16},{28,20},{1,9},{5... | collective-permute-start | bytes 786440 | tf_op jit(solution)/shard_map/ppermute | solution.py:308
  51.2 0.4 collective-permute-start.13
  51.6 2.1 %collective-permute-done.10 = bf16[512,128]{1,0:T(8,128)(2,1)S(1)} collective-permute-done((bf16[512,128]{1,0:T(8,128)(2,1)S(1)}, bf16[512,128]{1,0:T(8,128)(2,1)S(1)}, u32[]{:S(2)}, u32[]{:S(2)}) %collective-permute-start.10) | collective-permute-done | bytes 131104 | tf_op jit(solution)/shard_map/ppermute | solution.py:225
  53.9 0.8 collective-permute-start.16
  54.7 4.9 %shard_map.95 = (bf16[512,256]{1,0:T(8,128)(2,1)}, bf16[512,256]{1,0:T(8,128)(2,1)}, f32[512,256]{1,0:T(8,128)}, f32[512,256]{1,0:T(8,128)}, f32[512,256]{1,0:T(8,128)}, /*index=5*/f32[512,256]{1,0:T(8,128)}) custom-call(bf16[512,512]{1,0:T(8,128)(2,1)} %copy-done.13, bf16[512,512]{1,0:T(8,128)(2,1)} %copy-done.14, bf16[512,1024]{1,0:T(8,128)(2,1)} %refs_2_.6, ...), custom_call_target="tpu_custom_call" | custom-call | flops 17179869184 | bytes 16384 | tf_op jit(solution)/shard_map/pallas_call | solution.py:29
  59.6 0.7 collective-permute-start.17
  60.4 0.7 collective-permute-start.18
  61.0 3.9 %collective-permute-done.13.refs_1_ = bf16[512,256]{1,0:T(8,128)(2,1)S(1)} collective-permute-done((bf16[512,256]{1,0:T(8,128)(2,1)S(1)}, bf16[512,256]{1,0:T(8,128)(2,1)S(1)}, u32[]{:S(2)}, u32[]{:S(2)}) %collective-permute-start.13) | collective-permute-done | bytes 262176 | tf_op jit(solution)/shard_map/ppermute | solution.py:308
  65.0 0.8 collective-permute-start.14
  65.9 4.5 %collective-permute-start.21 = (bf16[512,256]{1,0:T(8,128)(2,1)S(1)}, bf16[512,256]{1,0:T(8,128)(2,1)S(1)}, u32[]{:S(2)}, u32[]{:S(2)}) collective-permute-start(bf16[512,256]{1,0:T(8,128)(2,1)S(1)} %copy-done.20), channel_id=1, source_target_pairs={{0,8},{4,12},{8,0},{12,4},{16,24},{20,28},{24,16},{28,20},{1,9},{5... | collective-permute-start | bytes 786440 | tf_op jit(solution)/shard_map/ppermute | solution.py:308
  70.4 0.1 collective-permute-done.17.refs_1_
  70.6 0.8 collective-permute-start.19
  71.5 6.2 %collective-permute-start.20 = (bf16[512,256]{1,0:T(8,128)(2,1)S(1)}, bf16[512,256]{1,0:T(8,128)(2,1)S(1)}, u32[]{:S(2)}, u32[]{:S(2)}) collective-permute-start(bf16[512,256]{1,0:T(8,128)(2,1)S(1)} %shard_map.99), channel_id=1, source_target_pairs={{0,8},{4,12},{8,0},{12,4},{16,24},{20,28},{24,16},{28,20},{1,9},{5... | collective-permute-start | bytes 786440 | tf_op jit(solution)/shard_map/ppermute | solution.py:308
  77.8 1.0 %collective-permute-start.23 = (bf16[512,256]{1,0:T(8,128)(2,1)S(1)}, bf16[512,256]{1,0:T(8,128)(2,1)S(1)}, u32[]{:S(2)}, u32[]{:S(2)}) collective-permute-start(bf16[512,256]{1,0:T(8,128)(2,1)S(1)} %shard_map.101), channel_id=1, source_target_pairs={{0,8},{4,12},{8,0},{12,4},{16,24},{20,28},{24,16},{28,20},{1,9},{5... | collective-permute-start | bytes 786440 | tf_op jit(solution)/shard_map/ppermute | solution.py:308
  78.9 0.9 collective-permute-start.22
  79.8 5.0 %shard_map.98 = (bf16[512,512]{1,0:T(8,128)(2,1)}, bf16[512,512]{1,0:T(8,128)(2,1)}, bf16[512,512]{1,0:T(8,128)(2,1)}) custom-call(bf16[512,512]{1,0:T(8,128)(2,1)S(1)} %copy-done.2, bf16[512,512]{1,0:T(8,128)(2,1)S(1)} %copy-done.4, bf16[512,512]{1,0:T(8,128)(2,1)S(1)} %copy-done.6, bf16[512,512]{1,0:T(8,128)(2,1)S(1)} %shard_map.89.refs_1_.refs_3_, ...), custom_call_target="tpu_custom_call" | custom-call | flops 1048576 | bytes 16384 | tf_op jit(solution)/shard_map/pallas_call | solution.py:29
  84.9 0.9 shard_map.100.refs_0_
  85.8 1.6 %collective-permute-done.23.refs_3_ = bf16[512,256]{1,0:T(8,128)(2,1)S(1)} collective-permute-done((bf16[512,256]{1,0:T(8,128)(2,1)S(1)}, bf16[512,256]{1,0:T(8,128)(2,1)S(1)}, u32[]{:S(2)}, u32[]{:S(2)}) %collective-permute-start.23) | collective-permute-done | bytes 262176 | tf_op jit(solution)/shard_map/ppermute | solution.py:308
  87.4 0.9 shard_map.103
  (75 shorter events, 0.9 us)
Async XLA Ops:
  0.6 30.6 %copy-start = (bf16[512,1024]{1,0:T(8,128)(2,1)S(1)}, bf16[512,1024]{1,0:T(8,128)(2,1)}, u32[]{:S(2)}) copy-start(bf16[512,1024]{1,0:T(8,128)(2,1)} %refs_2_.6) | copy-start | bytes 3145732
  0.6 26.5 %copy-start.2 = (bf16[512,512]{1,0:T(8,128)(2,1)S(1)}, bf16[512,512]{1,0:T(8,128)(2,1)}, u32[]{:S(2)}) copy-start(bf16[512,512]{1,0:T(8,128)(2,1)} %refs_0_.8) | copy-start | bytes 1572868
  0.7 26.4 %collective-permute-start.4 = (bf16[512,1024]{1,0:T(8,128)(2,1)}, bf16[512,1024]{1,0:T(8,128)(2,1)S(1)}, u32[]{:S(2)}, u32[]{:S(2)}) collective-permute-start(bf16[512,1024]{1,0:T(8,128)(2,1)} %refs_2_.6), channel_id=1, source_target_pairs={{0,2},{1,3},{2,0},{3,1},{4,6},{5,7},{6,4},{7,5},{8,10},{9,11},{10,... | collective-permute-start | bytes 3145736 | tf_op jit(solution)/shard_map/ppermute | solution.py:225
  6.1 5.2 %collective-permute-start = (bf16[512,128]{1,0:T(8,128)(2,1)}, bf16[512,128]{1,0:T(8,128)(2,1)S(1)}, u32[]{:S(2)}, u32[]{:S(2)}) collective-permute-start(bf16[512,128]{1,0:T(8,128)(2,1)} %get-tuple-element.48.refs_0_), channel_id=1, source_target_pairs={{0,4},{4,0},{8,12},{12,8},{16,20},{20,16},{24,28},{28,24},{1,5},{5... | collective-permute-start | bytes 393224 | tf_op jit(solution)/shard_map/ppermute | solution.py:225
  11.3 15.0 %collective-permute-start.5 = (bf16[512,512]{1,0:T(8,128)(2,1)}, bf16[512,512]{1,0:T(8,128)(2,1)}, u32[]{:S(2)}, u32[]{:S(2)}) collective-permute-start(bf16[512,512]{1,0:T(8,128)(2,1)} %get-tuple-element.53), channel_id=1, source_target_pairs={{0,4},{4,0},{8,12},{12,8},{16,20},{20,16},{24,28},{28,24},{1,5},{5... | collective-permute-start | bytes 1572872 | tf_op jit(solution)/shard_map/ppermute | solution.py:225
  13.8 5.0 %collective-permute-start.2 = (bf16[512,128]{1,0:T(8,128)(2,1)S(1)}, bf16[512,128]{1,0:T(8,128)(2,1)S(1)}, u32[]{:S(2)}, u32[]{:S(2)}) collective-permute-start(bf16[512,128]{1,0:T(8,128)(2,1)S(1)} %shard_map.85.refs_0_), channel_id=1, source_target_pairs={{0,8},{4,12},{8,0},{12,4},{16,24},{20,28},{24,16},{28,20},{1,9},{5... | collective-permute-start | bytes 393224 | tf_op jit(solution)/shard_map/ppermute | solution.py:225
  18.9 7.4 %collective-permute-start.3 = (bf16[512,128]{1,0:T(8,128)(2,1)S(1)}, bf16[512,128]{1,0:T(8,128)(2,1)S(1)}, u32[]{:S(2)}, u32[]{:S(2)}) collective-permute-start(bf16[512,128]{1,0:T(8,128)(2,1)S(1)} %shard_map.86), channel_id=1, source_target_pairs={{0,16},{4,20},{8,24},{12,28},{16,0},{20,4},{24,8},{28,12},{1,17},{... | collective-permute-start | bytes 393224 | tf_op jit(solution)/shard_map/ppermute | solution.py:225
  21.5 9.6 %collective-permute-start.1 = (bf16[512,1024]{1,0:T(8,128)(2,1)}, bf16[512,1024]{1,0:T(8,128)(2,1)S(1)}, u32[]{:S(2)}, u32[]{:S(2)}) collective-permute-start(bf16[512,1024]{1,0:T(8,128)(2,1)} %refs_2_.6), channel_id=1, source_target_pairs={{0,1},{1,0},{2,3},{3,2},{4,5},{5,4},{6,7},{7,6},{8,9},{9,8},{10,11... | collective-permute-start | bytes 3145736 | tf_op jit(solution)/shard_map/ppermute | solution.py:225
  21.5 1.0 %copy-start.1 = (bf16[512,512]{1,0:T(8,128)(2,1)S(1)}, bf16[512,512]{1,0:T(8,128)(2,1)}, u32[]{:S(2)}) copy-start(bf16[512,512]{1,0:T(8,128)(2,1)} %refs_0_.8) | copy-start | bytes 1572868
  22.6 1.0 %copy-start.3 = (bf16[512,512]{1,0:T(8,128)(2,1)S(1)}, bf16[512,512]{1,0:T(8,128)(2,1)}, u32[]{:S(2)}) copy-start(bf16[512,512]{1,0:T(8,128)(2,1)} %refs_1_.11) | copy-start | bytes 1572868
  23.6 1.0 %copy-start.5 = (bf16[512,512]{1,0:T(8,128)(2,1)S(1)}, bf16[512,512]{1,0:T(8,128)(2,1)}, u32[]{:S(2)}) copy-start(bf16[512,512]{1,0:T(8,128)(2,1)} %refs_2_.7) | copy-start | bytes 1572868
  24.7 6.5 %copy-start.7 = (bf16[4096,512]{1,0:T(8,128)(2,1)S(1)}, bf16[4096,512]{1,0:T(8,128)(2,1)}, u32[]{:S(2)}) copy-start(bf16[4096,512]{1,0:T(8,128)(2,1)} %refs_0_.6) | copy-start | bytes 12582916
  27.0 9.5 %copy-start.8 = (bf16[512,1024]{1,0:T(8,128)(2,1)}, bf16[512,1024]{1,0:T(8,128)(2,1)S(1)}, u32[]{:S(2)}) copy-start(bf16[512,1024]{1,0:T(8,128)(2,1)S(1)} %collective-permute-done.4.refs_3_.refs_4_) | copy-start | bytes 3145732
  27.8 8.8 %copy-start.13 = (bf16[512,512]{1,0:T(8,128)(2,1)}, bf16[512,512]{1,0:T(8,128)(2,1)S(1)}, u32[]{:S(2)}) copy-start(bf16[512,512]{1,0:T(8,128)(2,1)S(1)} %shard_map.88.refs_0_) | copy-start | bytes 1572868
  27.8 3.4 %collective-permute-start.6 = (bf16[512,1024]{1,0:T(8,128)(2,1)S(1)}, bf16[512,1024]{1,0:T(8,128)(2,1)S(1)}, u32[]{:S(2)}, u32[]{:S(2)}) collective-permute-start(bf16[512,1024]{1,0:T(8,128)(2,1)S(1)} %collective-permute-done.4.refs_3_.refs_4_), channel_id=1, source_target_pairs={{0,1},{1,0},{2,3},{3,2},{4,5},{5,4},{6,7},{7,6},{8,9},{9,8},{10,11... | collective-permute-start | bytes 3145736 | tf_op jit(solution)/shard_map/ppermute | solution.py:225
  27.8 14.3 %collective-permute-start.8 = (bf16[512,512]{1,0:T(8,128)(2,1)S(1)}, bf16[512,512]{1,0:T(8,128)(2,1)S(1)}, u32[]{:S(2)}, u32[]{:S(2)}) collective-permute-start(bf16[512,512]{1,0:T(8,128)(2,1)S(1)} %shard_map.88.refs_0_), channel_id=1, source_target_pairs={{0,4},{4,0},{8,12},{12,8},{16,20},{20,16},{24,28},{28,24},{1,5},{5... | collective-permute-start | bytes 1572872 | tf_op jit(solution)/shard_map/ppermute | solution.py:225
  29.7 14.3 %collective-permute-start.9 = (bf16[512,512]{1,0:T(8,128)(2,1)}, bf16[512,512]{1,0:T(8,128)(2,1)}, u32[]{:S(2)}, u32[]{:S(2)}) collective-permute-start(bf16[512,512]{1,0:T(8,128)(2,1)} %collective-permute-done.5.refs_1_.refs_6_), channel_id=1, source_target_pairs={{0,2},{1,3},{2,0},{3,1},{4,6},{5,7},{6,4},{7,5},{8,10},{9,11},{10,... | collective-permute-start | bytes 1572872 | tf_op jit(solution)/shard_map/ppermute | solution.py:225
  31.2 5.4 %copy-start.9 = (bf16[512,1024]{1,0:T(8,128)(2,1)}, bf16[512,1024]{1,0:T(8,128)(2,1)S(1)}, u32[]{:S(2)}) copy-start(bf16[512,1024]{1,0:T(8,128)(2,1)S(1)} %collective-permute-done.1.refs_2_.refs_3_) | copy-start | bytes 3145732
  31.2 5.4 %copy-start.10 = (bf16[512,1024]{1,0:T(8,128)(2,1)}, bf16[512,1024]{1,0:T(8,128)(2,1)S(1)}, u32[]{:S(2)}) copy-start(bf16[512,1024]{1,0:T(8,128)(2,1)S(1)} %collective-permute-done.6.refs_4_.refs_5_) | copy-start | bytes 3145732
  34.9 9.1 %collective-permute-start.7 = (bf16[512,128]{1,0:T(8,128)(2,1)S(1)}, bf16[512,128]{1,0:T(8,128)(2,1)S(1)}, u32[]{:S(2)}, u32[]{:S(2)}) collective-permute-start(bf16[512,128]{1,0:T(8,128)(2,1)S(1)} %shard_map.90.refs_0_), channel_id=1, source_target_pairs={{0,8},{4,12},{8,0},{12,4},{16,24},{20,28},{24,16},{28,20},{1,9},{5... | collective-permute-start | bytes 393224 | tf_op jit(solution)/shard_map/ppermute | solution.py:225
  36.6 10.1 %collective-permute-start.11 = (bf16[512,512]{1,0:T(8,128)(2,1)}, bf16[512,512]{1,0:T(8,128)(2,1)}, u32[]{:S(2)}, u32[]{:S(2)}) collective-permute-start(bf16[512,512]{1,0:T(8,128)(2,1)} %collective-permute-done.5.refs_1_.refs_6_), channel_id=1, source_target_pairs={{0,1},{1,0},{2,3},{3,2},{4,5},{5,4},{6,7},{7,6},{8,9},{9,8},{10,11... | collective-permute-start | bytes 1572872 | tf_op jit(solution)/shard_map/ppermute | solution.py:225
  37.3 1.0 %copy-start.11 = (f32[512,512]{1,0:T(8,128)}, f32[512,512]{1,0:T(8,128)S(1)}, u32[]{:S(2)}) copy-start(f32[512,512]{1,0:T(8,128)S(1)} %shard_map.91.refs_5_) | copy-start | bytes 3145732
  44.0 2.7 %collective-permute-start.12 = (bf16[512,512]{1,0:T(8,128)(2,1)}, bf16[512,512]{1,0:T(8,128)(2,1)S(1)}, u32[]{:S(2)}, u32[]{:S(2)}) collective-permute-start(bf16[512,512]{1,0:T(8,128)(2,1)} %collective-permute-done.9.refs_3_.refs_8_), channel_id=1, source_target_pairs={{0,1},{1,0},{2,3},{3,2},{4,5},{5,4},{6,7},{7,6},{8,9},{9,8},{10,11... | collective-permute-start | bytes 1572872 | tf_op jit(solution)/shard_map/ppermute | solution.py:225
  44.0 9.7 %collective-permute-start.10 = (bf16[512,128]{1,0:T(8,128)(2,1)S(1)}, bf16[512,128]{1,0:T(8,128)(2,1)S(1)}, u32[]{:S(2)}, u32[]{:S(2)}) collective-permute-start(bf16[512,128]{1,0:T(8,128)(2,1)S(1)} %shard_map.92), channel_id=1, source_target_pairs={{0,16},{4,20},{8,24},{12,28},{16,0},{20,4},{24,8},{28,12},{1,17},{... | collective-permute-start | bytes 393224 | tf_op jit(solution)/shard_map/ppermute | solution.py:225
  46.7 1.2 %copy-start.12 = (f32[512,512]{1,0:T(8,128)S(1)}, f32[512,512]{1,0:T(8,128)}, u32[]{:S(2)}) copy-start(f32[512,512]{1,0:T(8,128)} %copy-done.11) | copy-start | bytes 3145732
  47.9 1.0 %copy-start.15 = (bf16[512,512]{1,0:T(8,128)(2,1)S(1)}, bf16[512,512]{1,0:T(8,128)(2,1)}, u32[]{:S(2)}) copy-start(bf16[512,512]{1,0:T(8,128)(2,1)} %copy-done.14) | copy-start | bytes 1572868
  49.0 5.7 %copy-start.16 = (bf16[512,512]{1,0:T(8,128)(2,1)}, bf16[512,512]{1,0:T(8,128)(2,1)S(1)}, u32[]{:S(2)}) copy-start(bf16[512,512]{1,0:T(8,128)(2,1)S(1)} %collective-permute-done.12.refs_4_.refs_9_) | copy-start | bytes 1572868
  49.5 10.7 %collective-permute-start.15 = (bf16[512,256]{1,0:T(8,128)(2,1)S(1)}, bf16[512,256]{1,0:T(8,128)(2,1)S(1)}, u32[]{:S(2)}, u32[]{:S(2)}) collective-permute-start(bf16[512,256]{1,0:T(8,128)(2,1)S(1)} %get-tuple-element.77.refs_0_), channel_id=1, source_target_pairs={{0,8},{4,12},{8,0},{12,4},{16,24},{20,28},{24,16},{28,20},{1,9},{5... | collective-permute-start | bytes 786440 | tf_op jit(solution)/shard_map/ppermute | solution.py:308
  51.2 13.7 %collective-permute-start.13 = (bf16[512,256]{1,0:T(8,128)(2,1)S(1)}, bf16[512,256]{1,0:T(8,128)(2,1)S(1)}, u32[]{:S(2)}, u32[]{:S(2)}) collective-permute-start(bf16[512,256]{1,0:T(8,128)(2,1)S(1)} %get-tuple-element.70.refs_0_), channel_id=1, source_target_pairs={{0,8},{4,12},{8,0},{12,4},{16,24},{20,28},{24,16},{28,20},{1,9},{5... | collective-permute-start | bytes 786440 | tf_op jit(solution)/shard_map/ppermute | solution.py:308
  53.8 0.9 %copy-start.24 = (bf16[512,128]{1,0:T(8,128)(2,1)}, bf16[512,128]{1,0:T(8,128)(2,1)S(1)}, u32[]{:S(2)}) copy-start(bf16[512,128]{1,0:T(8,128)(2,1)S(1)} %collective-permute-done.10) | copy-start | bytes 393220
  53.9 6.4 %collective-permute-start.16 = (bf16[512,128]{1,0:T(8,128)(2,1)S(1)}, bf16[512,128]{1,0:T(8,128)(2,1)S(1)}, u32[]{:S(2)}, u32[]{:S(2)}) collective-permute-start(bf16[512,128]{1,0:T(8,128)(2,1)S(1)} %add_convert_fusion.1), channel_id=1, source_target_pairs={{0,4},{4,0},{8,12},{12,8},{16,20},{20,16},{24,28},{28,24},{1,5},{5... | collective-permute-start | bytes 393224 | tf_op jit(solution)/shard_map/ppermute | solution.py:225
  59.6 6.3 %copy-start.20 = (bf16[512,256]{1,0:T(8,128)(2,1)S(1)}, bf16[512,256]{1,0:T(8,128)(2,1)}, u32[]{:S(2)}) copy-start(bf16[512,256]{1,0:T(8,128)(2,1)} %get-tuple-element.88.refs_0_) | copy-start | bytes 786436
  59.6 11.0 %copy-start.22 = (bf16[512,256]{1,0:T(8,128)(2,1)S(1)}, bf16[512,256]{1,0:T(8,128)(2,1)}, u32[]{:S(2)}) copy-start(bf16[512,256]{1,0:T(8,128)(2,1)} %get-tuple-element.76.refs_0_) | copy-start | bytes 786436
  59.6 11.0 %collective-permute-start.17 = (bf16[512,256]{1,0:T(8,128)(2,1)}, bf16[512,256]{1,0:T(8,128)(2,1)S(1)}, u32[]{:S(2)}, u32[]{:S(2)}) collective-permute-start(bf16[512,256]{1,0:T(8,128)(2,1)} %get-tuple-element.76.refs_0_), channel_id=1, source_target_pairs={{0,8},{4,12},{8,0},{12,4},{16,24},{20,28},{24,16},{28,20},{1,9},{5... | collective-permute-start | bytes 786440 | tf_op jit(solution)/shard_map/ppermute | solution.py:308
  60.4 10.2 %collective-permute-start.18 = (bf16[512,256]{1,0:T(8,128)(2,1)S(1)}, bf16[512,256]{1,0:T(8,128)(2,1)S(1)}, u32[]{:S(2)}, u32[]{:S(2)}) collective-permute-start(bf16[512,256]{1,0:T(8,128)(2,1)S(1)} %shard_map.96), channel_id=1, source_target_pairs={{8,16},{12,20},{16,8},{20,12},{9,17},{13,21},{17,9},{21,13},{10,18... | collective-permute-start | bytes 786440 | tf_op jit(solution)/shard_map/ppermute | solution.py:308
  65.0 6.5 %copy-start.18 = (f32[512,256]{1,0:T(8,128)S(1)}, f32[512,256]{1,0:T(8,128)}, u32[]{:S(2)}) copy-start(f32[512,256]{1,0:T(8,128)} %get-tuple-element.85.refs_0_) | copy-start | bytes 1572868
  65.0 12.8 %copy-start.17 = (f32[512,256]{1,0:T(8,128)S(1)}, f32[512,256]{1,0:T(8,128)}, u32[]{:S(2)}) copy-start(f32[512,256]{1,0:T(8,128)} %get-tuple-element.89.refs_0_) | copy-start | bytes 1572868
  65.0 14.7 %copy-start.25 = (bf16[512,128]{1,0:T(8,128)(2,1)S(1)}, bf16[512,128]{1,0:T(8,128)(2,1)}, u32[]{:S(2)}) copy-start(bf16[512,128]{1,0:T(8,128)(2,1)} %copy-done.24) | copy-start | bytes 393220
  65.0 14.8 %copy-start.4 = (bf16[512,512]{1,0:T(8,128)(2,1)S(1)}, bf16[512,512]{1,0:T(8,128)(2,1)}, u32[]{:S(2)}) copy-start(bf16[512,512]{1,0:T(8,128)(2,1)} %refs_1_.11) | copy-start | bytes 1572868
  65.0 14.8 %copy-start.6 = (bf16[512,512]{1,0:T(8,128)(2,1)S(1)}, bf16[512,512]{1,0:T(8,128)(2,1)}, u32[]{:S(2)}) copy-start(bf16[512,512]{1,0:T(8,128)(2,1)} %refs_2_.7) | copy-start | bytes 1572868
  65.0 12.7 %collective-permute-start.14 = (bf16[512,256]{1,0:T(8,128)(2,1)S(1)}, bf16[512,256]{1,0:T(8,128)(2,1)S(1)}, u32[]{:S(2)}, u32[]{:S(2)}) collective-permute-start(bf16[512,256]{1,0:T(8,128)(2,1)S(1)} %shard_map.94), channel_id=1, source_target_pairs={{8,16},{12,20},{16,8},{20,12},{9,17},{13,21},{17,9},{21,13},{10,18... | collective-permute-start | bytes 786440 | tf_op jit(solution)/shard_map/ppermute | solution.py:308
  65.9 12.9 %collective-permute-start.21 = (bf16[512,256]{1,0:T(8,128)(2,1)S(1)}, bf16[512,256]{1,0:T(8,128)(2,1)S(1)}, u32[]{:S(2)}, u32[]{:S(2)}) collective-permute-start(bf16[512,256]{1,0:T(8,128)(2,1)S(1)} %copy-done.20), channel_id=1, source_target_pairs={{0,8},{4,12},{8,0},{12,4},{16,24},{20,28},{24,16},{28,20},{1,9},{5... | collective-permute-start | bytes 786440 | tf_op jit(solution)/shard_map/ppermute | solution.py:308
  70.6 14.3 %copy-start.23 = (f32[512,256]{1,0:T(8,128)S(1)}, f32[512,256]{1,0:T(8,128)}, u32[]{:S(2)}) copy-start(f32[512,256]{1,0:T(8,128)} %get-tuple-element.84.refs_0_) | copy-start | bytes 1572868
  70.6 14.3 %collective-permute-start.19 = (bf16[512,256]{1,0:T(8,128)(2,1)S(1)}, bf16[512,256]{1,0:T(8,128)(2,1)S(1)}, u32[]{:S(2)}, u32[]{:S(2)}) collective-permute-start(bf16[512,256]{1,0:T(8,128)(2,1)S(1)} %shard_map.97), channel_id=1, source_target_pairs={{8,16},{12,20},{16,8},{20,12},{9,17},{13,21},{17,9},{21,13},{10,18... | collective-permute-start | bytes 786440 | tf_op jit(solution)/shard_map/ppermute | solution.py:308
  71.5 13.4 %collective-permute-start.20 = (bf16[512,256]{1,0:T(8,128)(2,1)S(1)}, bf16[512,256]{1,0:T(8,128)(2,1)S(1)}, u32[]{:S(2)}, u32[]{:S(2)}) collective-permute-start(bf16[512,256]{1,0:T(8,128)(2,1)S(1)} %shard_map.99), channel_id=1, source_target_pairs={{0,8},{4,12},{8,0},{12,4},{16,24},{20,28},{24,16},{28,20},{1,9},{5... | collective-permute-start | bytes 786440 | tf_op jit(solution)/shard_map/ppermute | solution.py:308
  77.8 9.6 %collective-permute-start.23 = (bf16[512,256]{1,0:T(8,128)(2,1)S(1)}, bf16[512,256]{1,0:T(8,128)(2,1)S(1)}, u32[]{:S(2)}, u32[]{:S(2)}) collective-permute-start(bf16[512,256]{1,0:T(8,128)(2,1)S(1)} %shard_map.101), channel_id=1, source_target_pairs={{0,8},{4,12},{8,0},{12,4},{16,24},{20,28},{24,16},{28,20},{1,9},{5... | collective-permute-start | bytes 786440 | tf_op jit(solution)/shard_map/ppermute | solution.py:308
  78.9 6.9 %collective-permute-start.22 = (bf16[512,256]{1,0:T(8,128)(2,1)S(1)}, bf16[512,256]{1,0:T(8,128)(2,1)S(1)}, u32[]{:S(2)}, u32[]{:S(2)}) collective-permute-start(bf16[512,256]{1,0:T(8,128)(2,1)S(1)} %shard_map.102), channel_id=1, source_target_pairs={{8,16},{12,20},{16,8},{20,12},{9,17},{13,21},{17,9},{21,13},{10,18... | collective-permute-start | bytes 786440 | tf_op jit(solution)/shard_map/ppermute | solution.py:308
  84.9 2.5 %copy-start.19 = (f32[512,256]{1,0:T(8,128)S(1)}, f32[512,256]{1,0:T(8,128)}, u32[]{:S(2)}) copy-start(f32[512,256]{1,0:T(8,128)} %get-tuple-element.87.refs_1_) | copy-start | bytes 1572868
  (2 other events, 1.7 us)
